TPU v7x, 32 devices: a whole 2x2x4 slice. The times are simulated.
32 devices in a mesh: lon: 16 (over z, y, core), lat: 2 (over x).
Axes of the slice: x: 2, y: 2, z: 4, core: 2. Of those that a mesh axis runs over, the one named last changes fastest.
Arguments:
- state: bfloat16 [90, 384, 128], P('lat', 'lon'), may hold values from -6 to 6
- land_sea: int32 [90, 384], P('lat', 'lon'), may hold values 0 or 1
- cotangent: bfloat16 [90, 384, 128], P('lat', 'lon'), may hold values from -6 to 6
- dw_kernel: bfloat16 [2, 7, 7, 128], replicated, may hold values from -0.875 to 0.875
- conv_bias: float32 [2, 128], replicated, may hold values from -3 to 3
- norm_gain: float32 [2, 128], replicated, may hold values from 0.1 to 1.9
- norm_bias: float32 [2, 128], replicated, may hold values from -3 to 3
- weight_in: bfloat16 [2, 128, 512], replicated, may hold values from -0.5 to 0.5
- bias_in: float32 [2, 512], replicated, may hold values from -3 to 3
- weight_out: bfloat16 [2, 512, 128], replicated, may hold values from -0.25 to 0.25
- bias_out: float32 [2, 128], replicated, may hold values from -3 to 3
- layer_scale: float32 [2, 128], replicated, may hold values from 0.3 to 1
Outputs:
- output: bfloat16 [90, 384, 128], P('lat', 'lon')
- grad_state: bfloat16 [90, 384, 128], P('lat', 'lon')
- grad_dw_kernel: float32 [2, 7, 7, 128], replicated
- grad_conv_bias: float32 [2, 128], replicated
- grad_norm_gain: float32 [2, 128], replicated
- grad_norm_bias: float32 [2, 128], replicated
- grad_weight_in: float32 [2, 128, 512], replicated
- grad_bias_in: float32 [2, 512], replicated
- grad_weight_out: float32 [2, 512, 128], replicated
- grad_bias_out: float32 [2, 128], replicated
- grad_layer_scale: float32 [2, 128], replicated
All inputs are finite; a program needn't handle non-finite values. No bound on the sum of `land_sea` on one device may be relied on, other than what follows from the above.
Results may differ from a plain program's by a relative error of at most 0.02.
Values may be sent and summed in bfloat16 or wider, within the bound.
No kernel may reach another device: no remote copies, remote signals or barrier semaphores. Data moves between devices by JAX's collectives and lax.ppermute only.
A program may use at most 64 MiB of HBM per device.

v0:
```python
import math

import jax
import jax.numpy as jnp
from jax import lax
from jax.sharding import PartitionSpec as P

KSIZE = 7
BLOCKS = 2


EPS_NORM = 1e-06
INV_ROOT_TWO = 0.7071067811865476
INV_ROOT_TWO_PI = 0.3989422804014327


def with_halo(shard, sides, width, wrap):
    for axis, dim in sides:
        count, length = (lax.axis_size(axis), shard.shape[dim])
        up = [(i, (i + 1) % count) for i in range(count if wrap else count - 1)]
        down = [(j, i) for i, j in up]
        last = lax.slice_in_dim(shard, length - width, length, axis=dim)
        first = lax.slice_in_dim(shard, 0, width, axis=dim)
        before = lax.ppermute(last, axis, up)
        after = lax.ppermute(first, axis, down)
        shard = jnp.concatenate([before, shard, after], axis=dim)
    return shard


def depthwise(window, kernel, height, breadth):
    summed = jnp.zeros((height, breadth, window.shape[2]), jnp.float32)
    for tap_row in range(KSIZE):
        for tap_col in range(KSIZE):
            piece = window[tap_row : tap_row + height, tap_col : tap_col + breadth].astype(
                jnp.float32
            )
            summed = summed + piece * kernel[tap_row, tap_col].astype(jnp.float32)
    return summed


def block_forward(window, land_rows, params):
    (
        kernel,
        conv_bias,
        norm_gain,
        norm_bias,
        weight_in,
        bias_in,
        weight_out,
        bias_out,
        layer_scale,
    ) = params
    margin = KSIZE // 2
    height = window.shape[0] - 2 * margin
    breadth = window.shape[1] - 2 * margin
    channels = window.shape[2]
    cell_count = height * breadth
    mixed_sum = depthwise(window, kernel, height, breadth) + conv_bias
    center = mixed_sum - jnp.mean(mixed_sum, axis=-1, keepdims=True)
    inverse = lax.rsqrt(jnp.mean(center * center, axis=-1, keepdims=True) + EPS_NORM)
    normed = (center * inverse).reshape(cell_count, channels)
    lifted = (normed * norm_gain + norm_bias).astype(jnp.bfloat16)
    hidden = jnp.dot(lifted, weight_in, preferred_element_type=jnp.float32) + bias_in
    active = jax.nn.gelu(hidden, approximate=False).astype(jnp.bfloat16)
    branch = jnp.dot(active, weight_out, preferred_element_type=jnp.float32) + bias_out
    interior = (
        window[margin : margin + height, margin : margin + breadth]
        .astype(jnp.float32)
        .reshape(cell_count, channels)
    )
    ocean_mask = land_rows.reshape(cell_count, 1).astype(jnp.float32)
    result = (
        ((interior + layer_scale * branch) * ocean_mask)
        .astype(jnp.bfloat16)
        .reshape(height, breadth, channels)
    )
    return (result, (normed, inverse.reshape(cell_count, 1), lifted, hidden, active, branch))


def block_backward(window, land_rows, incoming, params, stored):
    (
        kernel,
        conv_bias,
        norm_gain,
        norm_bias,
        weight_in,
        bias_in,
        weight_out,
        bias_out,
        layer_scale,
    ) = params
    normed, inverse, lifted, hidden, active, branch = stored
    margin = KSIZE // 2
    height = window.shape[0] - 2 * margin
    breadth = window.shape[1] - 2 * margin
    channels = window.shape[2]
    cell_count = height * breadth
    ocean_mask = land_rows.reshape(cell_count, 1).astype(jnp.float32)
    masked = incoming.reshape(cell_count, channels).astype(jnp.float32) * ocean_mask
    grad_branch = (masked * layer_scale).astype(jnp.bfloat16)
    contract_rows = (((0,), (0,)), ((), ()))
    contract_cols = (((1,), (1,)), ((), ()))
    grad_scale = jnp.sum(masked * branch, axis=0)
    grad_bias_out = jnp.sum(grad_branch.astype(jnp.float32), axis=0)
    grad_weight_out = lax.dot_general(
        active, grad_branch, contract_rows, preferred_element_type=jnp.float32
    )
    grad_active = lax.dot_general(
        grad_branch, weight_out, contract_cols, preferred_element_type=jnp.float32
    )
    cumulative = 0.5 * (1.0 + lax.erf(hidden * INV_ROOT_TWO))
    density = jnp.exp(-0.5 * hidden * hidden) * INV_ROOT_TWO_PI
    grad_hidden = (grad_active * (cumulative + hidden * density)).astype(jnp.bfloat16)
    grad_bias_in = jnp.sum(grad_hidden.astype(jnp.float32), axis=0)
    grad_weight_in = lax.dot_general(
        lifted, grad_hidden, contract_rows, preferred_element_type=jnp.float32
    )
    grad_lifted = lax.dot_general(
        grad_hidden, weight_in, contract_cols, preferred_element_type=jnp.float32
    )
    grad_gain = jnp.sum(grad_lifted * normed, axis=0)
    grad_shift = jnp.sum(grad_lifted, axis=0)
    scaled = grad_lifted * norm_gain
    grad_mixed = inverse * (
        scaled
        - jnp.mean(scaled, axis=-1, keepdims=True)
        - normed * jnp.mean(scaled * normed, axis=-1, keepdims=True)
    )
    grad_mixed = grad_mixed.astype(jnp.bfloat16).reshape(height, breadth, channels)
    spread = grad_mixed.astype(jnp.float32)
    grad_conv_bias = jnp.sum(spread, axis=(0, 1))
    tap_sums = []
    for tap_row in range(KSIZE):
        for tap_col in range(KSIZE):
            piece = window[tap_row : tap_row + height, tap_col : tap_col + breadth].astype(
                jnp.float32
            )
            tap_sums.append(jnp.sum(spread * piece, axis=(0, 1)))
    grad_kernel = jnp.stack(tap_sums).reshape(KSIZE, KSIZE, channels)
    gradients = (
        grad_kernel,
        grad_conv_bias,
        grad_gain,
        grad_shift,
        grad_weight_in,
        grad_bias_in,
        grad_weight_out,
        grad_bias_out,
        grad_scale,
    )
    return (grad_mixed, masked.reshape(height, breadth, channels), gradients)


def adjoint(padded, masked, kernel):
    margin = KSIZE // 2
    height = masked.shape[0]
    breadth = masked.shape[1]
    summed = masked
    for tap_row in range(KSIZE):
        for tap_col in range(KSIZE):
            first_row = 2 * margin - tap_row
            first_col = 2 * margin - tap_col
            piece = padded[first_row : first_row + height, first_col : first_col + breadth].astype(
                jnp.float32
            )
            summed = summed + piece * kernel[tap_row, tap_col].astype(jnp.float32)
    return summed.astype(jnp.bfloat16)


def extend(tile_field):
    beside_all = with_halo(tile_field, (("lon", 1),), KSIZE // 2, True)
    return with_halo(beside_all, (("lat", 0),), KSIZE // 2, False)


def sum_everything(parts):
    (
        kernel_part,
        conv_part,
        gain_part,
        shift_part,
        first_part,
        first_bias,
        second_part,
        second_bias,
        scale_part,
    ) = parts
    return lax.psum(
        (
            kernel_part,
            conv_part,
            gain_part,
            shift_part,
            first_part,
            first_bias,
            second_part,
            second_bias,
            scale_part,
        ),
        ("lon", "lat"),
    )


def on_device(
    state,
    land_sea,
    cotangent,
    dw_kernel,
    conv_bias,
    norm_gain,
    norm_bias,
    weight_in,
    bias_in,
    weight_out,
    bias_out,
    layer_scale,
):
    stacked = (
        dw_kernel,
        conv_bias,
        norm_gain,
        norm_bias,
        weight_in,
        bias_in,
        weight_out,
        bias_out,
        layer_scale,
    )
    height = state.shape[0]
    breadth = state.shape[1]
    grad_norm = 1.0 / math.sqrt(lax.axis_size("lat") * height * lax.axis_size("lon") * breadth)
    current = state
    windows = []
    stored_all = []
    for layer_index in range(BLOCKS):
        params = tuple((member[layer_index] for member in stacked))
        window = extend(current)
        windows.append(window)
        outcome = block_forward(window, land_sea, params)
        current = outcome[0]
        stored_all.append(outcome[1])
    incoming = cotangent
    per_layer = [None] * BLOCKS
    for layer_index in reversed(range(BLOCKS)):
        params = tuple((member[layer_index] for member in stacked))
        stored = stored_all[layer_index]
        grad_mixed, masked, gradients = block_backward(
            windows[layer_index], land_sea, incoming, params, stored
        )
        incoming = adjoint(extend(grad_mixed), masked, params[0])
        per_layer[layer_index] = gradients
    combined = tuple(
        (
            jnp.stack([per_layer[layer_index][member] for layer_index in range(BLOCKS)])
            for member in range(9)
        )
    )
    combined = sum_everything(combined)
    scaled = [member * grad_norm for member in combined]
    return (
        current,
        incoming,
        scaled[0],
        scaled[1],
        scaled[2],
        scaled[3],
        scaled[4],
        scaled[5],
        scaled[6],
        scaled[7],
        scaled[8],
    )


def solution(mesh):
    placed = (
        P("lat", "lon", None),
        P("lat", "lon"),
        P("lat", "lon", None),
        P(),
        P(),
        P(),
        P(),
        P(),
        P(),
        P(),
        P(),
        P(),
    )
    return jax.shard_map(
        on_device,
        mesh=mesh,
        in_specs=placed,
        out_specs=(
            P("lat", "lon", None),
            P("lat", "lon", None),
            P(),
            P(),
            P(),
            P(),
            P(),
            P(),
            P(),
            P(),
            P(),
        ),
        check_vma=False,
    )
```

profile of v0, /device:TPU:0, one launch (start us, length us, event | category | flops | bytes accessed | tf_op | source)
XLA Modules:
  0.0 324.0 jit_solution(17240756172110758670)
XLA Ops:
  8.8 5.1 %collective-permute-start.1 = (bf16[45,3,128]{2,1,0:T(4,128)(2,1)S(1)}, bf16[45,3,128]{2,1,0:T(4,128)(2,1)S(1)}, u32[]{:S(2)}, u32[]{:S(2)}) collective-permute-start(bf16[45,3,128]{2,1,0:T(4,128)(2,1)S(1)} %get-tuple-element.208), channel_id=1, source_target_pairs={{2,0},{4,2},{6,4},{8,6},{10,8},{12,10},{14,12},{16,14},{18,16},{20... | collective-permute-start | bytes 103688 | tf_op jit(solution)/shard_map/ppermute | solution.py:25
  22.4 2.5 convert_reduce_fusion.3
  26.7 3.8 %collective-permute-start.2 = (bf16[3,30,128]{2,1,0:T(8,128)(2,1)S(1)}, bf16[3,30,128]{2,1,0:T(8,128)(2,1)S(1)}, u32[]{:S(2)}, u32[]{:S(2)}) collective-permute-start(bf16[3,30,128]{2,1,0:T(8,128)(2,1)S(1)} %get-tuple-element.198), channel_id=1, source_target_pairs={{0,1},{2,3},{4,5},{6,7},{8,9},{10,11},{12,13},{14,15},{16,17},{18,... | collective-permute-start | bytes 69128 | tf_op jit(solution)/shard_map/ppermute | solution.py:24
  32.0 4.2 %collective-permute-done.3 = bf16[3,30,128]{2,1,0:T(8,128)(2,1)S(1)} collective-permute-done((bf16[3,30,128]{2,1,0:T(8,128)(2,1)S(1)}, bf16[3,30,128]{2,1,0:T(8,128)(2,1)S(1)}, u32[]{:S(2)}, u32[]{:S(2)}) %collective-permute-start.3) | collective-permute-done | bytes 23072 | tf_op jit(solution)/shard_map/ppermute | solution.py:25
  36.4 5.0 %fusion.421 = (f32[45,24]{1,0:T(8,128)S(1)}, f32[45,24,128]{2,1,0:T(8,128)S(1)}) fusion(f32[128]{0:T(128)S(1)} %get-tuple-element.316, f32[128]{0:T(128)S(1)} %get-tuple-element.261, bf16[48,30,128]{2,1,0:T(8,128)(2,1)S(1)} %get-tuple-element.197, f32[128]{0:T(128)S(1)} %get-tuple-element.262, f32[128]{0:T(128)S(1)} %get-tuple-element.263, ...), kind=kLoop, calls=%fused_computation.872 | loop fusion | flops 21702600 | bytes 13335520 | tf_op jit(solution)/shard_map/reduce_sum | solution.py:59
  42.6 6.0 %fusion.4 = (bf16[1080,512]{1,0:T(8,128)(2,1)S(1)}, f32[1080,512]{1,0:T(8,128)}) fusion(f32[512]{0:T(512)S(1)} %bitcast.782, bf16[1080,128]{1,0:T(8,128)(2,1)S(1)} %bitcast.742, bf16[2,128,512]{2,1,0:T(8,128)(2,1)S(1)} %copy-done.11), kind=kOutput, calls=%fused_computation.113 | convolution fusion | flops 178053120 | bytes 3727360 | tf_op jit(solution)/shard_map/dot_general | solution.py:63
  51.0 4.4 %collective-permute-start.5 = (bf16[45,3,128]{2,1,0:T(4,128)(2,1)S(1)}, bf16[45,3,128]{2,1,0:T(4,128)(2,1)S(1)}, u32[]{:S(2)}, u32[]{:S(2)}) collective-permute-start(bf16[45,3,128]{2,1,0:T(4,128)(2,1)S(1)} %get-tuple-element.206), channel_id=1, source_target_pairs={{2,0},{4,2},{6,4},{8,6},{10,8},{12,10},{14,12},{16,14},{18,16},{20... | collective-permute-start | bytes 103688 | tf_op jit(solution)/shard_map/ppermute | solution.py:25
  60.6 4.0 %collective-permute-done.7 = bf16[3,30,128]{2,1,0:T(8,128)(2,1)S(1)} collective-permute-done((bf16[3,30,128]{2,1,0:T(8,128)(2,1)S(1)}, bf16[3,30,128]{2,1,0:T(8,128)(2,1)S(1)}, u32[]{:S(2)}, u32[]{:S(2)}) %collective-permute-start.7) | collective-permute-done | bytes 23072 | tf_op jit(solution)/shard_map/ppermute | solution.py:25
  64.8 5.0 %fusion.419 = (f32[45,24]{1,0:T(8,128)S(1)}, f32[45,24,128]{2,1,0:T(8,128)S(1)}) fusion(f32[128]{0:T(128)S(1)} %copy-done.149, f32[128]{0:T(128)S(1)} %get-tuple-element.212, bf16[48,30,128]{2,1,0:T(8,128)(2,1)S(1)} %get-tuple-element.193, f32[128]{0:T(128)S(1)} %get-tuple-element.213, f32[128]{0:T(128)S(1)} %get-tuple-element.214, ...), kind=kLoop, calls=%fused_computation.871 | loop fusion | flops 22946760 | bytes 12540640 | tf_op jit(solution)/shard_map/reduce_sum | solution.py:59
  73.4 7.0 %fusion.7 = (bf16[1080,512]{1,0:T(8,128)(2,1)}, f32[1080,512]{1,0:T(8,128)S(1)}) fusion(f32[512]{0:T(512)} %bitcast.780, bf16[1080,128]{1,0:T(8,128)(2,1)S(1)} %bitcast.741, bf16[2,128,512]{2,1,0:T(8,128)(2,1)} %param.19), kind=kOutput, calls=%fused_computation.116 | convolution fusion | flops 178053120 | bytes 3727360 | tf_op jit(solution)/shard_map/dot_general | solution.py:63
  80.4 1.9 convert_reduce_fusion
  87.8 4.4 %collective-permute-start.9 = (bf16[45,3,128]{2,1,0:T(4,128)(2,1)S(1)}, bf16[45,3,128]{2,1,0:T(4,128)(2,1)S(1)}, u32[]{:S(2)}, u32[]{:S(2)}) collective-permute-start(bf16[45,3,128]{2,1,0:T(4,128)(2,1)S(1)} %get-tuple-element.204), channel_id=1, source_target_pairs={{2,0},{4,2},{6,4},{8,6},{10,8},{12,10},{14,12},{16,14},{18,16},{20... | collective-permute-start | bytes 103688 | tf_op jit(solution)/shard_map/ppermute | solution.py:25
  95.6 4.8 %collective-permute-start.11 = (bf16[3,30,128]{2,1,0:T(8,128)(2,1)S(1)}, bf16[3,30,128]{2,1,0:T(8,128)(2,1)S(1)}, u32[]{:S(2)}, u32[]{:S(2)}) collective-permute-start(bf16[3,30,128]{2,1,0:T(8,128)(2,1)S(1)} %get-tuple-element.191), channel_id=1, source_target_pairs={{0,1},{2,3},{4,5},{6,7},{8,9},{10,11},{12,13},{14,15},{16,17},{18,... | collective-permute-start | bytes 69128 | tf_op jit(solution)/shard_map/ppermute | solution.py:24
  100.9 4.9 %stack.474 = f32[49,128]{1,0:T(8,128)S(1)} concatenate(f32[1,128]{1,0:T(1,128)S(1)} %bitcast.755, f32[1,128]{1,0:T(1,128)S(1)} %bitcast.756, f32[1,128]{1,0:T(1,128)} %bitcast.818, f32[1,128]{1,0:T(1,128)S(1)} %bitcast.757, f32[1,128]{1,0:T(1,128)} %bitcast.802, f32[1,128]{1,0:T(1,128)} %bitcast.803, f32[1,128]{1,0:T(1,128)} %bitcast.804, f32[1,128]{1,0:T(1,128)} %bitcast.805, ...), dimensions={0} | concatenate | bytes 50176 | tf_op jit(solution)/shard_map/stack | solution.py:139
  107.1 6.2 %multiply_convert_fusion.1 = (bf16[1080,128]{1,0:T(8,128)(2,1)S(1)}, bf16[45,24,128]{2,1,0:T(8,128)(2,1)S(1)}) fusion(f32[1080]{0:T(1024)S(1)} %convert_element_type.1163, f32[128]{0:T(128)S(1)} %copy-done.21, f32[128]{0:T(128)S(1)} %copy-done.102, bf16[48,30,128]{2,1,0:T(8,128)(2,1)S(1)} %get-tuple-element.189, f32[128]{0:T(128)S(1)} %copy-done.104, ...), kind=kLoop, calls=%fused_computation.516 | loop fusion | flops 23777280 | bytes 12821440 | tf_op jit(solution)/shard_map/convert_element_type | solution.py:100
  113.6 1.9 convert_reduce_fusion.1
  122.6 2.4 multiply_reduce_fusion.1
  128.9 38.9 %all-reduce = (f32[2,7,7,128]{3,2,1,0:T(8,128)S(1)}, f32[2,128]{1,0:T(2,128)S(1)}, f32[2,128]{1,0:T(2,128)S(1)}, f32[2,128]{1,0:T(2,128)S(1)}, f32[2,512]{1,0:T(...) all-reduce(f32[2,7,7,128]{3,2,1,0:T(8,128)S(1)} %pad_maximum_fusion, ...), channel_id=1, replica_groups=mesh['lon'=16,'lat'=2] {'lon','lat'}, use_global_device_ids=true, to_apply=%region_106.0 | all-reduce | flops 14848 | bytes 118784 | tf_op jit(solution)/shard_map/psum | solution.py:187
  173.5 4.8 %collective-permute-done.12 = bf16[45,3,128]{2,1,0:T(4,128)(2,1)S(1)} collective-permute-done((bf16[45,3,128]{2,1,0:T(4,128)(2,1)S(1)}, bf16[45,3,128]{2,1,0:T(4,128)(2,1)S(1)}, u32[]{:S(2)}, u32[]{:S(2)}) %collective-permute-start.12) | collective-permute-done | bytes 34592 | tf_op jit(solution)/shard_map/ppermute | solution.py:24
  179.7 4.5 %collective-permute-start.15 = (bf16[3,30,128]{2,1,0:T(8,128)(2,1)S(1)}, bf16[3,30,128]{2,1,0:T(8,128)(2,1)S(1)}, u32[]{:S(2)}, u32[]{:S(2)}) collective-permute-start(bf16[3,30,128]{2,1,0:T(8,128)(2,1)S(1)} %get-tuple-element.187), channel_id=1, source_target_pairs={{0,1},{2,3},{4,5},{6,7},{8,9},{10,11},{12,13},{14,15},{16,17},{18,... | collective-permute-start | bytes 69128 | tf_op jit(solution)/shard_map/ppermute | solution.py:24
  186.3 5.8 %fusion.280 = bf16[45,24,128]{2,1,0:T(8,128)(2,1)} fusion(bf16[45,24,128]{2,1,0:T(8,128)(2,1)S(1)} %bitcast.724, bf16[45,24,128]{2,1,0:T(8,128)(2,1)S(1)} %get-tuple-element.167, bf16[45,3,128]{2,1,0:T(4,128)(2,1)S(1)} %collective-permute-done.12, bf16[45,3,128]{2,1,0:T(4,128)(2,1)S(1)} %collective-permute-done.13, ...), kind=kLoop, calls=%fused_computation.534 | loop fusion | flops 23224320 | bytes 12540128 | tf_op jit(solution)/shard_map/convert_element_type | solution.py:167
  192.1 121.3 %all-reduce.4.cloned.1.call-done = (f32[2,128,512]{2,1,0:T(8,128)}, f32[2,512,128]{2,1,0:T(8,128)}) async-done(((f32[2,128,512]{2,1,0:T(8,128)}, f32[2,512,128]{2,1,0:T(8,128)}), (f32[2,128,512]{2,1,0:T(8,128)}, f32[2,512,128]{2,1,0:T(8,128)})) %all-reduce.4.cloned.1.call-update) | async-done | bytes 1048592 | tf_op jit(solution)/shard_map/psum | solution.py:187
  313.4 1.9 broadcast_multiply_fusion.1
  315.3 1.9 broadcast_multiply_fusion
  (476 shorter events, 54.3 us)
Async XLA Ops:
  7.2 29.0 %copy-start = (bf16[45,24,128]{2,1,0:T(8,128)(2,1)S(1)}, bf16[45,24,128]{2,1,0:T(8,128)(2,1)}, u32[]{:S(2)}) copy-start(bf16[45,24,128]{2,1,0:T(8,128)(2,1)} %param.12) | copy-start | bytes 829444
  7.2 306.2 %all-reduce.4.cloned.1.call-start = ((), (), s32[]{:S(2)}) async-start(), calls=%async_computation | async-start | bytes 2097152 | tf_op jit(solution)/shard_map/psum | solution.py:187
  8.2 17.6 %collective-permute-start = (bf16[45,3,128]{2,1,0:T(4,128)(2,1)S(1)}, bf16[45,3,128]{2,1,0:T(4,128)(2,1)S(1)}, u32[]{:S(2)}, u32[]{:S(2)}) collective-permute-start(bf16[45,3,128]{2,1,0:T(4,128)(2,1)S(1)} %get-tuple-element.207), channel_id=1, source_target_pairs={{0,2},{2,4},{4,6},{6,8},{8,10},{10,12},{12,14},{14,16},{16,18},{18... | collective-permute-start | bytes 103688 | tf_op jit(solution)/shard_map/ppermute | solution.py:24
  8.8 17.1 %collective-permute-start.1 = (bf16[45,3,128]{2,1,0:T(4,128)(2,1)S(1)}, bf16[45,3,128]{2,1,0:T(4,128)(2,1)S(1)}, u32[]{:S(2)}, u32[]{:S(2)}) collective-permute-start(bf16[45,3,128]{2,1,0:T(4,128)(2,1)S(1)} %get-tuple-element.208), channel_id=1, source_target_pairs={{2,0},{4,2},{6,4},{8,6},{10,8},{12,10},{14,12},{16,14},{18,16},{20... | collective-permute-start | bytes 103688 | tf_op jit(solution)/shard_map/ppermute | solution.py:25
  14.7 26.7 %copy-start.27 = (f32[128]{0:T(128)}, f32[128]{0:T(128)S(1)}, u32[]{:S(2)}) copy-start(f32[128]{0:T(128)S(1)} %get-tuple-element.299) | copy-start | bytes 1540
  14.7 26.7 %copy-start.29 = (f32[128]{0:T(128)}, f32[128]{0:T(128)S(1)}, u32[]{:S(2)}) copy-start(f32[128]{0:T(128)S(1)} %get-tuple-element.300) | copy-start | bytes 1540
  14.7 26.7 %copy-start.31 = (f32[128]{0:T(128)}, f32[128]{0:T(128)S(1)}, u32[]{:S(2)}) copy-start(f32[128]{0:T(128)S(1)} %get-tuple-element.301) | copy-start | bytes 1540
  14.7 26.7 %copy-start.33 = (f32[128]{0:T(128)}, f32[128]{0:T(128)S(1)}, u32[]{:S(2)}) copy-start(f32[128]{0:T(128)S(1)} %get-tuple-element.302) | copy-start | bytes 1540
  26.7 5.3 %collective-permute-start.2 = (bf16[3,30,128]{2,1,0:T(8,128)(2,1)S(1)}, bf16[3,30,128]{2,1,0:T(8,128)(2,1)S(1)}, u32[]{:S(2)}, u32[]{:S(2)}) collective-permute-start(bf16[3,30,128]{2,1,0:T(8,128)(2,1)S(1)} %get-tuple-element.198), channel_id=1, source_target_pairs={{0,1},{2,3},{4,5},{6,7},{8,9},{10,11},{12,13},{14,15},{16,17},{18,... | collective-permute-start | bytes 69128 | tf_op jit(solution)/shard_map/ppermute | solution.py:24
  30.5 5.7 %collective-permute-start.3 = (bf16[3,30,128]{2,1,0:T(8,128)(2,1)S(1)}, bf16[3,30,128]{2,1,0:T(8,128)(2,1)S(1)}, u32[]{:S(2)}, u32[]{:S(2)}) collective-permute-start(bf16[3,30,128]{2,1,0:T(8,128)(2,1)S(1)} %get-tuple-element.199), channel_id=1, source_target_pairs={{1,0},{3,2},{5,4},{7,6},{9,8},{11,10},{13,12},{15,14},{17,16},{19,... | collective-permute-start | bytes 69128 | tf_op jit(solution)/shard_map/ppermute | solution.py:25
  51.0 6.2 %collective-permute-start.4 = (bf16[45,3,128]{2,1,0:T(4,128)(2,1)S(1)}, bf16[45,3,128]{2,1,0:T(4,128)(2,1)S(1)}, u32[]{:S(2)}, u32[]{:S(2)}) collective-permute-start(bf16[45,3,128]{2,1,0:T(4,128)(2,1)S(1)} %get-tuple-element.205), channel_id=1, source_target_pairs={{0,2},{2,4},{4,6},{6,8},{8,10},{10,12},{12,14},{14,16},{16,18},{18... | collective-permute-start | bytes 103688 | tf_op jit(solution)/shard_map/ppermute | solution.py:24
  51.0 6.2 %collective-permute-start.5 = (bf16[45,3,128]{2,1,0:T(4,128)(2,1)S(1)}, bf16[45,3,128]{2,1,0:T(4,128)(2,1)S(1)}, u32[]{:S(2)}, u32[]{:S(2)}) collective-permute-start(bf16[45,3,128]{2,1,0:T(4,128)(2,1)S(1)} %get-tuple-element.206), channel_id=1, source_target_pairs={{2,0},{4,2},{6,4},{8,6},{10,8},{12,10},{14,12},{16,14},{18,16},{20... | collective-permute-start | bytes 103688 | tf_op jit(solution)/shard_map/ppermute | solution.py:25
  57.2 3.3 %collective-permute-start.6 = (bf16[3,30,128]{2,1,0:T(8,128)(2,1)S(1)}, bf16[3,30,128]{2,1,0:T(8,128)(2,1)S(1)}, u32[]{:S(2)}, u32[]{:S(2)}) collective-permute-start(bf16[3,30,128]{2,1,0:T(8,128)(2,1)S(1)} %get-tuple-element.194), channel_id=1, source_target_pairs={{0,1},{2,3},{4,5},{6,7},{8,9},{10,11},{12,13},{14,15},{16,17},{18,... | collective-permute-start | bytes 69128 | tf_op jit(solution)/shard_map/ppermute | solution.py:24
  58.9 5.7 %collective-permute-start.7 = (bf16[3,30,128]{2,1,0:T(8,128)(2,1)S(1)}, bf16[3,30,128]{2,1,0:T(8,128)(2,1)S(1)}, u32[]{:S(2)}, u32[]{:S(2)}) collective-permute-start(bf16[3,30,128]{2,1,0:T(8,128)(2,1)S(1)} %get-tuple-element.195), channel_id=1, source_target_pairs={{1,0},{3,2},{5,4},{7,6},{9,8},{11,10},{13,12},{15,14},{17,16},{19,... | collective-permute-start | bytes 69128 | tf_op jit(solution)/shard_map/ppermute | solution.py:25
  87.7 6.4 %collective-permute-start.8 = (bf16[45,3,128]{2,1,0:T(4,128)(2,1)S(1)}, bf16[45,3,128]{2,1,0:T(4,128)(2,1)S(1)}, u32[]{:S(2)}, u32[]{:S(2)}) collective-permute-start(bf16[45,3,128]{2,1,0:T(4,128)(2,1)S(1)} %get-tuple-element.203), channel_id=1, source_target_pairs={{0,2},{2,4},{4,6},{6,8},{8,10},{10,12},{12,14},{14,16},{16,18},{18... | collective-permute-start | bytes 103688 | tf_op jit(solution)/shard_map/ppermute | solution.py:24
  87.8 6.3 %collective-permute-start.9 = (bf16[45,3,128]{2,1,0:T(4,128)(2,1)S(1)}, bf16[45,3,128]{2,1,0:T(4,128)(2,1)S(1)}, u32[]{:S(2)}, u32[]{:S(2)}) collective-permute-start(bf16[45,3,128]{2,1,0:T(4,128)(2,1)S(1)} %get-tuple-element.204), channel_id=1, source_target_pairs={{2,0},{4,2},{6,4},{8,6},{10,8},{12,10},{14,12},{16,14},{18,16},{20... | collective-permute-start | bytes 103688 | tf_op jit(solution)/shard_map/ppermute | solution.py:25
  94.2 11.7 %collective-permute-start.10 = (bf16[3,30,128]{2,1,0:T(8,128)(2,1)S(1)}, bf16[3,30,128]{2,1,0:T(8,128)(2,1)S(1)}, u32[]{:S(2)}, u32[]{:S(2)}) collective-permute-start(bf16[3,30,128]{2,1,0:T(8,128)(2,1)S(1)} %get-tuple-element.190), channel_id=1, source_target_pairs={{1,0},{3,2},{5,4},{7,6},{9,8},{11,10},{13,12},{15,14},{17,16},{19,... | collective-permute-start | bytes 69128 | tf_op jit(solution)/shard_map/ppermute | solution.py:25
  95.6 10.2 %collective-permute-start.11 = (bf16[3,30,128]{2,1,0:T(8,128)(2,1)S(1)}, bf16[3,30,128]{2,1,0:T(8,128)(2,1)S(1)}, u32[]{:S(2)}, u32[]{:S(2)}) collective-permute-start(bf16[3,30,128]{2,1,0:T(8,128)(2,1)S(1)} %get-tuple-element.191), channel_id=1, source_target_pairs={{0,1},{2,3},{4,5},{6,7},{8,9},{10,11},{12,13},{14,15},{16,17},{18,... | collective-permute-start | bytes 69128 | tf_op jit(solution)/shard_map/ppermute | solution.py:24
  125.8 45.5 %copy-start.18 = (bf16[45,3,128]{2,1,0:T(4,128)(2,1)S(1)}, bf16[45,3,128]{2,1,0:T(4,128)(2,1)}, u32[]{:S(2)}) copy-start(bf16[45,3,128]{2,1,0:T(4,128)(2,1)} %get-tuple-element.201) | copy-start | bytes 103684
  125.8 58.4 %copy-start.6 = (f32[1,128,512]{2,1,0:T(8,128)S(1)}, f32[1,128,512]{2,1,0:T(8,128)}, u32[]{:S(2)}) copy-start(f32[1,128,512]{2,1,0:T(8,128)} %convolution_bitcast_fusion.3) | copy-start | bytes 786436
  171.3 2.2 collective-permute-start.13
  172.1 6.2 %collective-permute-start.12 = (bf16[45,3,128]{2,1,0:T(4,128)(2,1)S(1)}, bf16[45,3,128]{2,1,0:T(4,128)(2,1)S(1)}, u32[]{:S(2)}, u32[]{:S(2)}) collective-permute-start(bf16[45,3,128]{2,1,0:T(4,128)(2,1)S(1)} %get-tuple-element.202), channel_id=1, source_target_pairs={{0,2},{2,4},{4,6},{6,8},{8,10},{10,12},{12,14},{14,16},{16,18},{18... | collective-permute-start | bytes 103688 | tf_op jit(solution)/shard_map/ppermute | solution.py:24
  178.4 7.4 %collective-permute-start.14 = (bf16[3,30,128]{2,1,0:T(8,128)(2,1)S(1)}, bf16[3,30,128]{2,1,0:T(8,128)(2,1)S(1)}, u32[]{:S(2)}, u32[]{:S(2)}) collective-permute-start(bf16[3,30,128]{2,1,0:T(8,128)(2,1)S(1)} %get-tuple-element.186), channel_id=1, source_target_pairs={{1,0},{3,2},{5,4},{7,6},{9,8},{11,10},{13,12},{15,14},{17,16},{19,... | collective-permute-start | bytes 69128 | tf_op jit(solution)/shard_map/ppermute | solution.py:25
  179.7 6.1 %collective-permute-start.15 = (bf16[3,30,128]{2,1,0:T(8,128)(2,1)S(1)}, bf16[3,30,128]{2,1,0:T(8,128)(2,1)S(1)}, u32[]{:S(2)}, u32[]{:S(2)}) collective-permute-start(bf16[3,30,128]{2,1,0:T(8,128)(2,1)S(1)} %get-tuple-element.187), channel_id=1, source_target_pairs={{0,1},{2,3},{4,5},{6,7},{8,9},{10,11},{12,13},{14,15},{16,17},{18,... | collective-permute-start | bytes 69128 | tf_op jit(solution)/shard_map/ppermute | solution.py:24
  (179 other events, 2164.0 us)
Sparse Core Ops, SparseCore 0:
  185.9 127.5 all-reduce.3
where the time goes:
time: 325 us; the launch traced here: 324 us
  waiting for transfers between devices  137 us (42%)
  other arithmetic  52.3 us (16%)
  blocking collectives  38.9 us (12%)
  starting transfers between devices  35.3 us (11%)
  matrix products  25.1 us (8%)
  local copies, waits for them, and re-layouts  18.7 us (6%)
  between operations  17.1 us (5%)
    psum x1, waiting for transfers between devices, sum_everything(): lax.psum((kernel_part, conv_part, gain_part, shift_part, first_part, firs...  121 us
    psum x1, blocking collectives, sum_everything(): lax.psum((kernel_part, conv_part, gain_part, shift_part, first_part, firs...  38.9 us
    ppermute x8, starting transfers between devices, with_halo(): after = lax.ppermute(first, axis, down)  19.8 us
    ppermute x8, starting transfers between devices, with_halo(): before = lax.ppermute(last, axis, up)  15.4 us
    dot_general x2, matrix products, block_forward(): jnp.dot(lifted, weight_in, preferred_element_type=jnp.float32) + bias_in  13 us
    reduce_sum x2, other arithmetic, block_forward(): center = mixed_sum - jnp.mean(mixed_sum, axis=-1, keepdims=True)  9.99 us
    reduce_sum x6, other arithmetic, block_backward(): tap_sums.append(jnp.sum(spread * piece, axis=(0, 1)))  9.28 us
    ppermute x8, waiting for transfers between devices, with_halo(): after = lax.ppermute(first, axis, down)  8.69 us
  transfers between devices with their start and end apart: 17, of which 7 were waited for; matrix products, arithmetic and copies ran while one was open for 8% of the time, Pallas kernels for 0%

commit v1 on v0

v1 whole, which is shorter than its diff:
```python
import functools
import math

import jax
import jax.numpy as jnp
from jax import lax
from jax.experimental import pallas as pl
from jax.experimental.pallas import tpu as pltpu
from jax.sharding import PartitionSpec as P

KSIZE = 7
MARGIN = KSIZE // 2
TAPS = KSIZE * KSIZE
BLOCKS = 2
EPS_NORM = 1e-06
INV_ROOT_TWO = 0.7071067811865476
INV_ROOT_TWO_PI = 0.3989422804014327
LAND = 1024.0
LAND_BOUND = 512.0
F32 = jnp.float32
BF16 = jnp.bfloat16
STEP = 3
STATE_AT = 11
FIELD_AT = 8
INNER_AT = 3
WIDE = 3 * MARGIN
NARROW = 2 * MARGIN


def round_up(size, unit):
    return (size + unit - 1) // unit * unit


def conv_rows(source, base, first, count, width, kernel_ref, flip):
    sums = [None] * count
    for tap_col in range(KSIZE):
        taps = []
        for tap_row in range(KSIZE):
            index = tap_row * KSIZE + tap_col
            taps.append(kernel_ref[pl.ds(TAPS - 1 - index if flip else index, 1), :])
        for row in range(count + KSIZE - 1):
            piece = source[base + row, pl.ds(first + tap_col, width), :]
            for tap_row in range(KSIZE):
                out = row - tap_row
                if 0 <= out < count:
                    term = piece * taps[tap_row]
                    sums[out] = term if sums[out] is None else sums[out] + term
    return jnp.concatenate(sums, axis=0)


def normal_parts(hidden):
    cumulative = 0.5 + 0.5 * lax.erf(hidden * INV_ROOT_TWO)
    return cumulative, jnp.exp(-0.5 * hidden * hidden)


def fold(values):
    return jnp.sum(values.reshape(values.shape[0] // 8, 8, values.shape[1]), axis=0)


def normalise(mixed):
    center = mixed - jnp.mean(mixed, axis=-1, keepdims=True)
    inverse = lax.rsqrt(jnp.mean(center * center, axis=-1, keepdims=True) + EPS_NORM)
    return center * inverse, inverse


def normalise_back(grad, normed, inverse):
    return inverse * (
        grad
        - jnp.mean(grad, axis=-1, keepdims=True)
        - normed * jnp.mean(grad * normed, axis=-1, keepdims=True)
    )


def rows_of(ref, base, first, count, width):
    return jnp.concatenate(
        [ref[base + row, pl.ds(first, width), :] for row in range(count)], axis=0
    )


CONTRACT_COLS = (((1,), (1,)), ((), ()))
CONTRACT_ROWS = (((0,), (0,)), ((), ()))


def dot(left, right):
    return jnp.dot(left, right, preferred_element_type=F32)


def dot_cols(left, right):
    return lax.dot_general(left, right, CONTRACT_COLS, preferred_element_type=F32)


def dot_rows(left, right):
    return lax.dot_general(left, right, CONTRACT_ROWS, preferred_element_type=F32)


def tap_sums(grad_ref, grad_row, grad_col, field_ref, field_row, field_col, height, width, out):
    for cols in ((0, 1), (2, 3), (4, 5), (6,)):

        def advance(row, sums):
            sums = list(sums)
            grad = grad_ref[grad_row + row, pl.ds(grad_col, width), :]
            for tap_row in range(KSIZE):
                for place, tap_col in enumerate(cols):
                    piece = field_ref[
                        field_row + row + tap_row, pl.ds(field_col + tap_col, width), :
                    ]
                    index = place * KSIZE + tap_row
                    sums[index] = sums[index] + fold(grad * piece)
            return tuple(sums)

        zeros = tuple(jnp.zeros((8, grad_ref.shape[2]), F32) for _ in range(KSIZE * len(cols)))
        sums = lax.fori_loop(0, height, advance, zeros)
        for place, tap_col in enumerate(cols):
            for tap_row in range(KSIZE):
                total = jnp.sum(sums[place * KSIZE + tap_row], axis=0, keepdims=True)
                out[pl.ds(tap_row * KSIZE + tap_col, 1), :] = total


def tile_kernel(
    sizes,
    starts,
    state_in,
    coded_in,
    dw_in,
    conv_bias,
    norm_gain,
    norm_bias,
    weight_in,
    bias_in,
    weight_out,
    bias_out,
    layer_scale,
    output,
    mixed_out,
    masked_out,
    grads_out,
    state,
    coded,
    kernels,
    field,
    inner,
    result,
    normed_own,
    inverse_own,
    branch_own,
    slope_own,
    active_own,
    hidden_own,
    lifted_own,
    branch_grad_own,
    mixed_own,
    active_all,
    hidden_all,
    lifted_all,
    branch_grad_all,
    sums,
    hidden_sums,
    taps,
):
    height, breadth, first_rows, second_rows, window_rows = sizes
    channels = state.shape[2]
    own_start = starts[0]
    second_start = starts[1]
    first_start = starts[2]
    first_width = field.shape[1]
    second_width = inner.shape[1]
    pad = MARGIN

    for ref in (state, coded, field, inner):
        edge = jnp.zeros((pad,) + ref.shape[1:], F32)
        ref[pl.ds(0, pad)] = edge
        ref[pl.ds(pad + window_rows, pad)] = edge
    state[pl.ds(pad, window_rows)] = state_in[...].astype(F32)
    coded[pl.ds(pad, window_rows)] = coded_in[...].astype(F32)
    kernels[...] = dw_in[...].astype(F32)
    sums[...] = jnp.zeros_like(sums)
    hidden_sums[...] = jnp.zeros_like(hidden_sums)

    def param(ref, layer):
        return ref[pl.ds(layer, 1), :]

    def forward_first(step, carry):
        row = first_start + step * STEP
        cells = STEP * first_width
        mixed = conv_rows(state, row, 0, STEP, first_width, kernels.at[0], False)
        normed, inverse = normalise(mixed + param(conv_bias, 0))
        lifted = (normed * param(norm_gain, 0) + param(norm_bias, 0)).astype(BF16)
        hidden = dot(lifted, weight_in[0]) + param(bias_in, 0)
        cumulative, bell = normal_parts(hidden)
        active = hidden * cumulative
        branch = dot(active.astype(BF16), weight_out[0]) + param(bias_out, 0)
        center = rows_of(state, row + pad, MARGIN, STEP, first_width)
        mark = rows_of(coded, row + pad, 0, STEP, first_width)
        value = jnp.where(mark < LAND_BOUND, center + param(layer_scale, 0) * branch, 0.0)
        value = value.reshape(STEP, first_width, channels)

        for index in range(STEP):
            field[row + pad + index] = value[index]

        def own(values):
            shape = (STEP, first_width, values.shape[1])
            return values.reshape(shape)[:, FIELD_AT : FIELD_AT + breadth]

        slope = own(cumulative) + own(hidden) * (own(bell) * INV_ROOT_TWO_PI)
        spots = pl.ds(row, STEP)
        slope_own[spots] = slope
        active_own[spots] = own(active).astype(BF16)
        normed_own[spots] = own(normed)
        inverse_own[spots] = own(jnp.broadcast_to(inverse, normed.shape))
        branch_own[spots] = own(branch)
        lifted_own[spots] = own(normed * param(norm_gain, 0) + param(norm_bias, 0)).astype(BF16)
        return carry

    lax.fori_loop(0, first_rows // STEP, forward_first, 0)

    def both_second(step, carry):
        row = second_start + step * STEP
        cells = STEP * second_width
        shift = FIELD_AT - INNER_AT
        mixed = conv_rows(
            field, row, shift - MARGIN, STEP, second_width, kernels.at[1], False
        )
        normed, inverse = normalise(mixed + param(conv_bias, 1))
        lifted = normed * param(norm_gain, 1) + param(norm_bias, 1)
        hidden = dot(lifted.astype(BF16), weight_in[1]) + param(bias_in, 1)
        cumulative, bell = normal_parts(hidden)
        active = (hidden * cumulative).astype(BF16)
        branch = dot(active, weight_out[1]) + param(bias_out, 1)
        center = rows_of(field, row + pad, shift, STEP, second_width)
        mark = rows_of(coded, row + pad, shift, STEP, second_width)
        ocean = mark < LAND_BOUND
        value = jnp.where(ocean, center + param(layer_scale, 1) * branch, 0.0)
        value = value.reshape(STEP, second_width, channels)
        masked = jnp.where(ocean, mark, 0.0)
        grad_branch = (masked * param(layer_scale, 1)).astype(BF16)
        grad_active = dot_cols(grad_branch, weight_out[1])
        slope = cumulative + hidden * (bell * INV_ROOT_TWO_PI)
        grad_hidden = (grad_active * slope).astype(BF16)
        grad_lifted = dot_cols(grad_hidden, weight_in[1])
        grad_mixed = normalise_back(grad_lifted * param(norm_gain, 1), normed, inverse)
        grad_mixed = grad_mixed.reshape(STEP, second_width, channels)
        for index in range(STEP):
            result[row + index] = value[index]
            inner[row + pad + index] = grad_mixed[index]

        shape = (STEP, second_width, channels)
        row_of = lax.broadcasted_iota(jnp.int32, shape, 0) + (row - own_start)
        col_of = lax.broadcasted_iota(jnp.int32, shape, 1) - INNER_AT
        inside = (row_of >= 0) & (row_of < height) & (col_of >= 0) & (col_of < breadth)
        inside = jnp.where(inside, 1.0, 0.0).astype(F32).reshape(cells, channels)
        own_lifted = grad_lifted * inside
        own_branch = grad_branch.astype(F32) * inside
        sums[1, 0] += fold(masked * branch * inside)
        sums[1, 1] += fold(own_branch)
        sums[1, 2] += fold(own_lifted * normed)
        sums[1, 3] += fold(own_lifted)
        wide = jnp.concatenate([inside] * (hidden.shape[1] // channels), axis=1)
        hidden_sums[1] += fold(grad_hidden.astype(F32) * wide)
        spots = pl.ds(pl.multiple_of(step * cells, cells), cells)
        active_all[spots] = active
        hidden_all[spots] = grad_hidden
        lifted_all[spots] = (lifted * inside).astype(BF16)
        branch_grad_all[spots] = own_branch.astype(BF16)
        return carry

    lax.fori_loop(0, second_rows // STEP, both_second, 0)

    def backward_first(step, carry):
        row = own_start + step * STEP
        cells = STEP * breadth
        mark = rows_of(coded, row + pad, FIELD_AT, STEP, breadth)
        ocean = mark < LAND_BOUND
        masked_next = jnp.where(ocean, mark, 0.0)
        spread = conv_rows(inner, row, 0, STEP, breadth, kernels.at[1], True)
        masked = jnp.where(ocean, masked_next + spread, 0.0)
        grad_branch = (masked * param(layer_scale, 0)).astype(BF16)
        grad_active = dot_cols(grad_branch, weight_out[0])
        slope = slope_own[pl.ds(row, STEP)].reshape(cells, grad_active.shape[1])
        grad_hidden = (grad_active * slope).astype(BF16)
        grad_lifted = dot_cols(grad_hidden, weight_in[0])
        normed = normed_own[pl.ds(row, STEP)].reshape(cells, channels)
        inverse = inverse_own[pl.ds(row, STEP)].reshape(cells, channels)
        grad_mixed = normalise_back(grad_lifted * param(norm_gain, 0), normed, inverse)
        branch = branch_own[pl.ds(row, STEP)].reshape(cells, channels)
        sums[0, 0] += fold(masked * branch)
        sums[0, 1] += fold(grad_branch.astype(F32))
        sums[0, 2] += fold(grad_lifted * normed)
        sums[0, 3] += fold(grad_lifted)
        sums[0, 4] += fold(grad_mixed)
        hidden_sums[0] += fold(grad_hidden.astype(F32))
        inner_rows = rows_of(inner, row + pad, INNER_AT, STEP, breadth)
        sums[1, 4] += fold(inner_rows)
        tile = pl.ds(step * STEP, STEP)
        shape = (STEP, breadth, channels)
        grad_mixed = grad_mixed.reshape(shape)
        mixed_own[tile] = grad_mixed
        mixed_out[tile] = grad_mixed.astype(BF16)
        masked_out[tile] = masked.reshape(shape).astype(BF16)
        hidden_own[tile] = grad_hidden.reshape(STEP, breadth, grad_hidden.shape[1])
        branch_grad_own[tile] = grad_branch.reshape(shape)
        value = rows_of(result, row, INNER_AT, STEP, breadth)
        output[tile] = value.reshape(shape).astype(BF16)
        return carry

    lax.fori_loop(0, height // STEP, backward_first, 0)

    hidden_units = weight_in.shape[2]
    groups = hidden_units // channels
    tile = pl.ds(own_start, height)
    cells = height * breadth

    def flat(ref, spots):
        return ref[spots].reshape(cells, ref.shape[2])

    operands = (
        (
            flat(lifted_own, tile),
            flat(hidden_own, pl.ds(0, height)),
            flat(active_own, tile),
            flat(branch_grad_own, pl.ds(0, height)),
        ),
        (lifted_all[...], hidden_all[...], active_all[...], branch_grad_all[...]),
    )
    for layer, (lifted, grad_hidden, active, grad_branch) in enumerate(operands):
        at = layer * 2 * hidden_units
        grad_in = dot_rows(lifted, grad_hidden)
        for group in range(groups):
            grads_out[pl.ds(at + group * channels, channels), :] = grad_in[
                :, group * channels : (group + 1) * channels
            ].astype(BF16)
        grad_out = dot_rows(grad_branch, active)
        for group in range(groups):
            grads_out[pl.ds(at + hidden_units + group * channels, channels), :] = grad_out[
                :, group * channels : (group + 1) * channels
            ].T.astype(BF16)

    at = BLOCKS * 2 * hidden_units
    tail = grads_out.shape[0] - at
    taps[...] = jnp.zeros_like(taps)
    for layer in range(BLOCKS):
        base = layer * (TAPS + 5 + groups)
        if layer:
            tap_sums(
                inner,
                own_start + pad,
                INNER_AT,
                field,
                own_start,
                FIELD_AT - MARGIN,
                height,
                breadth,
                taps.at[pl.ds(base, TAPS)],
            )
        else:
            tap_sums(
                mixed_own,
                0,
                0,
                state,
                own_start,
                STATE_AT - MARGIN,
                height,
                breadth,
                taps.at[pl.ds(base, TAPS)],
            )
        for member in range(5):
            taps[pl.ds(base + TAPS + member, 1), :] = jnp.sum(
                sums[layer, member], axis=0, keepdims=True
            )
        hidden_total = jnp.sum(hidden_sums[layer], axis=0, keepdims=True)
        for group in range(groups):
            taps[pl.ds(base + TAPS + 5 + group, 1), :] = hidden_total[
                :, group * channels : (group + 1) * channels
            ]
    grads_out[pl.ds(at, tail), :] = taps[...].astype(BF16)


def state_kernel(window, masked, dw_in, out, wide, kernels):
    height, breadth, channels = masked.shape
    wide[...] = window[...].astype(F32)
    kernels[...] = dw_in[...].astype(F32)

    def advance(step, carry):
        row = step * STEP
        spread = conv_rows(wide, row, 0, STEP, breadth, kernels, True)
        tile = pl.ds(row, STEP)
        shape = (STEP, breadth, channels)
        out[tile] = (masked[tile].astype(F32) + spread.reshape(shape)).astype(BF16)
        return carry

    lax.fori_loop(0, height // STEP, advance, 0)


class Links:
    def __init__(self, mesh):
        self.lon = mesh.shape["lon"]
        self.lat = mesh.shape["lat"]
        self.axes = ("lon", "lat")

    def shift_lon(self, values, by):
        pairs = [(place, (place + by) % self.lon) for place in range(self.lon)]
        return lax.ppermute(values, "lon", pairs)

    def shift_lat(self, values, by):
        pairs = [
            (place, place + by) for place in range(self.lat) if 0 <= place + by < self.lat
        ]
        return lax.ppermute(values, "lat", pairs)

    def swap(self, values, lon_bits, lat_bits):
        pairs = []
        for lon in range(self.lon):
            for lat in range(self.lat):
                there = (lon ^ lon_bits) * self.lat + (lat ^ lat_bits)
                pairs.append((lon * self.lat + lat, there))
        return lax.ppermute(values, self.axes, pairs)

    def extend_lat(self, field, width, outside):
        place = lax.axis_index("lat")
        if self.lat == 2:
            mine = jnp.where(place == 0, field[-width:], field[:width])
            other = lax.ppermute(mine, "lat", [(0, 1), (1, 0)])
            below = jnp.concatenate([field, other], axis=0)
            above = jnp.concatenate([other, field], axis=0)
            return jnp.where(place == 0, below, above)
        before = self.shift_lat(field[-width:], 1)
        after = self.shift_lat(field[:width], -1)
        before = jnp.where(place == 0, outside, before)
        after = jnp.where(place == self.lat - 1, outside, after)
        return jnp.concatenate([before, field, after], axis=0)

    def sum_all(self, rows):
        lon = lax.axis_index("lon")
        lat = lax.axis_index("lat")
        bits = [(1 << bit, 0) for bit in range(self.lon.bit_length() - 1)]
        bits = bits[:1] + [(0, 1 << bit) for bit in range(self.lat.bit_length() - 1)] + bits[1:]

        def code(group):
            total = jnp.int32(0)
            for index, (lon_bit, lat_bit) in enumerate(group):
                held = (lon // lon_bit) % 2 if lon_bit else (lat // lat_bit) % 2
                total = total + held * (1 << index)
            return total

        def merged(group, choice):
            lon_bits = sum(bit[0] for index, bit in enumerate(group) if choice >> index & 1)
            lat_bits = sum(bit[1] for index, bit in enumerate(group) if choice >> index & 1)
            return lon_bits, lat_bits

        def scatter(values, group):
            count = 1 << len(group)
            pieces = values.reshape(count, -1, values.shape[1])
            here = code(group)
            total = lax.dynamic_index_in_dim(pieces, here, 0, False).astype(F32)
            for choice in range(1, count):
                sent = lax.dynamic_index_in_dim(pieces, here ^ choice, 0, False)
                total = total + self.swap(sent, *merged(group, choice)).astype(F32)
            return total.astype(BF16)

        def exchange(values, group):
            total = values.astype(F32)
            for choice in range(1, 1 << len(group)):
                total = total + self.swap(values, *merged(group, choice)).astype(F32)
            return total.astype(BF16)

        def gather(values, group):
            count = 1 << len(group)
            pieces = [values]
            for choice in range(1, count):
                pieces.append(self.swap(values, *merged(group, choice)))
            stack = jnp.stack(pieces)
            here = code(group)
            ordered = [
                lax.dynamic_index_in_dim(stack, here ^ place, 0, False) for place in range(count)
            ]
            return jnp.concatenate(ordered, axis=0)

        pair, quad, rest = bits[:1], bits[1:3], bits[3:]
        values = scatter(scatter(rows, pair), quad)
        while rest:
            values = exchange(values, rest[:2])
            rest = rest[2:]
        return gather(gather(values, quad), pair)


def on_device(links, state, land_sea, cotangent, *params):
    dw_kernel, weight_in = params[0], params[4]
    height, breadth, channels = state.shape
    hidden_units = weight_in.shape[2]
    groups = hidden_units // channels
    grad_norm = 1.0 / math.sqrt(links.lat * height * links.lon * breadth)
    lat = lax.axis_index("lat")
    sides = 1 if links.lat == 2 else 2
    window_rows = height + sides * WIDE
    first_rows = height + sides * NARROW
    second_rows = height + sides * MARGIN

    def start(margin):
        skipped = WIDE - margin
        return lat * skipped if sides == 1 else jnp.int32(skipped)

    starts = jnp.stack([start(0), start(MARGIN), start(NARROW)]).astype(jnp.int32)

    ocean = (land_sea != 0)[:, :, None]
    coded = jnp.where(ocean, cotangent, jnp.asarray(LAND, BF16))
    packed = jnp.concatenate([state, coded], axis=1)
    outside = jnp.concatenate(
        [
            jnp.zeros((1, breadth, 1), BF16),
            jnp.full((1, breadth, 1), LAND, BF16),
        ],
        axis=1,
    )
    packed = links.extend_lat(packed, WIDE, outside)
    state_rows = packed[:, :breadth]
    coded_rows = packed[:, breadth:]
    east_edge = jnp.concatenate([state_rows[:, -WIDE:], coded_rows[:, -NARROW:]], axis=1)
    west_edge = jnp.concatenate([state_rows[:, :WIDE], coded_rows[:, :NARROW]], axis=1)
    west = links.shift_lon(east_edge, 1)
    east = links.shift_lon(west_edge, -1)

    def window(parts, at, pitch):
        used = at + sum(part.shape[1] for part in parts)
        lead = jnp.zeros((window_rows, at, channels), BF16)
        rest = jnp.zeros((window_rows, pitch - used, channels), BF16)
        return jnp.concatenate([lead, *parts, rest], axis=1)

    state_pitch, field_pitch, inner_pitch = (
        round_up(breadth + size, 8) for size in (STATE_AT + WIDE, FIELD_AT + NARROW, NARROW)
    )
    state_window = window(
        [west[:, :WIDE], state_rows, east[:, :WIDE]], STATE_AT - WIDE, state_pitch
    )
    coded_window = window(
        [west[:, WIDE:], coded_rows, east[:, WIDE:]], FIELD_AT - NARROW, field_pitch
    )

    padded_rows = window_rows + 2 * MARGIN
    all_cells = second_rows * inner_pitch
    small_rows = round_up(BLOCKS * (TAPS + 5 + groups), 16)
    grad_rows = BLOCKS * 2 * hidden_units + small_rows
    unit = 16 * 8
    small_rows += round_up(grad_rows, unit) - grad_rows
    grad_rows = round_up(grad_rows, unit)
    tile = (height, breadth, channels)
    vmem = pl.BlockSpec(memory_space=pltpu.VMEM)
    own_rows = (window_rows, breadth)
    scratch = [
        pltpu.VMEM((padded_rows, state_pitch, channels), F32),
        pltpu.VMEM((padded_rows, field_pitch, channels), F32),
        pltpu.VMEM((BLOCKS, TAPS, channels), F32),
        pltpu.VMEM((padded_rows, field_pitch, channels), F32),
        pltpu.VMEM((padded_rows, inner_pitch, channels), F32),
        pltpu.VMEM((window_rows, inner_pitch, channels), F32),
        pltpu.VMEM(own_rows + (channels,), F32),
        pltpu.VMEM(own_rows + (channels,), F32),
        pltpu.VMEM(own_rows + (channels,), F32),
        pltpu.VMEM(own_rows + (hidden_units,), F32),
        pltpu.VMEM(own_rows + (hidden_units,), BF16),
        pltpu.VMEM((height, breadth, hidden_units), BF16),
        pltpu.VMEM(own_rows + (channels,), BF16),
        pltpu.VMEM(tile, BF16),
        pltpu.VMEM(tile, F32),
        pltpu.VMEM((all_cells, hidden_units), BF16),
        pltpu.VMEM((all_cells, hidden_units), BF16),
        pltpu.VMEM((all_cells, channels), BF16),
        pltpu.VMEM((all_cells, channels), BF16),
        pltpu.VMEM((BLOCKS, 5, 8, channels), F32),
        pltpu.VMEM((BLOCKS, 8, hidden_units), F32),
        pltpu.VMEM((small_rows, channels), F32),
    ]
    sizes = (height, breadth, first_rows, second_rows, window_rows)
    taps_in = dw_kernel.reshape(BLOCKS, TAPS, channels)
    output, grad_mixed, masked, grads = pl.pallas_call(
        functools.partial(tile_kernel, sizes),
        out_shape=(
            jax.ShapeDtypeStruct(tile, BF16),
            jax.ShapeDtypeStruct(tile, BF16),
            jax.ShapeDtypeStruct(tile, BF16),
            jax.ShapeDtypeStruct((grad_rows, channels), BF16),
        ),
        in_specs=[pl.BlockSpec(memory_space=pltpu.SMEM)] + [vmem] * 11,
        out_specs=(vmem,) * 4,
        scratch_shapes=scratch,
        compiler_params=pltpu.CompilerParams(vmem_limit_bytes=48 * 1024 * 1024),
        cost_estimate=pl.CostEstimate(
            flops=20 * all_cells * channels * hidden_units,
            bytes_accessed=4 * height * breadth * channels * 4,
            transcendentals=0,
        ),
    )(starts, state_window, coded_window, taps_in, *params[1:])

    before = links.shift_lon(grad_mixed[:, -MARGIN:], 1)
    after = links.shift_lon(grad_mixed[:, :MARGIN], -1)
    beside = jnp.concatenate([before, grad_mixed, after], axis=1)
    spread = links.extend_lat(beside, MARGIN, jnp.zeros((1, 1, 1), BF16))
    if sides == 1:
        empty = jnp.zeros((MARGIN,) + spread.shape[1:], BF16)
        first = jnp.concatenate([empty, spread], axis=0)
        last = jnp.concatenate([spread, empty], axis=0)
        spread = jnp.where(lat == 0, first, last)
    pitch = round_up(spread.shape[1], 8)
    spread = jnp.pad(spread, ((0, 0), (0, pitch - spread.shape[1]), (0, 0)))
    grad_state = pl.pallas_call(
        state_kernel,
        out_shape=jax.ShapeDtypeStruct(tile, BF16),
        in_specs=[vmem] * 3,
        out_specs=vmem,
        scratch_shapes=[pltpu.VMEM(spread.shape, F32), pltpu.VMEM((TAPS, channels), F32)],
        compiler_params=pltpu.CompilerParams(vmem_limit_bytes=16 * 1024 * 1024),
    )(spread, masked, taps_in[0])

    total = links.sum_all(grads).astype(F32) * grad_norm
    size = 2 * hidden_units
    at = BLOCKS * size
    weights = total[:at].reshape(BLOCKS, 2, groups, channels, channels)
    grad_in = weights[:, 0].transpose(0, 2, 1, 3).reshape(BLOCKS, channels, hidden_units)
    grad_out = weights[:, 1].reshape(BLOCKS, hidden_units, channels)
    small = total[at : at + BLOCKS * (TAPS + 5 + groups)].reshape(BLOCKS, -1, channels)
    grad_kernel = small[:, :TAPS].reshape(BLOCKS, KSIZE, KSIZE, channels)
    grad_bias_in = small[:, TAPS + 5 :].reshape(BLOCKS, hidden_units)
    return (
        output,
        grad_state,
        grad_kernel,
        small[:, TAPS + 4],
        small[:, TAPS + 2],
        small[:, TAPS + 3],
        grad_in,
        grad_bias_in,
        grad_out,
        small[:, TAPS + 1],
        small[:, TAPS],
    )


def solution(mesh):
    tile = P("lat", "lon", None)
    placed = (tile, P("lat", "lon"), tile) + (P(),) * 9
    return jax.shard_map(
        functools.partial(on_device, Links(mesh)),
        mesh=mesh,
        in_specs=placed,
        out_specs=(tile, tile) + (P(),) * 9,
        check_vma=False,
    )
```

time: 325 us -> 102 us (0.31)
  waiting for transfers between devices: 137 us -> 14.1 us
  Pallas kernels: 0 us -> 48.8 us
  other arithmetic: 52.3 us -> 4.02 us
  blocking collectives: 38.9 us -> 0 us
  matrix products: 25.1 us -> 0 us
  between operations: 17.1 us -> 1.06 us
  local copies, waits for them, and re-layouts: 18.7 us -> 7.16 us
  starting transfers between devices: 35.3 us -> 26.7 us
    psum x1 -> x0, waiting for transfers between devices: 121 us -> none  [sum_everything(): lax.psum((kernel_part, conv_part, gain_part, shift_part, first_part, firs...]
    pallas_call x0 -> x2, Pallas kernels: none -> 48.8 us  [the longest x1 45.2 us: on_device(): pl.pallas_call(functools.partial(tile_kernel, sizes), out_shape=(jax.Shap...]
    psum x1 -> x0, blocking collectives: 38.9 us -> none  [sum_everything(): lax.psum((kernel_part, conv_part, gain_part, shift_part, first_part, firs...]
    dot_general x12 -> x0, matrix products: 25.1 us -> none  [the longest x2 13 us: block_forward(): jnp.dot(lifted, weight_in, preferred_element_type=jnp.float32) + bias_in]
    reduce_sum x14 -> x0, other arithmetic: 24.3 us -> none  [the longest x2 9.99 us: block_forward(): center = mixed_sum - jnp.mean(mixed_sum, axis=-1, keepdims=True)]
    convert_element_type x5 -> x3, other arithmetic: 14.6 us -> 0.16 us  [the longest x2 0.12 us: scatter(): return total.astype(BF16)]
    ppermute x16 -> x17, starting transfers between devices: 35.3 us -> 26.7 us  [the longest x11 13.2 us: swap(): return lax.ppermute(values, self.axes, pairs)]
    mul x15 -> x1, other arithmetic: 8.53 us -> 0.09 us  [on_device(): total = links.sum_all(grads).astype(F32) * grad_norm]
  transfers between devices with their start and end apart: 17 -> 17, of which waited for: 7 -> 10; matrix products, arithmetic and copies ran while one was open for 8% -> 1% of each run, Pallas kernels for 0% -> 4%
where the time goes in v1:
time: 102 us
  Pallas kernels  48.8 us (48%)
  starting transfers between devices  26.7 us (26%)
  waiting for transfers between devices  14.1 us (14%)
  local copies, waits for them, and re-layouts  7.16 us (7%)
  other arithmetic  4.02 us (4%)
  between operations  1.06 us (1%)
    pallas_call x1, Pallas kernels, on_device(): pl.pallas_call(functools.partial(tile_kernel, sizes), out_shape=(jax.Shap...  45.2 us
    ppermute x11, starting transfers between devices, swap(): return lax.ppermute(values, self.axes, pairs)  13.2 us
    ppermute x4, starting transfers between devices, shift_lon(): return lax.ppermute(values, 'lon', pairs)  9.02 us
    ppermute x11, waiting for transfers between devices, swap(): return lax.ppermute(values, self.axes, pairs)  7.64 us
    ppermute x2, starting transfers between devices, extend_lat(): other = lax.ppermute(mine, 'lat', [(0, 1), (1, 0)])  4.45 us
    pallas_call x1, Pallas kernels, on_device(): pl.pallas_call(state_kernel, out_shape=jax.ShapeDtypeStruct(tile, BF16),...  3.58 us
    ppermute x4, waiting for transfers between devices, shift_lon(): return lax.ppermute(values, 'lon', pairs)  3.52 us
    ppermute x2, waiting for transfers between devices, extend_lat(): other = lax.ppermute(mine, 'lat', [(0, 1), (1, 0)])  2.96 us
  transfers between devices with their start and end apart: 17, of which 10 were waited for; matrix products, arithmetic and copies ran while one was open for 1% of the time, Pallas kernels for 4%

profile of v1, /device:TPU:0, one launch (start us, length us, event | category | flops | bytes accessed | tf_op | source)
XLA Modules:
  0.0 101.9 jit_solution(4117154054311196715)
XLA Ops:
  1.5 1.2 %broadcast_select_fusion = bf16[45,24,128]{2,1,0:T(8,128)(2,1)S(1)} fusion(bf16[45,24,128]{2,1,0:T(8,128)(2,1)} %param.14, pred[45,24]{1,0:T(8,128)(4,1)S(1)} %copy.29), kind=kLoop, calls=%fused_computation.18 | loop fusion | flops 138240 | bytes 554040 | tf_op jit(solution)/shard_map/jit(_where)/select_n | solution.py:505
  2.7 0.9 fusion.8
  3.6 3.0 %collective-permute-start = (bf16[9,48,128]{2,1,0:T(8,128)(2,1)S(1)}, bf16[9,48,128]{2,1,0:T(8,128)(2,1)S(1)}, u32[]{:S(2)}, u32[]{:S(2)}) collective-permute-start(bf16[9,48,128]{2,1,0:T(8,128)(2,1)S(1)} %fusion.8), channel_id=1, source_target_pairs={{0,1},{1,0},{2,3},{3,2},{4,5},{5,4},{6,7},{7,6},{8,9},{9,8},{10,11... | collective-permute-start | bytes 331784 | tf_op jit(solution)/shard_map/ppermute | solution.py:422
  6.7 3.0 %collective-permute-done = bf16[9,48,128]{2,1,0:T(8,128)(2,1)S(1)} collective-permute-done((bf16[9,48,128]{2,1,0:T(8,128)(2,1)S(1)}, bf16[9,48,128]{2,1,0:T(8,128)(2,1)S(1)}, u32[]{:S(2)}, u32[]{:S(2)}) %collective-permute-start) | collective-permute-done | bytes 110624 | tf_op jit(solution)/shard_map/ppermute | solution.py:422
  10.2 4.5 %collective-permute-start.2 = (bf16[54,15,128]{2,1,0:T(8,128)(2,1)S(1)}, bf16[54,15,128]{2,1,0:T(8,128)(2,1)S(1)}, u32[]{:S(2)}, u32[]{:S(2)}) collective-permute-start(bf16[54,15,128]{2,1,0:T(8,128)(2,1)S(1)} %pad_maximum_fusion.3), channel_id=1, source_target_pairs={{0,30},{2,0},{4,2},{6,4},{8,6},{10,8},{12,10},{14,12},{16,14},{18,... | collective-permute-start | bytes 622088 | tf_op jit(solution)/shard_map/ppermute | solution.py:402
  14.7 3.5 %collective-permute-done.1 = bf16[54,15,128]{2,1,0:T(8,128)(2,1)S(1)} collective-permute-done((bf16[54,15,128]{2,1,0:T(8,128)(2,1)S(1)}, bf16[54,15,128]{2,1,0:T(8,128)(2,1)S(1)}, u32[]{:S(2)}, u32[]{:S(2)}) %collective-permute-start.1) | collective-permute-done | bytes 207392 | tf_op jit(solution)/shard_map/ppermute | solution.py:402
  18.8 2.1 %concatenate.47.state_in = bf16[54,48,128]{2,1,0:T(8,128)(2,1)S(1)} concatenate(bf16[54,2,128]{2,1,0:T(2,128)(2,1)S(1)} %broadcast.16, bf16[54,9,128]{2,1,0:T(8,128)(2,1)S(1)} %bitcast.66, bf16[54,24,128]{2,1,0:T(8,128)(2,1)S(1)} %get-tuple-element.44, bf16[54,9,128]{2,1,0:T(8,128)(2,1)S(1)} %bitcast.67, bf16[54,4,128]{2,1,0:T(4,128)(2,1)S(1)} %broadcast_in_dim.19), dimensions={1} | concatenate | bytes 1327104 | tf_op jit(solution)/shard_map/concatenate | solution.py:526
  21.0 45.2 %shard_map.203 = (bf16[45,24,128]{2,1,0:T(8,128)(2,1)}, bf16[45,24,128]{2,1,0:T(8,128)(2,1)S(1)}, bf16[45,24,128]{2,1,0:T(8,128)(2,1)S(1)}, bf16[2176,128]{1,0:T(8,128)(2,1)S(1)}) custom-call(s32[3]{0:T(128)S(1)} %pad_add_fusion.starts, bf16[54,48,128]{2,1,0:T(8,128)(2,1)S(1)} %concatenate.47.state_in, bf16[54,40,128]{2,1,0:T(8,128)(2,1)S(1)} %concatenate.48.coded_in, ...), custom_call_target="tpu_custom_call" | custom-call | flops 2013265920 | bytes 2211840 | tf_op jit(solution)/shard_map/pallas_call | solution.py:574
  66.3 1.6 %collective-permute-start.6 = (bf16[1088,128]{1,0:T(8,128)(2,1)S(1)}, bf16[1088,128]{1,0:T(8,128)(2,1)S(1)}, u32[]{:S(2)}, u32[]{:S(2)}) collective-permute-start(bf16[1088,128]{1,0:T(8,128)(2,1)S(1)} %dynamic-slice_bitcast_fusion), channel_id=1, source_target_pairs={{0,2},{1,3},{2,0},{3,1},{4,6},{5,7},{6,4},{7,5},{8,10},{9,11},{10,... | collective-permute-start | bytes 835592 | tf_op jit(solution)/shard_map/ppermute | solution.py:416
  67.9 1.2 %collective-permute-done.6 = bf16[1088,128]{1,0:T(8,128)(2,1)S(1)} collective-permute-done((bf16[1088,128]{1,0:T(8,128)(2,1)S(1)}, bf16[1088,128]{1,0:T(8,128)(2,1)S(1)}, u32[]{:S(2)}, u32[]{:S(2)}) %collective-permute-start.6) | collective-permute-done | bytes 278560 | tf_op jit(solution)/shard_map/ppermute | solution.py:416
  69.2 1.7 %collective-permute-start.7 = (bf16[272,128]{1,0:T(8,128)(2,1)S(1)}, bf16[272,128]{1,0:T(8,128)(2,1)S(1)}, u32[]{:S(2)}, u32[]{:S(2)}) collective-permute-start(bf16[272,128]{1,0:T(8,128)(2,1)S(1)} %get-tuple-element.57), channel_id=1, source_target_pairs={{0,1},{1,0},{2,3},{3,2},{4,5},{5,4},{6,7},{7,6},{8,9},{9,8},{10,11... | collective-permute-start | bytes 208904 | tf_op jit(solution)/shard_map/ppermute | solution.py:416
  70.8 1.9 %collective-permute-start.8 = (bf16[272,128]{1,0:T(8,128)(2,1)S(1)}, bf16[272,128]{1,0:T(8,128)(2,1)S(1)}, u32[]{:S(2)}, u32[]{:S(2)}) collective-permute-start(bf16[272,128]{1,0:T(8,128)(2,1)S(1)} %get-tuple-element.59), channel_id=1, source_target_pairs={{0,4},{1,5},{2,6},{3,7},{4,0},{5,1},{6,2},{7,3},{8,12},{9,13},{10,... | collective-permute-start | bytes 208904 | tf_op jit(solution)/shard_map/ppermute | solution.py:416
  72.7 1.5 %collective-permute-done.7 = bf16[272,128]{1,0:T(8,128)(2,1)S(1)} collective-permute-done((bf16[272,128]{1,0:T(8,128)(2,1)S(1)}, bf16[272,128]{1,0:T(8,128)(2,1)S(1)}, u32[]{:S(2)}, u32[]{:S(2)}) %collective-permute-start.7) | collective-permute-done | bytes 69664 | tf_op jit(solution)/shard_map/ppermute | solution.py:416
  74.2 1.9 %collective-permute-done.9 = bf16[272,128]{1,0:T(8,128)(2,1)S(1)} collective-permute-done((bf16[272,128]{1,0:T(8,128)(2,1)S(1)}, bf16[272,128]{1,0:T(8,128)(2,1)S(1)}, u32[]{:S(2)}, u32[]{:S(2)}) %collective-permute-start.9) | collective-permute-done | bytes 69664 | tf_op jit(solution)/shard_map/ppermute | solution.py:416
  76.7 3.4 %collective-permute-start.12 = (bf16[272,128]{1,0:T(8,128)(2,1)S(1)}, bf16[272,128]{1,0:T(8,128)(2,1)S(1)}, u32[]{:S(2)}, u32[]{:S(2)}) collective-permute-start(bf16[272,128]{1,0:T(8,128)(2,1)S(1)} %fusion.7), channel_id=1, source_target_pairs={{0,24},{1,25},{2,26},{3,27},{4,28},{5,29},{6,30},{7,31},{8,16},{9,... | collective-permute-start | bytes 208904 | tf_op jit(solution)/shard_map/ppermute | solution.py:416
  80.1 1.0 collective-permute-start.10
  81.2 4.4 %collective-permute-start.4 = (bf16[45,3,128]{2,1,0:T(4,128)(2,1)S(1)}, bf16[45,3,128]{2,1,0:T(4,128)(2,1)S(1)}, u32[]{:S(2)}, u32[]{:S(2)}) collective-permute-start(bf16[45,3,128]{2,1,0:T(4,128)(2,1)S(1)} %get-tuple-element.61), channel_id=1, source_target_pairs={{0,30},{2,0},{4,2},{6,4},{8,6},{10,8},{12,10},{14,12},{16,14},{18,... | collective-permute-start | bytes 103688 | tf_op jit(solution)/shard_map/ppermute | solution.py:402
  86.1 1.8 %collective-permute-start.15 = (bf16[272,128]{1,0:T(8,128)(2,1)S(1)}, bf16[272,128]{1,0:T(8,128)(2,1)S(1)}, u32[]{:S(2)}, u32[]{:S(2)}) collective-permute-start(bf16[272,128]{1,0:T(8,128)(2,1)S(1)} %add_convert_fusion), channel_id=1, source_target_pairs={{0,5},{1,4},{2,7},{3,6},{4,1},{5,0},{6,3},{7,2},{8,13},{9,12},{10,... | collective-permute-start | bytes 208904 | tf_op jit(solution)/shard_map/ppermute | solution.py:416
  87.8 1.2 %collective-permute-start.14 = (bf16[272,128]{1,0:T(8,128)(2,1)S(1)}, bf16[272,128]{1,0:T(8,128)(2,1)S(1)}, u32[]{:S(2)}, u32[]{:S(2)}) collective-permute-start(bf16[272,128]{1,0:T(8,128)(2,1)S(1)} %add_convert_fusion), channel_id=1, source_target_pairs={{0,4},{1,5},{2,6},{3,7},{4,0},{5,1},{6,2},{7,3},{8,12},{9,13},{10,... | collective-permute-start | bytes 208904 | tf_op jit(solution)/shard_map/ppermute | solution.py:416
  89.7 1.4 %collective-permute-start.5 = (bf16[3,30,128]{2,1,0:T(8,128)(2,1)S(1)}, bf16[3,30,128]{2,1,0:T(8,128)(2,1)S(1)}, u32[]{:S(2)}, u32[]{:S(2)}) collective-permute-start(bf16[3,30,128]{2,1,0:T(8,128)(2,1)S(1)} %fusion.9), channel_id=1, source_target_pairs={{0,1},{1,0},{2,3},{3,2},{4,5},{5,4},{6,7},{7,6},{8,9},{9,8},{10,11... | collective-permute-start | bytes 69128 | tf_op jit(solution)/shard_map/ppermute | solution.py:422
  91.5 1.0 %collective-permute-done.14 = bf16[272,128]{1,0:T(8,128)(2,1)S(1)} collective-permute-done((bf16[272,128]{1,0:T(8,128)(2,1)S(1)}, bf16[272,128]{1,0:T(8,128)(2,1)S(1)}, u32[]{:S(2)}, u32[]{:S(2)}) %collective-permute-start.14) | collective-permute-done | bytes 69664 | tf_op jit(solution)/shard_map/ppermute | solution.py:416
  94.0 3.6 %shard_map.204 = bf16[45,24,128]{2,1,0:T(8,128)(2,1)} custom-call(bf16[51,32,128]{2,1,0:T(8,128)(2,1)S(1)} %pad.6.window, bf16[45,24,128]{2,1,0:T(8,128)(2,1)S(1)} %get-tuple-element.17.masked, bf16[49,128]{1,0:T(8,128)(2,1)S(1)} %squeeze.55.dw_in), custom_call_target="tpu_custom_call" | custom-call | tf_op jit(solution)/shard_map/pallas_call | solution.py:604
  98.6 0.9 fusion.11
  100.9 1.0 copy.33
  (78 shorter events, 8.1 us)
Async XLA Ops:
  0.6 9.0 %copy-start.8 = (bf16[45,24,128]{2,1,0:T(8,128)(2,1)S(1)}, bf16[45,24,128]{2,1,0:T(8,128)(2,1)}, u32[]{:S(2)}) copy-start(bf16[45,24,128]{2,1,0:T(8,128)(2,1)} %param.12) | copy-start | bytes 829444
  0.7 5.9 %copy-start.9 = (bf16[2,7,7,128]{3,0,2,1:T(2,128)(2,1)S(1)}, bf16[2,7,7,128]{3,0,2,1:T(2,128)(2,1)}, u32[]{:S(2)}) copy-start(bf16[2,7,7,128]{3,0,2,1:T(2,128)(2,1)} %param.15) | copy-start | bytes 75268
  3.6 6.1 %collective-permute-start = (bf16[9,48,128]{2,1,0:T(8,128)(2,1)S(1)}, bf16[9,48,128]{2,1,0:T(8,128)(2,1)S(1)}, u32[]{:S(2)}, u32[]{:S(2)}) collective-permute-start(bf16[9,48,128]{2,1,0:T(8,128)(2,1)S(1)} %fusion.8), channel_id=1, source_target_pairs={{0,1},{1,0},{2,3},{3,2},{4,5},{5,4},{6,7},{7,6},{8,9},{9,8},{10,11... | collective-permute-start | bytes 331784 | tf_op jit(solution)/shard_map/ppermute | solution.py:422
  10.0 8.2 %collective-permute-start.1 = (bf16[54,15,128]{2,1,0:T(8,128)(2,1)S(1)}, bf16[54,15,128]{2,1,0:T(8,128)(2,1)S(1)}, u32[]{:S(2)}, u32[]{:S(2)}) collective-permute-start(bf16[54,15,128]{2,1,0:T(8,128)(2,1)S(1)} %pad_maximum_fusion.2), channel_id=1, source_target_pairs={{0,2},{2,4},{4,6},{6,8},{8,10},{10,12},{12,14},{14,16},{16,18},{18... | collective-permute-start | bytes 622088 | tf_op jit(solution)/shard_map/ppermute | solution.py:402
  10.2 8.1 %collective-permute-start.2 = (bf16[54,15,128]{2,1,0:T(8,128)(2,1)S(1)}, bf16[54,15,128]{2,1,0:T(8,128)(2,1)S(1)}, u32[]{:S(2)}, u32[]{:S(2)}) collective-permute-start(bf16[54,15,128]{2,1,0:T(8,128)(2,1)S(1)} %pad_maximum_fusion.3), channel_id=1, source_target_pairs={{0,30},{2,0},{4,2},{6,4},{8,6},{10,8},{12,10},{14,12},{16,14},{18,... | collective-permute-start | bytes 622088 | tf_op jit(solution)/shard_map/ppermute | solution.py:402
  18.4 2.6 %copy-start = (bf16[2,128,512]{2,1,0:T(8,128)(2,1)S(1)}, bf16[2,128,512]{2,1,0:T(8,128)(2,1)}, u32[]{:S(2)}) copy-start(bf16[2,128,512]{2,1,0:T(8,128)(2,1)} %weight_in.1) | copy-start | bytes 786436
  18.4 2.5 %copy-start.1 = (bf16[2,512,128]{2,1,0:T(8,128)(2,1)S(1)}, bf16[2,512,128]{2,1,0:T(8,128)(2,1)}, u32[]{:S(2)}) copy-start(bf16[2,512,128]{2,1,0:T(8,128)(2,1)} %weight_out.1) | copy-start | bytes 786436
  18.4 2.5 %copy-start.2 = (f32[2,512]{1,0:T(2,128)S(1)}, f32[2,512]{1,0:T(2,128)}, u32[]{:S(2)}) copy-start(f32[2,512]{1,0:T(2,128)} %bias_in.1) | copy-start | bytes 12292
  18.4 2.5 %copy-start.3 = (f32[2,128]{1,0:T(2,128)S(1)}, f32[2,128]{1,0:T(2,128)}, u32[]{:S(2)}) copy-start(f32[2,128]{1,0:T(2,128)} %conv_bias.1) | copy-start | bytes 3076
  18.4 2.5 %copy-start.4 = (f32[2,128]{1,0:T(2,128)S(1)}, f32[2,128]{1,0:T(2,128)}, u32[]{:S(2)}) copy-start(f32[2,128]{1,0:T(2,128)} %norm_gain.1) | copy-start | bytes 3076
  66.3 2.8 %collective-permute-start.6 = (bf16[1088,128]{1,0:T(8,128)(2,1)S(1)}, bf16[1088,128]{1,0:T(8,128)(2,1)S(1)}, u32[]{:S(2)}, u32[]{:S(2)}) collective-permute-start(bf16[1088,128]{1,0:T(8,128)(2,1)S(1)} %dynamic-slice_bitcast_fusion), channel_id=1, source_target_pairs={{0,2},{1,3},{2,0},{3,1},{4,6},{5,7},{6,4},{7,5},{8,10},{9,11},{10,... | collective-permute-start | bytes 835592 | tf_op jit(solution)/shard_map/ppermute | solution.py:416
  69.2 5.1 %collective-permute-start.7 = (bf16[272,128]{1,0:T(8,128)(2,1)S(1)}, bf16[272,128]{1,0:T(8,128)(2,1)S(1)}, u32[]{:S(2)}, u32[]{:S(2)}) collective-permute-start(bf16[272,128]{1,0:T(8,128)(2,1)S(1)} %get-tuple-element.57), channel_id=1, source_target_pairs={{0,1},{1,0},{2,3},{3,2},{4,5},{5,4},{6,7},{7,6},{8,9},{9,8},{10,11... | collective-permute-start | bytes 208904 | tf_op jit(solution)/shard_map/ppermute | solution.py:416
  70.8 5.3 %collective-permute-start.9 = (bf16[272,128]{1,0:T(8,128)(2,1)S(1)}, bf16[272,128]{1,0:T(8,128)(2,1)S(1)}, u32[]{:S(2)}, u32[]{:S(2)}) collective-permute-start(bf16[272,128]{1,0:T(8,128)(2,1)S(1)} %get-tuple-element.58), channel_id=1, source_target_pairs={{0,5},{1,4},{2,7},{3,6},{4,1},{5,0},{6,3},{7,2},{8,13},{9,12},{10,... | collective-permute-start | bytes 208904 | tf_op jit(solution)/shard_map/ppermute | solution.py:416
  70.8 5.8 %collective-permute-start.8 = (bf16[272,128]{1,0:T(8,128)(2,1)S(1)}, bf16[272,128]{1,0:T(8,128)(2,1)S(1)}, u32[]{:S(2)}, u32[]{:S(2)}) collective-permute-start(bf16[272,128]{1,0:T(8,128)(2,1)S(1)} %get-tuple-element.59), channel_id=1, source_target_pairs={{0,4},{1,5},{2,6},{3,7},{4,0},{5,1},{6,2},{7,3},{8,12},{9,13},{10,... | collective-permute-start | bytes 208904 | tf_op jit(solution)/shard_map/ppermute | solution.py:416
  76.7 9.0 %collective-permute-start.12 = (bf16[272,128]{1,0:T(8,128)(2,1)S(1)}, bf16[272,128]{1,0:T(8,128)(2,1)S(1)}, u32[]{:S(2)}, u32[]{:S(2)}) collective-permute-start(bf16[272,128]{1,0:T(8,128)(2,1)S(1)} %fusion.7), channel_id=1, source_target_pairs={{0,24},{1,25},{2,26},{3,27},{4,28},{5,29},{6,30},{7,31},{8,16},{9,... | collective-permute-start | bytes 208904 | tf_op jit(solution)/shard_map/ppermute | solution.py:416
  80.1 5.9 %collective-permute-start.11 = (bf16[272,128]{1,0:T(8,128)(2,1)S(1)}, bf16[272,128]{1,0:T(8,128)(2,1)S(1)}, u32[]{:S(2)}, u32[]{:S(2)}) collective-permute-start(bf16[272,128]{1,0:T(8,128)(2,1)S(1)} %fusion.7), channel_id=1, source_target_pairs={{0,16},{1,17},{2,18},{3,19},{4,20},{5,21},{6,22},{7,23},{8,24},{9,... | collective-permute-start | bytes 208904 | tf_op jit(solution)/shard_map/ppermute | solution.py:416
  80.1 5.9 %collective-permute-start.10 = (bf16[272,128]{1,0:T(8,128)(2,1)S(1)}, bf16[272,128]{1,0:T(8,128)(2,1)S(1)}, u32[]{:S(2)}, u32[]{:S(2)}) collective-permute-start(bf16[272,128]{1,0:T(8,128)(2,1)S(1)} %fusion.7), channel_id=1, source_target_pairs={{0,8},{1,9},{2,10},{3,11},{4,12},{5,13},{6,14},{7,15},{8,0},{9,1},... | collective-permute-start | bytes 208904 | tf_op jit(solution)/shard_map/ppermute | solution.py:416
  81.2 8.5 %collective-permute-start.3 = (bf16[45,3,128]{2,1,0:T(4,128)(2,1)S(1)}, bf16[45,3,128]{2,1,0:T(4,128)(2,1)S(1)}, u32[]{:S(2)}, u32[]{:S(2)}) collective-permute-start(bf16[45,3,128]{2,1,0:T(4,128)(2,1)S(1)} %get-tuple-element.60), channel_id=1, source_target_pairs={{0,2},{2,4},{4,6},{6,8},{8,10},{10,12},{12,14},{14,16},{16,18},{18... | collective-permute-start | bytes 103688 | tf_op jit(solution)/shard_map/ppermute | solution.py:402
  81.2 8.4 %collective-permute-start.4 = (bf16[45,3,128]{2,1,0:T(4,128)(2,1)S(1)}, bf16[45,3,128]{2,1,0:T(4,128)(2,1)S(1)}, u32[]{:S(2)}, u32[]{:S(2)}) collective-permute-start(bf16[45,3,128]{2,1,0:T(4,128)(2,1)S(1)} %get-tuple-element.61), channel_id=1, source_target_pairs={{0,30},{2,0},{4,2},{6,4},{8,6},{10,8},{12,10},{14,12},{16,14},{18,... | collective-permute-start | bytes 103688 | tf_op jit(solution)/shard_map/ppermute | solution.py:402
  86.1 5.4 %collective-permute-start.15 = (bf16[272,128]{1,0:T(8,128)(2,1)S(1)}, bf16[272,128]{1,0:T(8,128)(2,1)S(1)}, u32[]{:S(2)}, u32[]{:S(2)}) collective-permute-start(bf16[272,128]{1,0:T(8,128)(2,1)S(1)} %add_convert_fusion), channel_id=1, source_target_pairs={{0,5},{1,4},{2,7},{3,6},{4,1},{5,0},{6,3},{7,2},{8,13},{9,12},{10,... | collective-permute-start | bytes 208904 | tf_op jit(solution)/shard_map/ppermute | solution.py:416
  87.8 4.7 %collective-permute-start.14 = (bf16[272,128]{1,0:T(8,128)(2,1)S(1)}, bf16[272,128]{1,0:T(8,128)(2,1)S(1)}, u32[]{:S(2)}, u32[]{:S(2)}) collective-permute-start(bf16[272,128]{1,0:T(8,128)(2,1)S(1)} %add_convert_fusion), channel_id=1, source_target_pairs={{0,4},{1,5},{2,6},{3,7},{4,0},{5,1},{6,2},{7,3},{8,12},{9,13},{10,... | collective-permute-start | bytes 208904 | tf_op jit(solution)/shard_map/ppermute | solution.py:416
  89.0 4.3 %collective-permute-start.13 = (bf16[272,128]{1,0:T(8,128)(2,1)S(1)}, bf16[272,128]{1,0:T(8,128)(2,1)S(1)}, u32[]{:S(2)}, u32[]{:S(2)}) collective-permute-start(bf16[272,128]{1,0:T(8,128)(2,1)S(1)} %add_convert_fusion), channel_id=1, source_target_pairs={{0,1},{1,0},{2,3},{3,2},{4,5},{5,4},{6,7},{7,6},{8,9},{9,8},{10,11... | collective-permute-start | bytes 208904 | tf_op jit(solution)/shard_map/ppermute | solution.py:416
  89.7 3.9 %collective-permute-start.5 = (bf16[3,30,128]{2,1,0:T(8,128)(2,1)S(1)}, bf16[3,30,128]{2,1,0:T(8,128)(2,1)S(1)}, u32[]{:S(2)}, u32[]{:S(2)}) collective-permute-start(bf16[3,30,128]{2,1,0:T(8,128)(2,1)S(1)} %fusion.9), channel_id=1, source_target_pairs={{0,1},{1,0},{2,3},{3,2},{4,5},{5,4},{6,7},{7,6},{8,9},{9,8},{10,11... | collective-permute-start | bytes 69128 | tf_op jit(solution)/shard_map/ppermute | solution.py:422
  93.4 4.1 %collective-permute-start.16 = (bf16[1088,128]{1,0:T(8,128)(2,1)S(1)}, bf16[1088,128]{1,0:T(8,128)(2,1)S(1)}, u32[]{:S(2)}, u32[]{:S(2)}) collective-permute-start(bf16[1088,128]{1,0:T(8,128)(2,1)S(1)} %get-tuple-element.51), channel_id=1, source_target_pairs={{0,2},{1,3},{2,0},{3,1},{4,6},{5,7},{6,4},{7,5},{8,10},{9,11},{10,... | collective-permute-start | bytes 835592 | tf_op jit(solution)/shard_map/ppermute | solution.py:416
  (3 other events, 7.6 us)

commit v2 on v1

--- a/solution.py
+++ b/solution.py
@@ -19,12 +19,19 @@
 LAND_BOUND = 512.0
 F32 = jnp.float32
 BF16 = jnp.bfloat16
-STEP = 3
+FIRST_STEP = 19
+SECOND_STEP = 8
+BACK_STEP = 9
+TAP_STEP = 5
 STATE_AT = 11
 FIELD_AT = 8
 INNER_AT = 3
 WIDE = 3 * MARGIN
 NARROW = 2 * MARGIN
+
+
+def divisor(size, most):
+    return max(step for step in range(1, most + 1) if size % step == 0)
 
 
 def round_up(size, unit):
@@ -94,22 +101,24 @@
 
 
 def tap_sums(grad_ref, grad_row, grad_col, field_ref, field_row, field_col, height, width, out):
-    for cols in ((0, 1), (2, 3), (4, 5), (6,)):
-
-        def advance(row, sums):
+    rows = divisor(height, TAP_STEP)
+    for cols in ((0, 1, 2, 3), (4, 5, 6)):
+
+        def advance(step, sums):
             sums = list(sums)
-            grad = grad_ref[grad_row + row, pl.ds(grad_col, width), :]
-            for tap_row in range(KSIZE):
-                for place, tap_col in enumerate(cols):
-                    piece = field_ref[
-                        field_row + row + tap_row, pl.ds(field_col + tap_col, width), :
-                    ]
-                    index = place * KSIZE + tap_row
-                    sums[index] = sums[index] + fold(grad * piece)
+            at = step * rows
+            grads = [grad_ref[grad_row + at + row, pl.ds(grad_col, width), :] for row in range(rows)]
+            for place, tap_col in enumerate(cols):
+                for row in range(rows + KSIZE - 1):
+                    piece = field_ref[field_row + at + row, pl.ds(field_col + tap_col, width), :]
+                    for tap_row in range(KSIZE):
+                        if 0 <= row - tap_row < rows:
+                            index = place * KSIZE + tap_row
+                            sums[index] = sums[index] + fold(grads[row - tap_row] * piece)
             return tuple(sums)
 
         zeros = tuple(jnp.zeros((8, grad_ref.shape[2]), F32) for _ in range(KSIZE * len(cols)))
-        sums = lax.fori_loop(0, height, advance, zeros)
+        sums = lax.fori_loop(0, height // rows, advance, zeros)
         for place, tap_col in enumerate(cols):
             for tap_row in range(KSIZE):
                 total = jnp.sum(sums[place * KSIZE + tap_row], axis=0, keepdims=True)
@@ -119,8 +128,11 @@
 def tile_kernel(
     sizes,
     starts,
-    state_in,
-    coded_in,
+    state_tile,
+    coded_tile,
+    lat_pieces,
+    west,
+    east,
     dw_in,
     conv_bias,
     norm_gain,
@@ -170,8 +182,23 @@
         edge = jnp.zeros((pad,) + ref.shape[1:], F32)
         ref[pl.ds(0, pad)] = edge
         ref[pl.ds(pad + window_rows, pad)] = edge
-    state[pl.ds(pad, window_rows)] = state_in[...].astype(F32)
-    coded[pl.ds(pad, window_rows)] = coded_in[...].astype(F32)
+    state[pl.ds(pad, window_rows)] = jnp.zeros((window_rows,) + state.shape[1:], F32)
+    coded[pl.ds(pad, window_rows)] = jnp.zeros((window_rows,) + coded.shape[1:], F32)
+
+    def place(window, at, values):
+        window[at[0], pl.ds(at[1], values.shape[1]), :] = values.astype(F32)
+
+    place(state, (pl.ds(pad + own_start, height), STATE_AT), state_tile[...])
+    place(coded, (pl.ds(pad + own_start, height), FIELD_AT), coded_tile[...])
+    for index in range(lat_pieces.shape[0]):
+        spots = pl.ds(pad + starts[3 + index], WIDE)
+        place(state, (spots, STATE_AT), lat_pieces[index, :, :breadth])
+        place(coded, (spots, FIELD_AT), lat_pieces[index, :, breadth:])
+    spots = pl.ds(pad, window_rows)
+    place(state, (spots, STATE_AT - WIDE), west[:, :WIDE])
+    place(state, (spots, STATE_AT + breadth), east[:, :WIDE])
+    place(coded, (spots, FIELD_AT - NARROW), west[:, WIDE:])
+    place(coded, (spots, FIELD_AT + breadth), east[:, WIDE:])
     kernels[...] = dw_in[...].astype(F32)
     sums[...] = jnp.zeros_like(sums)
     hidden_sums[...] = jnp.zeros_like(hidden_sums)
@@ -179,30 +206,32 @@
     def param(ref, layer):
         return ref[pl.ds(layer, 1), :]
 
+    first_step = divisor(first_rows, FIRST_STEP)
+
     def forward_first(step, carry):
-        row = first_start + step * STEP
-        cells = STEP * first_width
-        mixed = conv_rows(state, row, 0, STEP, first_width, kernels.at[0], False)
+        row = first_start + step * first_step
+        cells = first_step * first_width
+        mixed = conv_rows(state, row, 0, first_step, first_width, kernels.at[0], False)
         normed, inverse = normalise(mixed + param(conv_bias, 0))
         lifted = (normed * param(norm_gain, 0) + param(norm_bias, 0)).astype(BF16)
         hidden = dot(lifted, weight_in[0]) + param(bias_in, 0)
         cumulative, bell = normal_parts(hidden)
         active = hidden * cumulative
         branch = dot(active.astype(BF16), weight_out[0]) + param(bias_out, 0)
-        center = rows_of(state, row + pad, MARGIN, STEP, first_width)
-        mark = rows_of(coded, row + pad, 0, STEP, first_width)
+        center = rows_of(state, row + pad, MARGIN, first_step, first_width)
+        mark = rows_of(coded, row + pad, 0, first_step, first_width)
         value = jnp.where(mark < LAND_BOUND, center + param(layer_scale, 0) * branch, 0.0)
-        value = value.reshape(STEP, first_width, channels)
-
-        for index in range(STEP):
+        value = value.reshape(first_step, first_width, channels)
+
+        for index in range(first_step):
             field[row + pad + index] = value[index]
 
         def own(values):
-            shape = (STEP, first_width, values.shape[1])
+            shape = (first_step, first_width, values.shape[1])
             return values.reshape(shape)[:, FIELD_AT : FIELD_AT + breadth]
 
         slope = own(cumulative) + own(hidden) * (own(bell) * INV_ROOT_TWO_PI)
-        spots = pl.ds(row, STEP)
+        spots = pl.ds(row, first_step)
         slope_own[spots] = slope
         active_own[spots] = own(active).astype(BF16)
         normed_own[spots] = own(normed)
@@ -211,14 +240,16 @@
         lifted_own[spots] = own(normed * param(norm_gain, 0) + param(norm_bias, 0)).astype(BF16)
         return carry
 
-    lax.fori_loop(0, first_rows // STEP, forward_first, 0)
+    lax.fori_loop(0, first_rows // first_step, forward_first, 0)
+
+    second_step = divisor(second_rows, SECOND_STEP)
 
     def both_second(step, carry):
-        row = second_start + step * STEP
-        cells = STEP * second_width
+        row = second_start + step * second_step
+        cells = second_step * second_width
         shift = FIELD_AT - INNER_AT
         mixed = conv_rows(
-            field, row, shift - MARGIN, STEP, second_width, kernels.at[1], False
+            field, row, shift - MARGIN, second_step, second_width, kernels.at[1], False
         )
         normed, inverse = normalise(mixed + param(conv_bias, 1))
         lifted = normed * param(norm_gain, 1) + param(norm_bias, 1)
@@ -226,11 +257,11 @@
         cumulative, bell = normal_parts(hidden)
         active = (hidden * cumulative).astype(BF16)
         branch = dot(active, weight_out[1]) + param(bias_out, 1)
-        center = rows_of(field, row + pad, shift, STEP, second_width)
-        mark = rows_of(coded, row + pad, shift, STEP, second_width)
+        center = rows_of(field, row + pad, shift, second_step, second_width)
+        mark = rows_of(coded, row + pad, shift, second_step, second_width)
         ocean = mark < LAND_BOUND
         value = jnp.where(ocean, center + param(layer_scale, 1) * branch, 0.0)
-        value = value.reshape(STEP, second_width, channels)
+        value = value.reshape(second_step, second_width, channels)
         masked = jnp.where(ocean, mark, 0.0)
         grad_branch = (masked * param(layer_scale, 1)).astype(BF16)
         grad_active = dot_cols(grad_branch, weight_out[1])
@@ -238,12 +269,12 @@
         grad_hidden = (grad_active * slope).astype(BF16)
         grad_lifted = dot_cols(grad_hidden, weight_in[1])
         grad_mixed = normalise_back(grad_lifted * param(norm_gain, 1), normed, inverse)
-        grad_mixed = grad_mixed.reshape(STEP, second_width, channels)
-        for index in range(STEP):
+        grad_mixed = grad_mixed.reshape(second_step, second_width, channels)
+        for index in range(second_step):
             result[row + index] = value[index]
             inner[row + pad + index] = grad_mixed[index]
 
-        shape = (STEP, second_width, channels)
+        shape = (second_step, second_width, channels)
         row_of = lax.broadcasted_iota(jnp.int32, shape, 0) + (row - own_start)
         col_of = lax.broadcasted_iota(jnp.int32, shape, 1) - INNER_AT
         inside = (row_of >= 0) & (row_of < height) & (col_of >= 0) & (col_of < breadth)
@@ -263,46 +294,48 @@
         branch_grad_all[spots] = own_branch.astype(BF16)
         return carry
 
-    lax.fori_loop(0, second_rows // STEP, both_second, 0)
+    lax.fori_loop(0, second_rows // second_step, both_second, 0)
+
+    back_step = divisor(height, BACK_STEP)
 
     def backward_first(step, carry):
-        row = own_start + step * STEP
-        cells = STEP * breadth
-        mark = rows_of(coded, row + pad, FIELD_AT, STEP, breadth)
+        row = own_start + step * back_step
+        cells = back_step * breadth
+        mark = rows_of(coded, row + pad, FIELD_AT, back_step, breadth)
         ocean = mark < LAND_BOUND
         masked_next = jnp.where(ocean, mark, 0.0)
-        spread = conv_rows(inner, row, 0, STEP, breadth, kernels.at[1], True)
+        spread = conv_rows(inner, row, 0, back_step, breadth, kernels.at[1], True)
         masked = jnp.where(ocean, masked_next + spread, 0.0)
         grad_branch = (masked * param(layer_scale, 0)).astype(BF16)
         grad_active = dot_cols(grad_branch, weight_out[0])
-        slope = slope_own[pl.ds(row, STEP)].reshape(cells, grad_active.shape[1])
+        slope = slope_own[pl.ds(row, back_step)].reshape(cells, grad_active.shape[1])
         grad_hidden = (grad_active * slope).astype(BF16)
         grad_lifted = dot_cols(grad_hidden, weight_in[0])
-        normed = normed_own[pl.ds(row, STEP)].reshape(cells, channels)
-        inverse = inverse_own[pl.ds(row, STEP)].reshape(cells, channels)
+        normed = normed_own[pl.ds(row, back_step)].reshape(cells, channels)
+        inverse = inverse_own[pl.ds(row, back_step)].reshape(cells, channels)
         grad_mixed = normalise_back(grad_lifted * param(norm_gain, 0), normed, inverse)
-        branch = branch_own[pl.ds(row, STEP)].reshape(cells, channels)
+        branch = branch_own[pl.ds(row, back_step)].reshape(cells, channels)
         sums[0, 0] += fold(masked * branch)
         sums[0, 1] += fold(grad_branch.astype(F32))
         sums[0, 2] += fold(grad_lifted * normed)
         sums[0, 3] += fold(grad_lifted)
         sums[0, 4] += fold(grad_mixed)
         hidden_sums[0] += fold(grad_hidden.astype(F32))
-        inner_rows = rows_of(inner, row + pad, INNER_AT, STEP, breadth)
+        inner_rows = rows_of(inner, row + pad, INNER_AT, back_step, breadth)
         sums[1, 4] += fold(inner_rows)
-        tile = pl.ds(step * STEP, STEP)
-        shape = (STEP, breadth, channels)
+        tile = pl.ds(step * back_step, back_step)
+        shape = (back_step, breadth, channels)
         grad_mixed = grad_mixed.reshape(shape)
         mixed_own[tile] = grad_mixed
         mixed_out[tile] = grad_mixed.astype(BF16)
         masked_out[tile] = masked.reshape(shape).astype(BF16)
-        hidden_own[tile] = grad_hidden.reshape(STEP, breadth, grad_hidden.shape[1])
+        hidden_own[tile] = grad_hidden.reshape(back_step, breadth, grad_hidden.shape[1])
         branch_grad_own[tile] = grad_branch.reshape(shape)
-        value = rows_of(result, row, INNER_AT, STEP, breadth)
+        value = rows_of(result, row, INNER_AT, back_step, breadth)
         output[tile] = value.reshape(shape).astype(BF16)
         return carry
 
-    lax.fori_loop(0, height // STEP, backward_first, 0)
+    lax.fori_loop(0, height // back_step, backward_first, 0)
 
     hidden_units = weight_in.shape[2]
     groups = hidden_units // channels
@@ -380,15 +413,61 @@
     wide[...] = window[...].astype(F32)
     kernels[...] = dw_in[...].astype(F32)
 
+    rows = divisor(height, BACK_STEP)
+
     def advance(step, carry):
-        row = step * STEP
-        spread = conv_rows(wide, row, 0, STEP, breadth, kernels, True)
-        tile = pl.ds(row, STEP)
-        shape = (STEP, breadth, channels)
+        row = step * rows
+        spread = conv_rows(wide, row, 0, rows, breadth, kernels, True)
+        tile = pl.ds(row, rows)
+        shape = (rows, breadth, channels)
         out[tile] = (masked[tile].astype(F32) + spread.reshape(shape)).astype(BF16)
         return carry
 
-    lax.fori_loop(0, height // STEP, advance, 0)
+    lax.fori_loop(0, height // rows, advance, 0)
+
+
+def code_kernel(lat, state, land_sea, cotangent, coded, edge):
+    height, breadth, channels = state.shape
+    ocean = jnp.where(land_sea[...] != 0, 1.0, 0.0).astype(F32)
+    shape = (height, breadth, breadth)
+    row_of = lax.broadcasted_iota(jnp.int32, shape, 1)
+    col_of = lax.broadcasted_iota(jnp.int32, shape, 2)
+    chosen = jnp.where(row_of == col_of, ocean[:, None, :], 0.0)
+    chosen = chosen.reshape(height * breadth, breadth).astype(BF16)
+    wide = dot(chosen, jnp.ones((breadth, channels), BF16)).reshape(height, breadth, channels)
+    coded[...] = jnp.where(wide > 0.5, cotangent[...].astype(F32), LAND).astype(BF16)
+    for side in range(edge.shape[0]):
+        first = (1 - lat[0]) * (height - WIDE) if edge.shape[0] == 1 else (1 - side) * (height - WIDE)
+        edge[side, :, :breadth] = state[pl.ds(first, WIDE)]
+        edge[side, :, breadth:] = coded[pl.ds(first, WIDE)]
+
+
+def gradient_kernel(grad_norm, held, own, other, *outs_and_scratch):
+    *outs, total = outs_and_scratch
+    kernel, conv_bias, gain, shift, first, first_bias, second, second_bias, scale = outs
+    half = own.shape[0]
+    channels = own.shape[1]
+    total[pl.ds(held[0] * half, half)] = own[...].astype(F32) * grad_norm
+    total[pl.ds((1 - held[0]) * half, half)] = other[...].astype(F32) * grad_norm
+    units = second.shape[1]
+    groups = units // channels
+    for layer in range(BLOCKS):
+        at = layer * 2 * units
+        for group in range(groups):
+            first[layer, :, group * channels : (group + 1) * channels] = total[
+                at + group * channels : at + (group + 1) * channels
+            ]
+        second[layer] = total[at + units : at + 2 * units]
+        at = BLOCKS * 2 * units + layer * (TAPS + 5 + groups)
+        for tap_row in range(KSIZE):
+            kernel[layer, tap_row] = total[at + tap_row * KSIZE : at + (tap_row + 1) * KSIZE]
+        for member, out in enumerate((scale, second_bias, gain, shift, conv_bias)):
+            out[layer : layer + 1] = total[at + TAPS + member : at + TAPS + member + 1]
+        for group in range(groups):
+            row = at + TAPS + 5 + group
+            first_bias[layer : layer + 1, group * channels : (group + 1) * channels] = total[
+                row : row + 1
+            ]
 
 
 class Links:
@@ -480,7 +559,8 @@
         while rest:
             values = exchange(values, rest[:2])
             rest = rest[2:]
-        return gather(gather(values, quad), pair)
+        values = gather(values, quad)
+        return code(pair), values, self.swap(values, *pair[0])
 
 
 def on_device(links, state, land_sea, cotangent, *params):
@@ -499,40 +579,49 @@
         skipped = WIDE - margin
         return lat * skipped if sides == 1 else jnp.int32(skipped)
 
-    starts = jnp.stack([start(0), start(MARGIN), start(NARROW)]).astype(jnp.int32)
-
-    ocean = (land_sea != 0)[:, :, None]
-    coded = jnp.where(ocean, cotangent, jnp.asarray(LAND, BF16))
-    packed = jnp.concatenate([state, coded], axis=1)
-    outside = jnp.concatenate(
-        [
-            jnp.zeros((1, breadth, 1), BF16),
-            jnp.full((1, breadth, 1), LAND, BF16),
-        ],
-        axis=1,
-    )
-    packed = links.extend_lat(packed, WIDE, outside)
-    state_rows = packed[:, :breadth]
-    coded_rows = packed[:, breadth:]
-    east_edge = jnp.concatenate([state_rows[:, -WIDE:], coded_rows[:, -NARROW:]], axis=1)
-    west_edge = jnp.concatenate([state_rows[:, :WIDE], coded_rows[:, :NARROW]], axis=1)
-    west = links.shift_lon(east_edge, 1)
-    east = links.shift_lon(west_edge, -1)
-
-    def window(parts, at, pitch):
-        used = at + sum(part.shape[1] for part in parts)
-        lead = jnp.zeros((window_rows, at, channels), BF16)
-        rest = jnp.zeros((window_rows, pitch - used, channels), BF16)
-        return jnp.concatenate([lead, *parts, rest], axis=1)
-
+    vmem = pl.BlockSpec(memory_space=pltpu.VMEM)
+    smem = pl.BlockSpec(memory_space=pltpu.SMEM)
+    tile = (height, breadth, channels)
+    coded, edges = pl.pallas_call(
+        code_kernel,
+        out_shape=(
+            jax.ShapeDtypeStruct(tile, BF16),
+            jax.ShapeDtypeStruct((sides, WIDE, 2 * breadth, channels), BF16),
+        ),
+        in_specs=[smem, vmem, vmem, vmem],
+        out_specs=(vmem, vmem),
+    )(lat.reshape(1), state, land_sea, cotangent)
+    if sides == 1:
+        pieces = links.swap(edges, 0, 1)
+        places = [(1 - lat) * height]
+    else:
+        outside = jnp.concatenate(
+            [jnp.zeros((1, breadth, 1), BF16), jnp.full((1, breadth, 1), LAND, BF16)], axis=1
+        )
+        above = jnp.where(lat == 0, outside, links.shift_lat(edges[0], 1))
+        below = jnp.where(lat == links.lat - 1, outside, links.shift_lat(edges[1], -1))
+        pieces = jnp.stack([above, below])
+        places = [jnp.int32(0), jnp.int32(WIDE + height)]
+
+    def edge(tile_cols):
+        own = jnp.concatenate([state[:, tile_cols[0]], coded[:, tile_cols[1]]], axis=1)
+        ends = [
+            jnp.concatenate(
+                [piece[:, :breadth][:, tile_cols[0]], piece[:, breadth:][:, tile_cols[1]]], axis=1
+            )
+            for piece in pieces
+        ]
+        if sides == 2:
+            return jnp.concatenate([ends[0], own, ends[1]], axis=0)
+        after = jnp.concatenate([own, ends[0]], axis=0)
+        before = jnp.concatenate([ends[0], own], axis=0)
+        return jnp.where(lat == 0, after, before)
+
+    west = links.shift_lon(edge((slice(-WIDE, None), slice(-NARROW, None))), 1)
+    east = links.shift_lon(edge((slice(WIDE), slice(NARROW))), -1)
+    starts = jnp.stack([start(0), start(MARGIN), start(NARROW), *places]).astype(jnp.int32)
     state_pitch, field_pitch, inner_pitch = (
         round_up(breadth + size, 8) for size in (STATE_AT + WIDE, FIELD_AT + NARROW, NARROW)
-    )
-    state_window = window(
-        [west[:, :WIDE], state_rows, east[:, :WIDE]], STATE_AT - WIDE, state_pitch
-    )
-    coded_window = window(
-        [west[:, WIDE:], coded_rows, east[:, WIDE:]], FIELD_AT - NARROW, field_pitch
     )
 
     padded_rows = window_rows + 2 * MARGIN
@@ -542,8 +631,6 @@
     unit = 16 * 8
     small_rows += round_up(grad_rows, unit) - grad_rows
     grad_rows = round_up(grad_rows, unit)
-    tile = (height, breadth, channels)
-    vmem = pl.BlockSpec(memory_space=pltpu.VMEM)
     own_rows = (window_rows, breadth)
     scratch = [
         pltpu.VMEM((padded_rows, state_pitch, channels), F32),
@@ -579,7 +666,7 @@
             jax.ShapeDtypeStruct(tile, BF16),
             jax.ShapeDtypeStruct((grad_rows, channels), BF16),
         ),
-        in_specs=[pl.BlockSpec(memory_space=pltpu.SMEM)] + [vmem] * 11,
+        in_specs=[smem] + [vmem] * 14,
         out_specs=(vmem,) * 4,
         scratch_shapes=scratch,
         compiler_params=pltpu.CompilerParams(vmem_limit_bytes=48 * 1024 * 1024),
@@ -588,7 +675,7 @@
             bytes_accessed=4 * height * breadth * channels * 4,
             transcendentals=0,
         ),
-    )(starts, state_window, coded_window, taps_in, *params[1:])
+    )(starts, state, coded, pieces, west, east, taps_in, *params[1:])
 
     before = links.shift_lon(grad_mixed[:, -MARGIN:], 1)
     after = links.shift_lon(grad_mixed[:, :MARGIN], -1)
@@ -608,30 +695,21 @@
         out_specs=vmem,
         scratch_shapes=[pltpu.VMEM(spread.shape, F32), pltpu.VMEM((TAPS, channels), F32)],
         compiler_params=pltpu.CompilerParams(vmem_limit_bytes=16 * 1024 * 1024),
+        cost_estimate=pl.CostEstimate(
+            flops=4_000_000_000, bytes_accessed=8_000_000, transcendentals=0
+        ),
     )(spread, masked, taps_in[0])
 
-    total = links.sum_all(grads).astype(F32) * grad_norm
-    size = 2 * hidden_units
-    at = BLOCKS * size
-    weights = total[:at].reshape(BLOCKS, 2, groups, channels, channels)
-    grad_in = weights[:, 0].transpose(0, 2, 1, 3).reshape(BLOCKS, channels, hidden_units)
-    grad_out = weights[:, 1].reshape(BLOCKS, hidden_units, channels)
-    small = total[at : at + BLOCKS * (TAPS + 5 + groups)].reshape(BLOCKS, -1, channels)
-    grad_kernel = small[:, :TAPS].reshape(BLOCKS, KSIZE, KSIZE, channels)
-    grad_bias_in = small[:, TAPS + 5 :].reshape(BLOCKS, hidden_units)
-    return (
-        output,
-        grad_state,
-        grad_kernel,
-        small[:, TAPS + 4],
-        small[:, TAPS + 2],
-        small[:, TAPS + 3],
-        grad_in,
-        grad_bias_in,
-        grad_out,
-        small[:, TAPS + 1],
-        small[:, TAPS],
-    )
+    held, own, other = links.sum_all(grads)
+    shapes = [(BLOCKS, KSIZE, KSIZE, channels)] + [member.shape for member in params[1:]]
+    gradients = pl.pallas_call(
+        functools.partial(gradient_kernel, grad_norm),
+        out_shape=tuple(jax.ShapeDtypeStruct(shape, F32) for shape in shapes),
+        in_specs=[smem, vmem, vmem],
+        out_specs=(vmem,) * 9,
+        scratch_shapes=[pltpu.VMEM((grad_rows, channels), F32)],
+    )(held.reshape(1), own, other)
+    return (output, grad_state, *gradients)
 
 
 def solution(mesh):

time: 102 us -> 83 us (0.81)
  Pallas kernels: 48.8 us -> 36.2 us
  other arithmetic: 4.02 us -> 0.82 us
  local copies, waits for them, and re-layouts: 7.16 us -> 4.04 us
  starting transfers between devices: 26.7 us -> 24.9 us
  waiting for transfers between devices: 14.1 us -> 15.7 us
    pallas_call x1, Pallas kernels: 45.2 us -> 28.9 us  [on_device(): pl.pallas_call(functools.partial(tile_kernel, sizes), out_shape=(jax.Shap...]
    pallas_call x0 -> x2, Pallas kernels: none -> 4.25 us  [the longest x1 2.19 us: on_device(): pl.pallas_call(functools.partial(gradient_kernel, grad_norm), out_shape=t...]
    ppermute x2 -> x1, starting transfers between devices: 4.45 us -> 1.25 us  [extend_lat(): other = lax.ppermute(mine, 'lat', [(0, 1), (1, 0)])]
    ppermute x11 -> x12, starting transfers between devices: 13.2 us -> 16.2 us  [swap(): return lax.ppermute(values, self.axes, pairs)]
    ppermute x2 -> x1, waiting for transfers between devices: 2.96 us -> 0.01 us  [extend_lat(): other = lax.ppermute(mine, 'lat', [(0, 1), (1, 0)])]
    ppermute x4, waiting for transfers between devices: 3.52 us -> 6.1 us  [shift_lon(): return lax.ppermute(values, 'lon', pairs)]
    concatenate x2 -> x0, local copies, waits for them, and re-layouts: 2.42 us -> none  [window(): return jnp.concatenate([lead, *parts, rest], axis=1)]
    slice x11 -> x4, local copies, waits for them, and re-layouts: 2.46 us -> 0.14 us  [the longest x1 0.07 us: edge(): state[:, tile_cols[0]]]
  transfers between devices with their start and end apart: 17 -> 17, of which waited for: 10 -> 9; matrix products, arithmetic and copies ran while one was open for 1% -> 1% of each run, Pallas kernels for 4% -> 4%
where the time goes in v2:
time: 83 us; the launch traced here: 82.7 us
  Pallas kernels  36.2 us (44%)
  starting transfers between devices  24.9 us (30%)
  waiting for transfers between devices  15.7 us (19%)
  local copies, waits for them, and re-layouts  4.04 us (5%)
  between operations  1.04 us (1%)
    pallas_call x1, Pallas kernels, on_device(): pl.pallas_call(functools.partial(tile_kernel, sizes), out_shape=(jax.Shap...  28.9 us
    ppermute x12, starting transfers between devices, swap(): return lax.ppermute(values, self.axes, pairs)  16.2 us
    ppermute x12, waiting for transfers between devices, swap(): return lax.ppermute(values, self.axes, pairs)  9.61 us
    ppermute x4, starting transfers between devices, shift_lon(): return lax.ppermute(values, 'lon', pairs)  7.47 us
    ppermute x4, waiting for transfers between devices, shift_lon(): return lax.ppermute(values, 'lon', pairs)  6.1 us
    unnamed x28, local copies, waits for them, and re-layouts  3.62 us
    pallas_call x1, Pallas kernels, on_device(): pl.pallas_call(state_kernel, out_shape=jax.ShapeDtypeStruct(tile, BF16),...  2.98 us
    pallas_call x1, Pallas kernels, on_device(): pl.pallas_call(functools.partial(gradient_kernel, grad_norm), out_shape=t...  2.19 us
  transfers between devices with their start and end apart: 17, of which 9 were waited for; matrix products, arithmetic and copies ran while one was open for 1% of the time, Pallas kernels for 4%

profile of v2, /device:TPU:0, one launch (start us, length us, event | category | flops | bytes accessed | tf_op | source)
XLA Modules:
  0.0 82.7 jit_solution(9925538846968670669)
XLA Ops:
  0.6 1.4 %copy.26.land_sea = s32[45,24]{1,0:T(8,128)} copy(s32[45,24]{0,1:T(8,128)} %param.13) | data formatting | bytes 8640 | tf_op args[1]
  2.0 2.1 %shard_map.203 = (bf16[45,24,128]{2,1,0:T(8,128)(2,1)}, bf16[1,9,48,128]{3,2,1,0:T(8,128)(2,1)}) custom-call(s32[1]{0:T(128)} %bitcast.4.lat, bf16[45,24,128]{2,1,0:T(8,128)(2,1)} %state_tile.1, s32[45,24]{1,0:T(8,128)} %copy.26.land_sea, bf16[45,24,128]{2,1,0:T(8,128)(2,1)} %cotangent.1), custom_call_target="tpu_custom_call" | custom-call | tf_op jit(solution)/shard_map/pallas_call | solution.py:585
  4.1 2.9 %collective-permute-start = (bf16[1,9,48,128]{3,2,1,0:T(8,128)(2,1)}, bf16[1,9,48,128]{3,2,1,0:T(8,128)(2,1)S(1)}, u32[]{:S(2)}, u32[]{:S(2)}) collective-permute-start(bf16[1,9,48,128]{3,2,1,0:T(8,128)(2,1)} %get-tuple-element.27), channel_id=1, source_target_pairs={{0,1},{1,0},{2,3},{3,2},{4,5},{5,4},{6,7},{7,6},{8,9},{9,8},{10,11... | collective-permute-start | bytes 331784 | tf_op jit(solution)/shard_map/ppermute | solution.py:495
  7.2 3.1 %collective-permute-done.lat_pieces = bf16[1,9,48,128]{3,2,1,0:T(8,128)(2,1)S(1)} collective-permute-done((bf16[1,9,48,128]{3,2,1,0:T(8,128)(2,1)}, bf16[1,9,48,128]{3,2,1,0:T(8,128)(2,1)S(1)}, u32[]{:S(2)}, u32[]{:S(2)}) %collective-permute-start) | collective-permute-done | bytes 110624 | tf_op jit(solution)/shard_map/ppermute | solution.py:495
  10.7 4.5 %collective-permute-start.2 = (bf16[54,15,128]{2,1,0:T(8,128)(2,1)S(1)}, bf16[54,15,128]{2,1,0:T(8,128)(2,1)S(1)}, u32[]{:S(2)}, u32[]{:S(2)}) collective-permute-start(bf16[54,15,128]{2,1,0:T(8,128)(2,1)S(1)} %maximum_select_fusion.2), channel_id=1, source_target_pairs={{0,30},{2,0},{4,2},{6,4},{8,6},{10,8},{12,10},{14,12},{16,14},{18,... | collective-permute-start | bytes 622088 | tf_op jit(solution)/shard_map/ppermute | solution.py:481
  15.3 3.4 %collective-permute-done.1.west = bf16[54,15,128]{2,1,0:T(8,128)(2,1)S(1)} collective-permute-done((bf16[54,15,128]{2,1,0:T(8,128)(2,1)S(1)}, bf16[54,15,128]{2,1,0:T(8,128)(2,1)S(1)}, u32[]{:S(2)}, u32[]{:S(2)}) %collective-permute-start.1) | collective-permute-done | bytes 207392 | tf_op jit(solution)/shard_map/ppermute | solution.py:481
  18.7 28.9 %shard_map.204 = (bf16[45,24,128]{2,1,0:T(8,128)(2,1)}, bf16[45,24,128]{2,1,0:T(8,128)(2,1)S(1)}, bf16[45,24,128]{2,1,0:T(8,128)(2,1)S(1)}, bf16[2176,128]{1,0:T(8,128)(2,1)S(1)}) custom-call(s32[4]{0:T(128)S(1)} %pad_add_fusion.starts, bf16[45,24,128]{2,1,0:T(8,128)(2,1)S(1)} %copy-done, bf16[45,24,128]{2,1,0:T(8,128)(2,1)S(1)} %copy-done.1, ...), custom_call_target="tpu_custom_call" | custom-call | flops 2013265920 | bytes 2211840 | tf_op jit(solution)/shard_map/pallas_call | solution.py:661
  47.7 1.7 %collective-permute-start.6 = (bf16[1088,128]{1,0:T(8,128)(2,1)S(1)}, bf16[1088,128]{1,0:T(8,128)(2,1)S(1)}, u32[]{:S(2)}, u32[]{:S(2)}) collective-permute-start(bf16[1088,128]{1,0:T(8,128)(2,1)S(1)} %dynamic-slice_bitcast_fusion), channel_id=1, source_target_pairs={{0,2},{1,3},{2,0},{3,1},{4,6},{5,7},{6,4},{7,5},{8,10},{9,11},{10,... | collective-permute-start | bytes 835592 | tf_op jit(solution)/shard_map/ppermute | solution.py:495
  49.6 3.0 %collective-permute-start.4 = (bf16[45,3,128]{2,1,0:T(4,128)(2,1)S(1)}, bf16[45,3,128]{2,1,0:T(4,128)(2,1)S(1)}, u32[]{:S(2)}, u32[]{:S(2)}) collective-permute-start(bf16[45,3,128]{2,1,0:T(4,128)(2,1)S(1)} %get-tuple-element.71), channel_id=1, source_target_pairs={{0,30},{2,0},{4,2},{6,4},{8,6},{10,8},{12,10},{14,12},{16,14},{18,... | collective-permute-start | bytes 103688 | tf_op jit(solution)/shard_map/ppermute | solution.py:481
  52.8 2.8 %collective-permute-start.8 = (bf16[272,128]{1,0:T(8,128)(2,1)S(1)}, bf16[272,128]{1,0:T(8,128)(2,1)S(1)}, u32[]{:S(2)}, u32[]{:S(2)}) collective-permute-start(bf16[272,128]{1,0:T(8,128)(2,1)S(1)} %get-tuple-element.69), channel_id=1, source_target_pairs={{0,4},{1,5},{2,6},{3,7},{4,0},{5,1},{6,2},{7,3},{8,12},{9,13},{10,... | collective-permute-start | bytes 208904 | tf_op jit(solution)/shard_map/ppermute | solution.py:495
  56.2 2.7 %collective-permute-done.3 = bf16[45,3,128]{2,1,0:T(4,128)(2,1)S(1)} collective-permute-done((bf16[45,3,128]{2,1,0:T(4,128)(2,1)S(1)}, bf16[45,3,128]{2,1,0:T(4,128)(2,1)S(1)}, u32[]{:S(2)}, u32[]{:S(2)}) %collective-permute-start.3) | collective-permute-done | bytes 34592 | tf_op jit(solution)/shard_map/ppermute | solution.py:481
  59.0 1.3 %collective-permute-start.5 = (bf16[3,30,128]{2,1,0:T(8,128)(2,1)S(1)}, bf16[3,30,128]{2,1,0:T(8,128)(2,1)S(1)}, u32[]{:S(2)}, u32[]{:S(2)}) collective-permute-start(bf16[3,30,128]{2,1,0:T(8,128)(2,1)S(1)} %fusion.4), channel_id=1, source_target_pairs={{0,1},{1,0},{2,3},{3,2},{4,5},{5,4},{6,7},{7,6},{8,9},{9,8},{10,11... | collective-permute-start | bytes 69128 | tf_op jit(solution)/shard_map/ppermute | solution.py:501
  60.5 4.3 %collective-permute-start.10 = (bf16[272,128]{1,0:T(8,128)(2,1)S(1)}, bf16[272,128]{1,0:T(8,128)(2,1)S(1)}, u32[]{:S(2)}, u32[]{:S(2)}) collective-permute-start(bf16[272,128]{1,0:T(8,128)(2,1)S(1)} %fusion.3), channel_id=1, source_target_pairs={{0,8},{1,9},{2,10},{3,11},{4,12},{5,13},{6,14},{7,15},{8,0},{9,1},... | collective-permute-start | bytes 208904 | tf_op jit(solution)/shard_map/ppermute | solution.py:495
  65.0 1.7 %collective-permute-done.12 = bf16[272,128]{1,0:T(8,128)(2,1)S(1)} collective-permute-done((bf16[272,128]{1,0:T(8,128)(2,1)S(1)}, bf16[272,128]{1,0:T(8,128)(2,1)S(1)}, u32[]{:S(2)}, u32[]{:S(2)}) %collective-permute-start.12) | collective-permute-done | bytes 69664 | tf_op jit(solution)/shard_map/ppermute | solution.py:495
  67.2 0.8 %collective-permute-done.10 = bf16[272,128]{1,0:T(8,128)(2,1)S(1)} collective-permute-done((bf16[272,128]{1,0:T(8,128)(2,1)S(1)}, bf16[272,128]{1,0:T(8,128)(2,1)S(1)}, u32[]{:S(2)}, u32[]{:S(2)}) %collective-permute-start.10) | collective-permute-done | bytes 69664 | tf_op jit(solution)/shard_map/ppermute | solution.py:495
  68.1 1.8 %collective-permute-start.15 = (bf16[272,128]{1,0:T(8,128)(2,1)S(1)}, bf16[272,128]{1,0:T(8,128)(2,1)S(1)}, u32[]{:S(2)}, u32[]{:S(2)}) collective-permute-start(bf16[272,128]{1,0:T(8,128)(2,1)S(1)} %add_convert_fusion), channel_id=1, source_target_pairs={{0,5},{1,4},{2,7},{3,6},{4,1},{5,0},{6,3},{7,2},{8,13},{9,12},{10,... | collective-permute-start | bytes 208904 | tf_op jit(solution)/shard_map/ppermute | solution.py:495
  69.8 1.1 %collective-permute-start.14 = (bf16[272,128]{1,0:T(8,128)(2,1)S(1)}, bf16[272,128]{1,0:T(8,128)(2,1)S(1)}, u32[]{:S(2)}, u32[]{:S(2)}) collective-permute-start(bf16[272,128]{1,0:T(8,128)(2,1)S(1)} %add_convert_fusion), channel_id=1, source_target_pairs={{0,4},{1,5},{2,6},{3,7},{4,0},{5,1},{6,2},{7,3},{8,12},{9,13},{10,... | collective-permute-start | bytes 208904 | tf_op jit(solution)/shard_map/ppermute | solution.py:495
  70.9 0.7 collective-permute-start.13
  71.8 1.7 %collective-permute-done.15 = bf16[272,128]{1,0:T(8,128)(2,1)S(1)} collective-permute-done((bf16[272,128]{1,0:T(8,128)(2,1)S(1)}, bf16[272,128]{1,0:T(8,128)(2,1)S(1)}, u32[]{:S(2)}, u32[]{:S(2)}) %collective-permute-start.15) | collective-permute-done | bytes 69664 | tf_op jit(solution)/shard_map/ppermute | solution.py:495
  73.4 0.9 %collective-permute-done.14 = bf16[272,128]{1,0:T(8,128)(2,1)S(1)} collective-permute-done((bf16[272,128]{1,0:T(8,128)(2,1)S(1)}, bf16[272,128]{1,0:T(8,128)(2,1)S(1)}, u32[]{:S(2)}, u32[]{:S(2)}) %collective-permute-start.14) | collective-permute-done | bytes 69664 | tf_op jit(solution)/shard_map/ppermute | solution.py:495
  74.3 0.8 %collective-permute-done.13 = bf16[272,128]{1,0:T(8,128)(2,1)S(1)} collective-permute-done((bf16[272,128]{1,0:T(8,128)(2,1)S(1)}, bf16[272,128]{1,0:T(8,128)(2,1)S(1)}, u32[]{:S(2)}, u32[]{:S(2)}) %collective-permute-start.13) | collective-permute-done | bytes 69664 | tf_op jit(solution)/shard_map/ppermute | solution.py:495
  75.4 3.0 %shard_map.205 = bf16[45,24,128]{2,1,0:T(8,128)(2,1)} custom-call(bf16[51,32,128]{2,1,0:T(8,128)(2,1)S(1)} %pad.6.window, bf16[45,24,128]{2,1,0:T(8,128)(2,1)S(1)} %get-tuple-element.30.masked, bf16[49,128]{1,0:T(8,128)(2,1)S(1)} %squeeze.31.dw_in), custom_call_target="tpu_custom_call" | custom-call | flops 4000000000 | bytes 8000000 | tf_op jit(solution)/shard_map/pallas_call | solution.py:691
  79.1 2.2 %shard_map.206 = (f32[2,7,7,128]{3,2,1,0:T(8,128)}, f32[2,128]{1,0:T(2,128)}, f32[2,128]{1,0:T(2,128)}, f32[2,128]{1,0:T(2,128)}, f32[2,128,512]{2,1,0:T(8,128)}...) custom-call(s32[1]{0:T(128)} %bitcast.7.held, ...), custom_call_target="tpu_custom_call" | custom-call | tf_op jit(solution)/shard_map/pallas_call | solution.py:705
  81.3 1.5 %copy.28 = f32[2,7,7,128]{3,0,2,1:T(2,128)} copy(f32[2,7,7,128]{3,2,1,0:T(8,128)} %get-tuple-element.54) | data formatting | bytes 100352
  (65 shorter events, 3.5 us)
Async XLA Ops:
  2.0 5.0 %copy-start = (bf16[45,24,128]{2,1,0:T(8,128)(2,1)S(1)}, bf16[45,24,128]{2,1,0:T(8,128)(2,1)}, u32[]{:S(2)}) copy-start(bf16[45,24,128]{2,1,0:T(8,128)(2,1)} %state_tile.1) | copy-start | bytes 829444
  4.1 6.2 %collective-permute-start = (bf16[1,9,48,128]{3,2,1,0:T(8,128)(2,1)}, bf16[1,9,48,128]{3,2,1,0:T(8,128)(2,1)S(1)}, u32[]{:S(2)}, u32[]{:S(2)}) collective-permute-start(bf16[1,9,48,128]{3,2,1,0:T(8,128)(2,1)} %get-tuple-element.27), channel_id=1, source_target_pairs={{0,1},{1,0},{2,3},{3,2},{4,5},{5,4},{6,7},{7,6},{8,9},{9,8},{10,11... | collective-permute-start | bytes 331784 | tf_op jit(solution)/shard_map/ppermute | solution.py:495
  10.5 8.2 %collective-permute-start.1 = (bf16[54,15,128]{2,1,0:T(8,128)(2,1)S(1)}, bf16[54,15,128]{2,1,0:T(8,128)(2,1)S(1)}, u32[]{:S(2)}, u32[]{:S(2)}) collective-permute-start(bf16[54,15,128]{2,1,0:T(8,128)(2,1)S(1)} %maximum_select_fusion.1), channel_id=1, source_target_pairs={{0,2},{2,4},{4,6},{6,8},{8,10},{10,12},{12,14},{14,16},{16,18},{18... | collective-permute-start | bytes 622088 | tf_op jit(solution)/shard_map/ppermute | solution.py:481
  10.5 8.2 %copy-start.2 = (bf16[2,128,512]{2,1,0:T(8,128)(2,1)S(1)}, bf16[2,128,512]{2,1,0:T(8,128)(2,1)}, u32[]{:S(2)}) copy-start(bf16[2,128,512]{2,1,0:T(8,128)(2,1)} %weight_in.1) | copy-start | bytes 786436
  10.5 8.1 %copy-start.3 = (bf16[2,512,128]{2,1,0:T(8,128)(2,1)S(1)}, bf16[2,512,128]{2,1,0:T(8,128)(2,1)}, u32[]{:S(2)}) copy-start(bf16[2,512,128]{2,1,0:T(8,128)(2,1)} %weight_out.1) | copy-start | bytes 786436
  10.7 4.5 %copy-start.12 = (bf16[2,7,7,128]{3,0,2,1:T(2,128)(2,1)S(1)}, bf16[2,7,7,128]{3,0,2,1:T(2,128)(2,1)}, u32[]{:S(2)}) copy-start(bf16[2,7,7,128]{3,0,2,1:T(2,128)(2,1)} %param.15) | copy-start | bytes 75268
  10.7 8.0 %collective-permute-start.2 = (bf16[54,15,128]{2,1,0:T(8,128)(2,1)S(1)}, bf16[54,15,128]{2,1,0:T(8,128)(2,1)S(1)}, u32[]{:S(2)}, u32[]{:S(2)}) collective-permute-start(bf16[54,15,128]{2,1,0:T(8,128)(2,1)S(1)} %maximum_select_fusion.2), channel_id=1, source_target_pairs={{0,30},{2,0},{4,2},{6,4},{8,6},{10,8},{12,10},{14,12},{16,14},{18,... | collective-permute-start | bytes 622088 | tf_op jit(solution)/shard_map/ppermute | solution.py:481
  15.1 3.6 %copy-start.7 = (f32[2,128]{1,0:T(2,128)S(1)}, f32[2,128]{1,0:T(2,128)}, u32[]{:S(2)}) copy-start(f32[2,128]{1,0:T(2,128)} %norm_bias.1) | copy-start | bytes 3076
  15.1 3.6 %copy-start.8 = (f32[2,128]{1,0:T(2,128)S(1)}, f32[2,128]{1,0:T(2,128)}, u32[]{:S(2)}) copy-start(f32[2,128]{1,0:T(2,128)} %bias_out.1) | copy-start | bytes 3076
  15.1 3.6 %copy-start.9 = (f32[2,128]{1,0:T(2,128)S(1)}, f32[2,128]{1,0:T(2,128)}, u32[]{:S(2)}) copy-start(f32[2,128]{1,0:T(2,128)} %layer_scale.1) | copy-start | bytes 3076
  47.7 4.9 %collective-permute-start.6 = (bf16[1088,128]{1,0:T(8,128)(2,1)S(1)}, bf16[1088,128]{1,0:T(8,128)(2,1)S(1)}, u32[]{:S(2)}, u32[]{:S(2)}) collective-permute-start(bf16[1088,128]{1,0:T(8,128)(2,1)S(1)} %dynamic-slice_bitcast_fusion), channel_id=1, source_target_pairs={{0,2},{1,3},{2,0},{3,1},{4,6},{5,7},{6,4},{7,5},{8,10},{9,11},{10,... | collective-permute-start | bytes 835592 | tf_op jit(solution)/shard_map/ppermute | solution.py:495
  49.6 6.6 %collective-permute-start.4 = (bf16[45,3,128]{2,1,0:T(4,128)(2,1)S(1)}, bf16[45,3,128]{2,1,0:T(4,128)(2,1)S(1)}, u32[]{:S(2)}, u32[]{:S(2)}) collective-permute-start(bf16[45,3,128]{2,1,0:T(4,128)(2,1)S(1)} %get-tuple-element.71), channel_id=1, source_target_pairs={{0,30},{2,0},{4,2},{6,4},{8,6},{10,8},{12,10},{14,12},{16,14},{18,... | collective-permute-start | bytes 103688 | tf_op jit(solution)/shard_map/ppermute | solution.py:481
  52.6 6.4 %collective-permute-start.3 = (bf16[45,3,128]{2,1,0:T(4,128)(2,1)S(1)}, bf16[45,3,128]{2,1,0:T(4,128)(2,1)S(1)}, u32[]{:S(2)}, u32[]{:S(2)}) collective-permute-start(bf16[45,3,128]{2,1,0:T(4,128)(2,1)S(1)} %get-tuple-element.70), channel_id=1, source_target_pairs={{0,2},{2,4},{4,6},{6,8},{8,10},{10,12},{12,14},{14,16},{16,18},{18... | collective-permute-start | bytes 103688 | tf_op jit(solution)/shard_map/ppermute | solution.py:481
  52.7 7.5 %collective-permute-start.9 = (bf16[272,128]{1,0:T(8,128)(2,1)S(1)}, bf16[272,128]{1,0:T(8,128)(2,1)S(1)}, u32[]{:S(2)}, u32[]{:S(2)}) collective-permute-start(bf16[272,128]{1,0:T(8,128)(2,1)S(1)} %get-tuple-element.68), channel_id=1, source_target_pairs={{0,5},{1,4},{2,7},{3,6},{4,1},{5,0},{6,3},{7,2},{8,13},{9,12},{10,... | collective-permute-start | bytes 208904 | tf_op jit(solution)/shard_map/ppermute | solution.py:495
  52.8 7.5 %collective-permute-start.8 = (bf16[272,128]{1,0:T(8,128)(2,1)S(1)}, bf16[272,128]{1,0:T(8,128)(2,1)S(1)}, u32[]{:S(2)}, u32[]{:S(2)}) collective-permute-start(bf16[272,128]{1,0:T(8,128)(2,1)S(1)} %get-tuple-element.69), channel_id=1, source_target_pairs={{0,4},{1,5},{2,6},{3,7},{4,0},{5,1},{6,2},{7,3},{8,12},{9,13},{10,... | collective-permute-start | bytes 208904 | tf_op jit(solution)/shard_map/ppermute | solution.py:495
  55.6 4.6 %collective-permute-start.7 = (bf16[272,128]{1,0:T(8,128)(2,1)S(1)}, bf16[272,128]{1,0:T(8,128)(2,1)S(1)}, u32[]{:S(2)}, u32[]{:S(2)}) collective-permute-start(bf16[272,128]{1,0:T(8,128)(2,1)S(1)} %get-tuple-element.67), channel_id=1, source_target_pairs={{0,1},{1,0},{2,3},{3,2},{4,5},{5,4},{6,7},{7,6},{8,9},{9,8},{10,11... | collective-permute-start | bytes 208904 | tf_op jit(solution)/shard_map/ppermute | solution.py:495
  59.0 5.8 %collective-permute-start.5 = (bf16[3,30,128]{2,1,0:T(8,128)(2,1)S(1)}, bf16[3,30,128]{2,1,0:T(8,128)(2,1)S(1)}, u32[]{:S(2)}, u32[]{:S(2)}) collective-permute-start(bf16[3,30,128]{2,1,0:T(8,128)(2,1)S(1)} %fusion.4), channel_id=1, source_target_pairs={{0,1},{1,0},{2,3},{3,2},{4,5},{5,4},{6,7},{7,6},{8,9},{9,8},{10,11... | collective-permute-start | bytes 69128 | tf_op jit(solution)/shard_map/ppermute | solution.py:501
  60.3 6.4 %collective-permute-start.12 = (bf16[272,128]{1,0:T(8,128)(2,1)S(1)}, bf16[272,128]{1,0:T(8,128)(2,1)S(1)}, u32[]{:S(2)}, u32[]{:S(2)}) collective-permute-start(bf16[272,128]{1,0:T(8,128)(2,1)S(1)} %fusion.3), channel_id=1, source_target_pairs={{0,24},{1,25},{2,26},{3,27},{4,28},{5,29},{6,30},{7,31},{8,16},{9,... | collective-permute-start | bytes 208904 | tf_op jit(solution)/shard_map/ppermute | solution.py:495
  60.4 6.8 %collective-permute-start.11 = (bf16[272,128]{1,0:T(8,128)(2,1)S(1)}, bf16[272,128]{1,0:T(8,128)(2,1)S(1)}, u32[]{:S(2)}, u32[]{:S(2)}) collective-permute-start(bf16[272,128]{1,0:T(8,128)(2,1)S(1)} %fusion.3), channel_id=1, source_target_pairs={{0,16},{1,17},{2,18},{3,19},{4,20},{5,21},{6,22},{7,23},{8,24},{9,... | collective-permute-start | bytes 208904 | tf_op jit(solution)/shard_map/ppermute | solution.py:495
  60.5 7.6 %collective-permute-start.10 = (bf16[272,128]{1,0:T(8,128)(2,1)S(1)}, bf16[272,128]{1,0:T(8,128)(2,1)S(1)}, u32[]{:S(2)}, u32[]{:S(2)}) collective-permute-start(bf16[272,128]{1,0:T(8,128)(2,1)S(1)} %fusion.3), channel_id=1, source_target_pairs={{0,8},{1,9},{2,10},{3,11},{4,12},{5,13},{6,14},{7,15},{8,0},{9,1},... | collective-permute-start | bytes 208904 | tf_op jit(solution)/shard_map/ppermute | solution.py:495
  68.1 5.4 %collective-permute-start.15 = (bf16[272,128]{1,0:T(8,128)(2,1)S(1)}, bf16[272,128]{1,0:T(8,128)(2,1)S(1)}, u32[]{:S(2)}, u32[]{:S(2)}) collective-permute-start(bf16[272,128]{1,0:T(8,128)(2,1)S(1)} %add_convert_fusion), channel_id=1, source_target_pairs={{0,5},{1,4},{2,7},{3,6},{4,1},{5,0},{6,3},{7,2},{8,13},{9,12},{10,... | collective-permute-start | bytes 208904 | tf_op jit(solution)/shard_map/ppermute | solution.py:495
  69.8 4.5 %collective-permute-start.14 = (bf16[272,128]{1,0:T(8,128)(2,1)S(1)}, bf16[272,128]{1,0:T(8,128)(2,1)S(1)}, u32[]{:S(2)}, u32[]{:S(2)}) collective-permute-start(bf16[272,128]{1,0:T(8,128)(2,1)S(1)} %add_convert_fusion), channel_id=1, source_target_pairs={{0,4},{1,5},{2,6},{3,7},{4,0},{5,1},{6,2},{7,3},{8,12},{9,13},{10,... | collective-permute-start | bytes 208904 | tf_op jit(solution)/shard_map/ppermute | solution.py:495
  70.9 4.3 %collective-permute-start.13 = (bf16[272,128]{1,0:T(8,128)(2,1)S(1)}, bf16[272,128]{1,0:T(8,128)(2,1)S(1)}, u32[]{:S(2)}, u32[]{:S(2)}) collective-permute-start(bf16[272,128]{1,0:T(8,128)(2,1)S(1)} %add_convert_fusion), channel_id=1, source_target_pairs={{0,1},{1,0},{2,3},{3,2},{4,5},{5,4},{6,7},{7,6},{8,9},{9,8},{10,11... | collective-permute-start | bytes 208904 | tf_op jit(solution)/shard_map/ppermute | solution.py:495
  75.3 3.1 %collective-permute-start.16 = (bf16[1088,128]{1,0:T(8,128)(2,1)S(1)}, bf16[1088,128]{1,0:T(8,128)(2,1)S(1)}, u32[]{:S(2)}, u32[]{:S(2)}) collective-permute-start(bf16[1088,128]{1,0:T(8,128)(2,1)S(1)} %pad_maximum_fusion.1.own), channel_id=1, source_target_pairs={{0,2},{1,3},{2,0},{3,1},{4,6},{5,7},{6,4},{7,5},{8,10},{9,11},{10,... | collective-permute-start | bytes 835592 | tf_op jit(solution)/shard_map/ppermute | solution.py:495
  (6 other events, 17.4 us)

commit v3 on v2

--- a/solution.py
+++ b/solution.py
@@ -355,7 +355,7 @@
         (lifted_all[...], hidden_all[...], active_all[...], branch_grad_all[...]),
     )
     for layer, (lifted, grad_hidden, active, grad_branch) in enumerate(operands):
-        at = layer * 2 * hidden_units
+        at = layer * (grads_out.shape[0] // BLOCKS)
         grad_in = dot_rows(lifted, grad_hidden)
         for group in range(groups):
             grads_out[pl.ds(at + group * channels, channels), :] = grad_in[
@@ -367,11 +367,9 @@
                 :, group * channels : (group + 1) * channels
             ].T.astype(BF16)
 
-    at = BLOCKS * 2 * hidden_units
-    tail = grads_out.shape[0] - at
     taps[...] = jnp.zeros_like(taps)
     for layer in range(BLOCKS):
-        base = layer * (TAPS + 5 + groups)
+        base = layer * (taps.shape[0] // BLOCKS)
         if layer:
             tap_sums(
                 inner,
@@ -405,7 +403,10 @@
             taps[pl.ds(base + TAPS + 5 + group, 1), :] = hidden_total[
                 :, group * channels : (group + 1) * channels
             ]
-    grads_out[pl.ds(at, tail), :] = taps[...].astype(BF16)
+    small = taps.shape[0] // BLOCKS
+    for layer in range(BLOCKS):
+        at = layer * (grads_out.shape[0] // BLOCKS) + 2 * hidden_units
+        grads_out[pl.ds(at, small), :] = taps[pl.ds(layer * small, small), :].astype(BF16)
 
 
 def state_kernel(window, masked, dw_in, out, wide, kernels):
@@ -429,45 +430,44 @@
 def code_kernel(lat, state, land_sea, cotangent, coded, edge):
     height, breadth, channels = state.shape
     ocean = jnp.where(land_sea[...] != 0, 1.0, 0.0).astype(F32)
-    shape = (height, breadth, breadth)
-    row_of = lax.broadcasted_iota(jnp.int32, shape, 1)
-    col_of = lax.broadcasted_iota(jnp.int32, shape, 2)
-    chosen = jnp.where(row_of == col_of, ocean[:, None, :], 0.0)
-    chosen = chosen.reshape(height * breadth, breadth).astype(BF16)
-    wide = dot(chosen, jnp.ones((breadth, channels), BF16)).reshape(height, breadth, channels)
-    coded[...] = jnp.where(wide > 0.5, cotangent[...].astype(F32), LAND).astype(BF16)
+    for row in range(height):
+        wide = jnp.broadcast_to(ocean[:, row : row + 1], (breadth, channels))
+        coded[row] = jnp.where(wide > 0.5, cotangent[row].astype(F32), LAND).astype(BF16)
     for side in range(edge.shape[0]):
         first = (1 - lat[0]) * (height - WIDE) if edge.shape[0] == 1 else (1 - side) * (height - WIDE)
         edge[side, :, :breadth] = state[pl.ds(first, WIDE)]
         edge[side, :, breadth:] = coded[pl.ds(first, WIDE)]
 
 
-def gradient_kernel(grad_norm, held, own, other, *outs_and_scratch):
-    *outs, total = outs_and_scratch
+def gradient_kernel(grad_norm, held, own, other, *outs):
     kernel, conv_bias, gain, shift, first, first_bias, second, second_bias, scale = outs
-    half = own.shape[0]
     channels = own.shape[1]
-    total[pl.ds(held[0] * half, half)] = own[...].astype(F32) * grad_norm
-    total[pl.ds((1 - held[0]) * half, half)] = other[...].astype(F32) * grad_norm
     units = second.shape[1]
     groups = units // channels
-    for layer in range(BLOCKS):
-        at = layer * 2 * units
+
+    def unpack(rows, layer):
         for group in range(groups):
-            first[layer, :, group * channels : (group + 1) * channels] = total[
-                at + group * channels : at + (group + 1) * channels
-            ]
-        second[layer] = total[at + units : at + 2 * units]
-        at = BLOCKS * 2 * units + layer * (TAPS + 5 + groups)
-        for tap_row in range(KSIZE):
-            kernel[layer, tap_row] = total[at + tap_row * KSIZE : at + (tap_row + 1) * KSIZE]
+            spots = pl.ds(group * channels, channels)
+            first[layer, :, spots] = rows[spots].astype(F32) * grad_norm
+        second[layer] = rows[pl.ds(units, units)].astype(F32) * grad_norm
+        small = rows[pl.ds(2 * units, rows.shape[0] - 2 * units)].astype(F32) * grad_norm
+        for index in range(TAPS):
+            kernel[index // KSIZE, index % KSIZE, layer : layer + 1] = small[index : index + 1]
         for member, out in enumerate((scale, second_bias, gain, shift, conv_bias)):
-            out[layer : layer + 1] = total[at + TAPS + member : at + TAPS + member + 1]
+            out[layer : layer + 1] = small[TAPS + member : TAPS + member + 1]
         for group in range(groups):
-            row = at + TAPS + 5 + group
-            first_bias[layer : layer + 1, group * channels : (group + 1) * channels] = total[
-                row : row + 1
-            ]
+            row = TAPS + 5 + group
+            first_bias[layer : layer + 1, pl.ds(group * channels, channels)] = small[row : row + 1]
+
+    @pl.when(held[0] == 0)
+    def _():
+        unpack(own, 0)
+        unpack(other, 1)
+
+    @pl.when(held[0] != 0)
+    def _():
+        unpack(own, 1)
+        unpack(other, 0)
 
 
 class Links:
@@ -508,7 +508,7 @@
         after = jnp.where(place == self.lat - 1, outside, after)
         return jnp.concatenate([before, field, after], axis=0)
 
-    def sum_all(self, rows):
+    def sum_all(self, rows, beside):
         lon = lax.axis_index("lon")
         lat = lax.axis_index("lat")
         bits = [(1 << bit, 0) for bit in range(self.lon.bit_length() - 1)]
@@ -560,7 +560,8 @@
             values = exchange(values, rest[:2])
             rest = rest[2:]
         values = gather(values, quad)
-        return code(pair), values, self.swap(values, *pair[0])
+        values, beside = lax.optimization_barrier((values, beside))
+        return code(pair), values, self.swap(values, *pair[0]), beside
 
 
 def on_device(links, state, land_sea, cotangent, *params):
@@ -590,7 +591,7 @@
         ),
         in_specs=[smem, vmem, vmem, vmem],
         out_specs=(vmem, vmem),
-    )(lat.reshape(1), state, land_sea, cotangent)
+    )(lat.reshape(1), state, land_sea.T, cotangent)
     if sides == 1:
         pieces = links.swap(edges, 0, 1)
         places = [(1 - lat) * height]
@@ -626,11 +627,9 @@
 
     padded_rows = window_rows + 2 * MARGIN
     all_cells = second_rows * inner_pitch
-    small_rows = round_up(BLOCKS * (TAPS + 5 + groups), 16)
-    grad_rows = BLOCKS * 2 * hidden_units + small_rows
-    unit = 16 * 8
-    small_rows += round_up(grad_rows, unit) - grad_rows
-    grad_rows = round_up(grad_rows, unit)
+    layer_rows = round_up(2 * hidden_units + TAPS + 5 + groups, 4 * 16)
+    small_rows = BLOCKS * (layer_rows - 2 * hidden_units)
+    grad_rows = BLOCKS * layer_rows
     own_rows = (window_rows, breadth)
     scratch = [
         pltpu.VMEM((padded_rows, state_pitch, channels), F32),
@@ -700,16 +699,16 @@
         ),
     )(spread, masked, taps_in[0])
 
-    held, own, other = links.sum_all(grads)
-    shapes = [(BLOCKS, KSIZE, KSIZE, channels)] + [member.shape for member in params[1:]]
-    gradients = pl.pallas_call(
+    held, own, other, grad_state = links.sum_all(grads, grad_state)
+    shapes = [(KSIZE, KSIZE, BLOCKS, channels)] + [member.shape for member in params[1:]]
+    grad_kernel, *gradients = pl.pallas_call(
         functools.partial(gradient_kernel, grad_norm),
         out_shape=tuple(jax.ShapeDtypeStruct(shape, F32) for shape in shapes),
         in_specs=[smem, vmem, vmem],
         out_specs=(vmem,) * 9,
-        scratch_shapes=[pltpu.VMEM((grad_rows, channels), F32)],
+        compiler_params=pltpu.CompilerParams(vmem_limit_bytes=8 * 1024 * 1024),
     )(held.reshape(1), own, other)
-    return (output, grad_state, *gradients)
+    return (output, grad_state, grad_kernel.transpose(2, 0, 1, 3), *gradients)
 
 
 def solution(mesh):

time: 83 us -> 83.5 us (level)
  waiting for transfers between devices: 15.7 us -> 21.4 us
  local copies, waits for them, and re-layouts: 4.04 us -> 1.16 us
  Pallas kernels: 36.2 us -> 35.1 us
  starting transfers between devices: 24.9 us -> 23.8 us
    ppermute x12, waiting for transfers between devices: 9.61 us -> 12.7 us  [swap(): return lax.ppermute(values, self.axes, pairs)]
    unnamed x28 -> x22, local copies, waits for them, and re-layouts: 3.62 us -> 0.74 us
    ppermute x4, waiting for transfers between devices: 6.1 us -> 8.74 us  [shift_lon(): return lax.ppermute(values, 'lon', pairs)]
    ppermute x12, starting transfers between devices: 16.2 us -> 14.6 us  [swap(): return lax.ppermute(values, self.axes, pairs)]
    pallas_call x1, Pallas kernels: 2.19 us -> 1.13 us  [on_device(): pl.pallas_call(functools.partial(gradient_kernel, grad_norm), out_shape=t...]
  transfers between devices with their start and end apart: 17 -> 17, of which waited for: 9 -> 10; matrix products, arithmetic and copies ran while one was open for 1% -> 1% of each run, Pallas kernels for 4% -> 4%
where the time goes in v3:
time: 83.5 us; the launch traced here: 83.3 us
  Pallas kernels  35.1 us (42%)
  starting transfers between devices  23.8 us (29%)
  waiting for transfers between devices  21.4 us (26%)
  local copies, waits for them, and re-layouts  1.16 us (1%)
  between operations  1.02 us (1%)
    pallas_call x1, Pallas kernels, on_device(): pl.pallas_call(functools.partial(tile_kernel, sizes), out_shape=(jax.Shap...  28.9 us
    ppermute x12, starting transfers between devices, swap(): return lax.ppermute(values, self.axes, pairs)  14.6 us
    ppermute x12, waiting for transfers between devices, swap(): return lax.ppermute(values, self.axes, pairs)  12.7 us
    ppermute x4, waiting for transfers between devices, shift_lon(): return lax.ppermute(values, 'lon', pairs)  8.74 us
    ppermute x4, starting transfers between devices, shift_lon(): return lax.ppermute(values, 'lon', pairs)  7.98 us
    pallas_call x1, Pallas kernels, on_device(): pl.pallas_call(state_kernel, out_shape=jax.ShapeDtypeStruct(tile, BF16),...  2.98 us
    pallas_call x1, Pallas kernels, on_device(): pl.pallas_call(code_kernel, out_shape=(jax.ShapeDtypeStruct(tile, BF16),...  2.05 us
  transfers between devices with their start and end apart: 17, of which 10 were waited for; matrix products, arithmetic and copies ran while one was open for 1% of the time, Pallas kernels for 4%

profile of v3, /device:TPU:0, one launch (start us, length us, event | category | flops | bytes accessed | tf_op | source)
XLA Modules:
  0.0 83.3 jit_solution(589945151177214119)
XLA Ops:
  0.7 2.1 %shard_map.203 = (bf16[45,24,128]{2,1,0:T(8,128)(2,1)}, bf16[1,9,48,128]{3,2,1,0:T(8,128)(2,1)}) custom-call(s32[1]{0:T(128)} %bitcast.4.lat, bf16[45,24,128]{2,1,0:T(8,128)(2,1)} %state_tile.1, s32[24,45]{1,0:T(8,128)} %bitcast.49, bf16[45,24,128]{2,1,0:T(8,128)(2,1)} %cotangent.1), custom_call_target="tpu_custom_call" | custom-call | tf_op jit(solution)/shard_map/pallas_call | solution.py:586
  2.7 2.9 %collective-permute-start = (bf16[1,9,48,128]{3,2,1,0:T(8,128)(2,1)}, bf16[1,9,48,128]{3,2,1,0:T(8,128)(2,1)S(1)}, u32[]{:S(2)}, u32[]{:S(2)}) collective-permute-start(bf16[1,9,48,128]{3,2,1,0:T(8,128)(2,1)} %get-tuple-element.29), channel_id=1, source_target_pairs={{0,1},{1,0},{2,3},{3,2},{4,5},{5,4},{6,7},{7,6},{8,9},{9,8},{10,11... | collective-permute-start | bytes 331784 | tf_op jit(solution)/shard_map/ppermute | solution.py:495
  5.8 3.1 %collective-permute-done.lat_pieces = bf16[1,9,48,128]{3,2,1,0:T(8,128)(2,1)S(1)} collective-permute-done((bf16[1,9,48,128]{3,2,1,0:T(8,128)(2,1)}, bf16[1,9,48,128]{3,2,1,0:T(8,128)(2,1)S(1)}, u32[]{:S(2)}, u32[]{:S(2)}) %collective-permute-start) | collective-permute-done | bytes 110624 | tf_op jit(solution)/shard_map/ppermute | solution.py:495
  9.1 3.4 %collective-permute-start.2 = (bf16[54,15,128]{2,1,0:T(8,128)(2,1)S(1)}, bf16[54,15,128]{2,1,0:T(8,128)(2,1)S(1)}, u32[]{:S(2)}, u32[]{:S(2)}) collective-permute-start(bf16[54,15,128]{2,1,0:T(8,128)(2,1)S(1)} %maximum_select_fusion.2), channel_id=1, source_target_pairs={{0,30},{2,0},{4,2},{6,4},{8,6},{10,8},{12,10},{14,12},{16,14},{18,... | collective-permute-start | bytes 622088 | tf_op jit(solution)/shard_map/ppermute | solution.py:481
  12.7 0.7 copy-done.10
  13.5 2.4 %collective-permute-done.2.east = bf16[54,15,128]{2,1,0:T(8,128)(2,1)S(1)} collective-permute-done((bf16[54,15,128]{2,1,0:T(8,128)(2,1)S(1)}, bf16[54,15,128]{2,1,0:T(8,128)(2,1)S(1)}, u32[]{:S(2)}, u32[]{:S(2)}) %collective-permute-start.2) | collective-permute-done | bytes 207392 | tf_op jit(solution)/shard_map/ppermute | solution.py:481
  15.9 4.8 %collective-permute-done.1.west = bf16[54,15,128]{2,1,0:T(8,128)(2,1)S(1)} collective-permute-done((bf16[54,15,128]{2,1,0:T(8,128)(2,1)S(1)}, bf16[54,15,128]{2,1,0:T(8,128)(2,1)S(1)}, u32[]{:S(2)}, u32[]{:S(2)}) %collective-permute-start.1) | collective-permute-done | bytes 207392 | tf_op jit(solution)/shard_map/ppermute | solution.py:481
  20.8 28.9 %shard_map.204 = (bf16[45,24,128]{2,1,0:T(8,128)(2,1)}, bf16[45,24,128]{2,1,0:T(8,128)(2,1)S(1)}, bf16[45,24,128]{2,1,0:T(8,128)(2,1)S(1)}, bf16[2176,128]{1,0:T(8,128)(2,1)S(1)}) custom-call(s32[4]{0:T(128)S(1)} %pad_add_fusion.starts, bf16[45,24,128]{2,1,0:T(8,128)(2,1)S(1)} %copy-done, bf16[45,24,128]{2,1,0:T(8,128)(2,1)S(1)} %copy-done.1, ...), custom_call_target="tpu_custom_call" | custom-call | flops 2013265920 | bytes 2211840 | tf_op jit(solution)/shard_map/pallas_call | solution.py:660
  50.4 4.0 %collective-permute-start.14 = (bf16[45,3,128]{2,1,0:T(4,128)(2,1)S(1)}, bf16[45,3,128]{2,1,0:T(4,128)(2,1)S(1)}, u32[]{:S(2)}, u32[]{:S(2)}) collective-permute-start(bf16[45,3,128]{2,1,0:T(4,128)(2,1)S(1)} %get-tuple-element.53), channel_id=1, source_target_pairs={{0,30},{2,0},{4,2},{6,4},{8,6},{10,8},{12,10},{14,12},{16,14},{18,... | collective-permute-start | bytes 103688 | tf_op jit(solution)/shard_map/ppermute | solution.py:481
  54.5 1.6 %collective-permute-done.13 = bf16[45,3,128]{2,1,0:T(4,128)(2,1)S(1)} collective-permute-done((bf16[45,3,128]{2,1,0:T(4,128)(2,1)S(1)}, bf16[45,3,128]{2,1,0:T(4,128)(2,1)S(1)}, u32[]{:S(2)}, u32[]{:S(2)}) %collective-permute-start.13) | collective-permute-done | bytes 34592 | tf_op jit(solution)/shard_map/ppermute | solution.py:481
  56.1 1.2 %collective-permute-start.15 = (bf16[3,30,128]{2,1,0:T(8,128)(2,1)S(1)}, bf16[3,30,128]{2,1,0:T(8,128)(2,1)S(1)}, u32[]{:S(2)}, u32[]{:S(2)}) collective-permute-start(bf16[3,30,128]{2,1,0:T(8,128)(2,1)S(1)} %fusion.4), channel_id=1, source_target_pairs={{0,1},{1,0},{2,3},{3,2},{4,5},{5,4},{6,7},{7,6},{8,9},{9,8},{10,11... | collective-permute-start | bytes 69128 | tf_op jit(solution)/shard_map/ppermute | solution.py:501
  57.4 1.0 %collective-permute-start.4 = (bf16[272,128]{1,0:T(8,128)(2,1)S(1)}, bf16[272,128]{1,0:T(8,128)(2,1)S(1)}, u32[]{:S(2)}, u32[]{:S(2)}) collective-permute-start(bf16[272,128]{1,0:T(8,128)(2,1)S(1)} %get-tuple-element.49), channel_id=1, source_target_pairs={{0,1},{1,0},{2,3},{3,2},{4,5},{5,4},{6,7},{7,6},{8,9},{9,8},{10,11... | collective-permute-start | bytes 208904 | tf_op jit(solution)/shard_map/ppermute | solution.py:495
  58.4 2.6 %collective-permute-start.6 = (bf16[272,128]{1,0:T(8,128)(2,1)S(1)}, bf16[272,128]{1,0:T(8,128)(2,1)S(1)}, u32[]{:S(2)}, u32[]{:S(2)}) collective-permute-start(bf16[272,128]{1,0:T(8,128)(2,1)S(1)} %get-tuple-element.50), channel_id=1, source_target_pairs={{0,5},{1,4},{2,7},{3,6},{4,1},{5,0},{6,3},{7,2},{8,13},{9,12},{10,... | collective-permute-start | bytes 208904 | tf_op jit(solution)/shard_map/ppermute | solution.py:495
  61.8 0.9 %collective-permute-done.5 = bf16[272,128]{1,0:T(8,128)(2,1)S(1)} collective-permute-done((bf16[272,128]{1,0:T(8,128)(2,1)S(1)}, bf16[272,128]{1,0:T(8,128)(2,1)S(1)}, u32[]{:S(2)}, u32[]{:S(2)}) %collective-permute-start.5) | collective-permute-done | bytes 69664 | tf_op jit(solution)/shard_map/ppermute | solution.py:495
  62.7 0.9 %collective-permute-done.6 = bf16[272,128]{1,0:T(8,128)(2,1)S(1)} collective-permute-done((bf16[272,128]{1,0:T(8,128)(2,1)S(1)}, bf16[272,128]{1,0:T(8,128)(2,1)S(1)}, u32[]{:S(2)}, u32[]{:S(2)}) %collective-permute-start.6) | collective-permute-done | bytes 69664 | tf_op jit(solution)/shard_map/ppermute | solution.py:495
  64.2 3.9 %collective-permute-start.9 = (bf16[272,128]{1,0:T(8,128)(2,1)S(1)}, bf16[272,128]{1,0:T(8,128)(2,1)S(1)}, u32[]{:S(2)}, u32[]{:S(2)}) collective-permute-start(bf16[272,128]{1,0:T(8,128)(2,1)S(1)} %fusion.3), channel_id=1, source_target_pairs={{0,24},{1,25},{2,26},{3,27},{4,28},{5,29},{6,30},{7,31},{8,16},{9,... | collective-permute-start | bytes 208904 | tf_op jit(solution)/shard_map/ppermute | solution.py:495
  68.3 4.5 %collective-permute-done.8 = bf16[272,128]{1,0:T(8,128)(2,1)S(1)} collective-permute-done((bf16[272,128]{1,0:T(8,128)(2,1)S(1)}, bf16[272,128]{1,0:T(8,128)(2,1)S(1)}, u32[]{:S(2)}, u32[]{:S(2)}) %collective-permute-start.8) | collective-permute-done | bytes 69664 | tf_op jit(solution)/shard_map/ppermute | solution.py:495
  72.8 1.2 %collective-permute-start.10 = (bf16[272,128]{1,0:T(8,128)(2,1)S(1)}, bf16[272,128]{1,0:T(8,128)(2,1)S(1)}, u32[]{:S(2)}, u32[]{:S(2)}) collective-permute-start(bf16[272,128]{1,0:T(8,128)(2,1)S(1)} %add_convert_fusion), channel_id=1, source_target_pairs={{0,1},{1,0},{2,3},{3,2},{4,5},{5,4},{6,7},{7,6},{8,9},{9,8},{10,11... | collective-permute-start | bytes 208904 | tf_op jit(solution)/shard_map/ppermute | solution.py:495
  74.0 1.3 %collective-permute-start.11 = (bf16[272,128]{1,0:T(8,128)(2,1)S(1)}, bf16[272,128]{1,0:T(8,128)(2,1)S(1)}, u32[]{:S(2)}, u32[]{:S(2)}) collective-permute-start(bf16[272,128]{1,0:T(8,128)(2,1)S(1)} %add_convert_fusion), channel_id=1, source_target_pairs={{0,4},{1,5},{2,6},{3,7},{4,0},{5,1},{6,2},{7,3},{8,12},{9,13},{10,... | collective-permute-start | bytes 208904 | tf_op jit(solution)/shard_map/ppermute | solution.py:495
  75.3 1.1 %collective-permute-start.12 = (bf16[272,128]{1,0:T(8,128)(2,1)S(1)}, bf16[272,128]{1,0:T(8,128)(2,1)S(1)}, u32[]{:S(2)}, u32[]{:S(2)}) collective-permute-start(bf16[272,128]{1,0:T(8,128)(2,1)S(1)} %add_convert_fusion), channel_id=1, source_target_pairs={{0,5},{1,4},{2,7},{3,6},{4,1},{5,0},{6,3},{7,2},{8,13},{9,12},{10,... | collective-permute-start | bytes 208904 | tf_op jit(solution)/shard_map/ppermute | solution.py:495
  76.3 3.0 %shard_map.205 = bf16[45,24,128]{2,1,0:T(8,128)(2,1)} custom-call(bf16[51,32,128]{2,1,0:T(8,128)(2,1)S(1)} %pad.6.window, bf16[45,24,128]{2,1,0:T(8,128)(2,1)S(1)} %get-tuple-element.33.masked, bf16[49,128]{1,0:T(8,128)(2,1)S(1)} %squeeze.39.dw_in), custom_call_target="tpu_custom_call" | custom-call | flops 4000000000 | bytes 8000000 | tf_op jit(solution)/shard_map/pallas_call | solution.py:690
  79.3 1.1 %collective-permute-done.12 = bf16[272,128]{1,0:T(8,128)(2,1)S(1)} collective-permute-done((bf16[272,128]{1,0:T(8,128)(2,1)S(1)}, bf16[272,128]{1,0:T(8,128)(2,1)S(1)}, u32[]{:S(2)}, u32[]{:S(2)}) %collective-permute-start.12) | collective-permute-done | bytes 69664 | tf_op jit(solution)/shard_map/ppermute | solution.py:495
  80.7 1.5 %collective-permute-done.16.other = bf16[1088,128]{1,0:T(8,128)(2,1)S(1)} collective-permute-done((bf16[1088,128]{1,0:T(8,128)(2,1)S(1)}, bf16[1088,128]{1,0:T(8,128)(2,1)S(1)}, u32[]{:S(2)}, u32[]{:S(2)}) %collective-permute-start.16) | collective-permute-done | bytes 278560 | tf_op jit(solution)/shard_map/ppermute | solution.py:495
  82.2 1.1 %shard_map.206 = (f32[7,7,2,128]{3,2,1,0:T(2,128)}, f32[2,128]{1,0:T(2,128)}, f32[2,128]{1,0:T(2,128)}, f32[2,128]{1,0:T(2,128)}, f32[2,128,512]{2,1,0:T(8,128)}...) custom-call(s32[1]{0:T(128)} %bitcast.24.held, ...), custom_call_target="tpu_custom_call" | custom-call | tf_op jit(solution)/shard_map/pallas_call | solution.py:704
  (59 shorter events, 3.2 us)
Async XLA Ops:
  2.7 6.2 %collective-permute-start = (bf16[1,9,48,128]{3,2,1,0:T(8,128)(2,1)}, bf16[1,9,48,128]{3,2,1,0:T(8,128)(2,1)S(1)}, u32[]{:S(2)}, u32[]{:S(2)}) collective-permute-start(bf16[1,9,48,128]{3,2,1,0:T(8,128)(2,1)} %get-tuple-element.29), channel_id=1, source_target_pairs={{0,1},{1,0},{2,3},{3,2},{4,5},{5,4},{6,7},{7,6},{8,9},{9,8},{10,11... | collective-permute-start | bytes 331784 | tf_op jit(solution)/shard_map/ppermute | solution.py:495
  9.1 6.9 %collective-permute-start.2 = (bf16[54,15,128]{2,1,0:T(8,128)(2,1)S(1)}, bf16[54,15,128]{2,1,0:T(8,128)(2,1)S(1)}, u32[]{:S(2)}, u32[]{:S(2)}) collective-permute-start(bf16[54,15,128]{2,1,0:T(8,128)(2,1)S(1)} %maximum_select_fusion.2), channel_id=1, source_target_pairs={{0,30},{2,0},{4,2},{6,4},{8,6},{10,8},{12,10},{14,12},{16,14},{18,... | collective-permute-start | bytes 622088 | tf_op jit(solution)/shard_map/ppermute | solution.py:481
  12.5 8.2 %copy-start.2 = (bf16[2,128,512]{2,1,0:T(8,128)(2,1)S(1)}, bf16[2,128,512]{2,1,0:T(8,128)(2,1)}, u32[]{:S(2)}) copy-start(bf16[2,128,512]{2,1,0:T(8,128)(2,1)} %weight_in.1) | copy-start | bytes 786436
  12.5 8.2 %copy-start.3 = (bf16[2,512,128]{2,1,0:T(8,128)(2,1)S(1)}, bf16[2,512,128]{2,1,0:T(8,128)(2,1)}, u32[]{:S(2)}) copy-start(bf16[2,512,128]{2,1,0:T(8,128)(2,1)} %weight_out.1) | copy-start | bytes 786436
  12.6 8.1 %collective-permute-start.1 = (bf16[54,15,128]{2,1,0:T(8,128)(2,1)S(1)}, bf16[54,15,128]{2,1,0:T(8,128)(2,1)S(1)}, u32[]{:S(2)}, u32[]{:S(2)}) collective-permute-start(bf16[54,15,128]{2,1,0:T(8,128)(2,1)S(1)} %maximum_select_fusion.1), channel_id=1, source_target_pairs={{0,2},{2,4},{4,6},{6,8},{8,10},{10,12},{12,14},{14,16},{16,18},{18... | collective-permute-start | bytes 622088 | tf_op jit(solution)/shard_map/ppermute | solution.py:481
  13.4 7.3 %copy-start.7 = (f32[2,128]{1,0:T(2,128)S(1)}, f32[2,128]{1,0:T(2,128)}, u32[]{:S(2)}) copy-start(f32[2,128]{1,0:T(2,128)} %norm_bias.1) | copy-start | bytes 3076
  13.4 7.3 %copy-start.8 = (f32[2,128]{1,0:T(2,128)S(1)}, f32[2,128]{1,0:T(2,128)}, u32[]{:S(2)}) copy-start(f32[2,128]{1,0:T(2,128)} %bias_out.1) | copy-start | bytes 3076
  13.4 7.3 %copy-start.9 = (f32[2,128]{1,0:T(2,128)S(1)}, f32[2,128]{1,0:T(2,128)}, u32[]{:S(2)}) copy-start(f32[2,128]{1,0:T(2,128)} %layer_scale.1) | copy-start | bytes 3076
  13.4 7.3 %copy-start.4 = (f32[2,512]{1,0:T(2,128)S(1)}, f32[2,512]{1,0:T(2,128)}, u32[]{:S(2)}) copy-start(f32[2,512]{1,0:T(2,128)} %bias_in.1) | copy-start | bytes 12292
  13.4 7.3 %copy-start.5 = (f32[2,128]{1,0:T(2,128)S(1)}, f32[2,128]{1,0:T(2,128)}, u32[]{:S(2)}) copy-start(f32[2,128]{1,0:T(2,128)} %conv_bias.1) | copy-start | bytes 3076
  49.7 7.6 %collective-permute-start.3 = (bf16[1088,128]{1,0:T(8,128)(2,1)S(1)}, bf16[1088,128]{1,0:T(8,128)(2,1)S(1)}, u32[]{:S(2)}, u32[]{:S(2)}) collective-permute-start(bf16[1088,128]{1,0:T(8,128)(2,1)S(1)} %dynamic-slice_bitcast_fusion), channel_id=1, source_target_pairs={{0,2},{1,3},{2,0},{3,1},{4,6},{5,7},{6,4},{7,5},{8,10},{9,11},{10,... | collective-permute-start | bytes 835592 | tf_op jit(solution)/shard_map/ppermute | solution.py:495
  49.9 6.2 %collective-permute-start.13 = (bf16[45,3,128]{2,1,0:T(4,128)(2,1)S(1)}, bf16[45,3,128]{2,1,0:T(4,128)(2,1)S(1)}, u32[]{:S(2)}, u32[]{:S(2)}) collective-permute-start(bf16[45,3,128]{2,1,0:T(4,128)(2,1)S(1)} %get-tuple-element.52), channel_id=1, source_target_pairs={{0,2},{2,4},{4,6},{6,8},{8,10},{10,12},{12,14},{14,16},{16,18},{18... | collective-permute-start | bytes 103688 | tf_op jit(solution)/shard_map/ppermute | solution.py:481
  50.4 5.7 %collective-permute-start.14 = (bf16[45,3,128]{2,1,0:T(4,128)(2,1)S(1)}, bf16[45,3,128]{2,1,0:T(4,128)(2,1)S(1)}, u32[]{:S(2)}, u32[]{:S(2)}) collective-permute-start(bf16[45,3,128]{2,1,0:T(4,128)(2,1)S(1)} %get-tuple-element.53), channel_id=1, source_target_pairs={{0,30},{2,0},{4,2},{6,4},{8,6},{10,8},{12,10},{14,12},{16,14},{18,... | collective-permute-start | bytes 103688 | tf_op jit(solution)/shard_map/ppermute | solution.py:481
  56.1 4.9 %collective-permute-start.15 = (bf16[3,30,128]{2,1,0:T(8,128)(2,1)S(1)}, bf16[3,30,128]{2,1,0:T(8,128)(2,1)S(1)}, u32[]{:S(2)}, u32[]{:S(2)}) collective-permute-start(bf16[3,30,128]{2,1,0:T(8,128)(2,1)S(1)} %fusion.4), channel_id=1, source_target_pairs={{0,1},{1,0},{2,3},{3,2},{4,5},{5,4},{6,7},{7,6},{8,9},{9,8},{10,11... | collective-permute-start | bytes 69128 | tf_op jit(solution)/shard_map/ppermute | solution.py:501
  57.4 4.4 %collective-permute-start.4 = (bf16[272,128]{1,0:T(8,128)(2,1)S(1)}, bf16[272,128]{1,0:T(8,128)(2,1)S(1)}, u32[]{:S(2)}, u32[]{:S(2)}) collective-permute-start(bf16[272,128]{1,0:T(8,128)(2,1)S(1)} %get-tuple-element.49), channel_id=1, source_target_pairs={{0,1},{1,0},{2,3},{3,2},{4,5},{5,4},{6,7},{7,6},{8,9},{9,8},{10,11... | collective-permute-start | bytes 208904 | tf_op jit(solution)/shard_map/ppermute | solution.py:495
  58.4 4.3 %collective-permute-start.5 = (bf16[272,128]{1,0:T(8,128)(2,1)S(1)}, bf16[272,128]{1,0:T(8,128)(2,1)S(1)}, u32[]{:S(2)}, u32[]{:S(2)}) collective-permute-start(bf16[272,128]{1,0:T(8,128)(2,1)S(1)} %get-tuple-element.51), channel_id=1, source_target_pairs={{0,4},{1,5},{2,6},{3,7},{4,0},{5,1},{6,2},{7,3},{8,12},{9,13},{10,... | collective-permute-start | bytes 208904 | tf_op jit(solution)/shard_map/ppermute | solution.py:495
  58.4 5.2 %collective-permute-start.6 = (bf16[272,128]{1,0:T(8,128)(2,1)S(1)}, bf16[272,128]{1,0:T(8,128)(2,1)S(1)}, u32[]{:S(2)}, u32[]{:S(2)}) collective-permute-start(bf16[272,128]{1,0:T(8,128)(2,1)S(1)} %get-tuple-element.50), channel_id=1, source_target_pairs={{0,5},{1,4},{2,7},{3,6},{4,1},{5,0},{6,3},{7,2},{8,13},{9,12},{10,... | collective-permute-start | bytes 208904 | tf_op jit(solution)/shard_map/ppermute | solution.py:495
  63.7 4.6 %collective-permute-start.7 = (bf16[272,128]{1,0:T(8,128)(2,1)S(1)}, bf16[272,128]{1,0:T(8,128)(2,1)S(1)}, u32[]{:S(2)}, u32[]{:S(2)}) collective-permute-start(bf16[272,128]{1,0:T(8,128)(2,1)S(1)} %fusion.3), channel_id=1, source_target_pairs={{0,8},{1,9},{2,10},{3,11},{4,12},{5,13},{6,14},{7,15},{8,0},{9,1},... | collective-permute-start | bytes 208904 | tf_op jit(solution)/shard_map/ppermute | solution.py:495
  63.7 9.0 %collective-permute-start.8 = (bf16[272,128]{1,0:T(8,128)(2,1)S(1)}, bf16[272,128]{1,0:T(8,128)(2,1)S(1)}, u32[]{:S(2)}, u32[]{:S(2)}) collective-permute-start(bf16[272,128]{1,0:T(8,128)(2,1)S(1)} %fusion.3), channel_id=1, source_target_pairs={{0,16},{1,17},{2,18},{3,19},{4,20},{5,21},{6,22},{7,23},{8,24},{9,... | collective-permute-start | bytes 208904 | tf_op jit(solution)/shard_map/ppermute | solution.py:495
  64.2 8.5 %collective-permute-start.9 = (bf16[272,128]{1,0:T(8,128)(2,1)S(1)}, bf16[272,128]{1,0:T(8,128)(2,1)S(1)}, u32[]{:S(2)}, u32[]{:S(2)}) collective-permute-start(bf16[272,128]{1,0:T(8,128)(2,1)S(1)} %fusion.3), channel_id=1, source_target_pairs={{0,24},{1,25},{2,26},{3,27},{4,28},{5,29},{6,30},{7,31},{8,16},{9,... | collective-permute-start | bytes 208904 | tf_op jit(solution)/shard_map/ppermute | solution.py:495
  72.8 6.5 %collective-permute-start.10 = (bf16[272,128]{1,0:T(8,128)(2,1)S(1)}, bf16[272,128]{1,0:T(8,128)(2,1)S(1)}, u32[]{:S(2)}, u32[]{:S(2)}) collective-permute-start(bf16[272,128]{1,0:T(8,128)(2,1)S(1)} %add_convert_fusion), channel_id=1, source_target_pairs={{0,1},{1,0},{2,3},{3,2},{4,5},{5,4},{6,7},{7,6},{8,9},{9,8},{10,11... | collective-permute-start | bytes 208904 | tf_op jit(solution)/shard_map/ppermute | solution.py:495
  74.0 5.3 %collective-permute-start.11 = (bf16[272,128]{1,0:T(8,128)(2,1)S(1)}, bf16[272,128]{1,0:T(8,128)(2,1)S(1)}, u32[]{:S(2)}, u32[]{:S(2)}) collective-permute-start(bf16[272,128]{1,0:T(8,128)(2,1)S(1)} %add_convert_fusion), channel_id=1, source_target_pairs={{0,4},{1,5},{2,6},{3,7},{4,0},{5,1},{6,2},{7,3},{8,12},{9,13},{10,... | collective-permute-start | bytes 208904 | tf_op jit(solution)/shard_map/ppermute | solution.py:495
  75.3 5.2 %collective-permute-start.12 = (bf16[272,128]{1,0:T(8,128)(2,1)S(1)}, bf16[272,128]{1,0:T(8,128)(2,1)S(1)}, u32[]{:S(2)}, u32[]{:S(2)}) collective-permute-start(bf16[272,128]{1,0:T(8,128)(2,1)S(1)} %add_convert_fusion), channel_id=1, source_target_pairs={{0,5},{1,4},{2,7},{3,6},{4,1},{5,0},{6,3},{7,2},{8,13},{9,12},{10,... | collective-permute-start | bytes 208904 | tf_op jit(solution)/shard_map/ppermute | solution.py:495
  80.6 1.6 %collective-permute-start.16 = (bf16[1088,128]{1,0:T(8,128)(2,1)S(1)}, bf16[1088,128]{1,0:T(8,128)(2,1)S(1)}, u32[]{:S(2)}, u32[]{:S(2)}) collective-permute-start(bf16[1088,128]{1,0:T(8,128)(2,1)S(1)} %pad_maximum_fusion.1.own), channel_id=1, source_target_pairs={{0,2},{1,3},{2,0},{3,1},{4,6},{5,7},{6,4},{7,5},{8,10},{9,11},{10,... | collective-permute-start | bytes 835592 | tf_op jit(solution)/shard_map/ppermute | solution.py:495
  (4 other events, 16.1 us)

commit v4 on v3

--- a/solution.py
+++ b/solution.py
@@ -20,9 +20,9 @@
 F32 = jnp.float32
 BF16 = jnp.bfloat16
 FIRST_STEP = 19
-SECOND_STEP = 8
-BACK_STEP = 9
-TAP_STEP = 5
+SECOND_STEP = 17
+BACK_STEP = 45
+TAP_STEP = 9
 STATE_AT = 11
 FIELD_AT = 8
 INNER_AT = 3
@@ -38,21 +38,39 @@
     return (size + unit - 1) // unit * unit
 
 
+def pack_rows(above, below):
+    shape = (above.shape[0] // 8, 8, above.shape[1])
+    return jnp.concatenate([above.reshape(shape), below.reshape(shape)], axis=1).astype(BF16)
+
+
 def conv_rows(source, base, first, count, width, kernel_ref, flip):
-    sums = [None] * count
+    pairs = (count + 1) // 2
+    sums = [[None, None] for _ in range(pairs)]
+    channels = source.shape[2]
     for tap_col in range(KSIZE):
+        parts = [None] * pairs
         taps = []
         for tap_row in range(KSIZE):
             index = tap_row * KSIZE + tap_col
-            taps.append(kernel_ref[pl.ds(TAPS - 1 - index if flip else index, 1), :])
-        for row in range(count + KSIZE - 1):
-            piece = source[base + row, pl.ds(first + tap_col, width), :]
-            for tap_row in range(KSIZE):
-                out = row - tap_row
-                if 0 <= out < count:
-                    term = piece * taps[tap_row]
-                    sums[out] = term if sums[out] is None else sums[out] + term
-    return jnp.concatenate(sums, axis=0)
+            tap = kernel_ref[pl.ds(TAPS - 1 - index if flip else index, 1), :]
+            taps.append(jnp.broadcast_to(tap, (16, channels)).astype(BF16)[None])
+        above = source[base, pl.ds(first + tap_col, width), :]
+        for row in range(2 * pairs + KSIZE - 2):
+            below = source[base + row + 1, pl.ds(first + tap_col, width), :]
+            both = pack_rows(above, below)
+            above = below
+            for tap_row in range(row % 2, KSIZE, 2):
+                out = (row - tap_row) // 2
+                if 0 <= out < pairs:
+                    term = both * taps[tap_row]
+                    parts[out] = term if parts[out] is None else parts[out] + term
+        for out in range(pairs):
+            for side in range(2):
+                value = parts[out].astype(F32)[:, 8 * side : 8 * side + 8]
+                old = sums[out][side]
+                sums[out][side] = value if old is None else old + value
+    rows = [sums[row // 2][row % 2].reshape(width, channels) for row in range(count)]
+    return jnp.concatenate(rows, axis=0)
 
 
 def normal_parts(hidden):
@@ -102,19 +120,36 @@
 
 def tap_sums(grad_ref, grad_row, grad_col, field_ref, field_row, field_col, height, width, out):
     rows = divisor(height, TAP_STEP)
+    pairs = (rows + 1) // 2
     for cols in ((0, 1, 2, 3), (4, 5, 6)):
 
         def advance(step, sums):
             sums = list(sums)
             at = step * rows
             grads = [grad_ref[grad_row + at + row, pl.ds(grad_col, width), :] for row in range(rows)]
+            grads += [jnp.zeros_like(grads[0])] * (2 * pairs - rows)
+            grads = [pack_rows(grads[2 * pair], grads[2 * pair + 1]) for pair in range(pairs)]
             for place, tap_col in enumerate(cols):
-                for row in range(rows + KSIZE - 1):
-                    piece = field_ref[field_row + at + row, pl.ds(field_col + tap_col, width), :]
-                    for tap_row in range(KSIZE):
-                        if 0 <= row - tap_row < rows:
-                            index = place * KSIZE + tap_row
-                            sums[index] = sums[index] + fold(grads[row - tap_row] * piece)
+                spots = pl.ds(field_col + tap_col, width)
+                parts = [None] * KSIZE
+                above = field_ref[field_row + at, spots, :]
+                for row in range(2 * pairs + KSIZE - 2):
+                    below = field_ref[field_row + at + row + 1, spots, :]
+                    both = pack_rows(above, below)
+                    above = below
+                    for tap_row in range(row % 2, KSIZE, 2):
+                        pair = (row - tap_row) // 2
+                        if 0 <= pair < pairs:
+                            term = grads[pair] * both
+                            old = parts[tap_row]
+                            parts[tap_row] = term if old is None else old + term
+                for tap_row in range(KSIZE):
+                    part = parts[tap_row]
+                    total = part[0]
+                    for group in range(1, part.shape[0]):
+                        total = total + part[group]
+                    index = place * KSIZE + tap_row
+                    sums[index] = sums[index] + fold(total.astype(F32))
             return tuple(sums)
 
         zeros = tuple(jnp.zeros((8, grad_ref.shape[2]), F32) for _ in range(KSIZE * len(cols)))
@@ -179,9 +214,9 @@
     pad = MARGIN
 
     for ref in (state, coded, field, inner):
-        edge = jnp.zeros((pad,) + ref.shape[1:], F32)
-        ref[pl.ds(0, pad)] = edge
-        ref[pl.ds(pad + window_rows, pad)] = edge
+        ref[pl.ds(0, pad)] = jnp.zeros((pad,) + ref.shape[1:], F32)
+        below = ref.shape[0] - pad - window_rows
+        ref[pl.ds(pad + window_rows, below)] = jnp.zeros((below,) + ref.shape[1:], F32)
     state[pl.ds(pad, window_rows)] = jnp.zeros((window_rows,) + state.shape[1:], F32)
     coded[pl.ds(pad, window_rows)] = jnp.zeros((window_rows,) + coded.shape[1:], F32)
 
@@ -625,7 +660,7 @@
         round_up(breadth + size, 8) for size in (STATE_AT + WIDE, FIELD_AT + NARROW, NARROW)
     )
 
-    padded_rows = window_rows + 2 * MARGIN
+    padded_rows = window_rows + 2 * MARGIN + 1
     all_cells = second_rows * inner_pitch
     layer_rows = round_up(2 * hidden_units + TAPS + 5 + groups, 4 * 16)
     small_rows = BLOCKS * (layer_rows - 2 * hidden_units)
@@ -686,7 +721,7 @@
         last = jnp.concatenate([spread, empty], axis=0)
         spread = jnp.where(lat == 0, first, last)
     pitch = round_up(spread.shape[1], 8)
-    spread = jnp.pad(spread, ((0, 0), (0, pitch - spread.shape[1]), (0, 0)))
+    spread = jnp.pad(spread, ((0, 1), (0, pitch - spread.shape[1]), (0, 0)))
     grad_state = pl.pallas_call(
         state_kernel,
         out_shape=jax.ShapeDtypeStruct(tile, BF16),

time: 83.5 us -> 74.9 us (0.90)
  Pallas kernels: 35.1 us -> 25 us
  waiting for transfers between devices: 21.4 us -> 22.3 us
    pallas_call x1, Pallas kernels: 28.9 us -> 19.7 us  [on_device(): pl.pallas_call(functools.partial(tile_kernel, sizes), out_shape=(jax.Shap...]
    ppermute x12, waiting for transfers between devices: 12.7 us -> 13.6 us  [swap(): return lax.ppermute(values, self.axes, pairs)]
    pallas_call x1, Pallas kernels: 2.98 us -> 2.1 us  [on_device(): pl.pallas_call(state_kernel, out_shape=jax.ShapeDtypeStruct(tile, BF16),...]
  transfers between devices with their start and end apart: 17 -> 17, of which waited for: 10 -> 11; matrix products, arithmetic and copies ran while one was open for 1% -> 1% of each run, Pallas kernels for 4% -> 3%
where the time goes in v4:
time: 74.9 us; the launch traced here: 74.8 us
  Pallas kernels  25 us (33%)
  starting transfers between devices  24.5 us (33%)
  waiting for transfers between devices  22.3 us (30%)
  local copies, waits for them, and re-layouts  1.16 us (2%)
  between operations  1.02 us (1%)
  other arithmetic  0.81 us (1%)
    pallas_call x1, Pallas kernels, on_device(): pl.pallas_call(functools.partial(tile_kernel, sizes), out_shape=(jax.Shap...  19.7 us
    ppermute x12, starting transfers between devices, swap(): return lax.ppermute(values, self.axes, pairs)  14.6 us
    ppermute x12, waiting for transfers between devices, swap(): return lax.ppermute(values, self.axes, pairs)  13.6 us
    ppermute x4, waiting for transfers between devices, shift_lon(): return lax.ppermute(values, 'lon', pairs)  8.74 us
    ppermute x4, starting transfers between devices, shift_lon(): return lax.ppermute(values, 'lon', pairs)  7.98 us
    pallas_call x1, Pallas kernels, on_device(): pl.pallas_call(state_kernel, out_shape=jax.ShapeDtypeStruct(tile, BF16),...  2.1 us
    pallas_call x1, Pallas kernels, on_device(): pl.pallas_call(code_kernel, out_shape=(jax.ShapeDtypeStruct(tile, BF16),...  2.05 us
    ppermute x1, starting transfers between devices, extend_lat(): other = lax.ppermute(mine, 'lat', [(0, 1), (1, 0)])  1.89 us
  transfers between devices with their start and end apart: 17, of which 11 were waited for; matrix products, arithmetic and copies ran while one was open for 1% of the time, Pallas kernels for 3%

profile of v4, /device:TPU:0, one launch (start us, length us, event | category | flops | bytes accessed | tf_op | source)
XLA Modules:
  0.0 74.8 jit_solution(517880739428239301)
XLA Ops:
  0.7 2.1 %shard_map.203 = (bf16[45,24,128]{2,1,0:T(8,128)(2,1)}, bf16[1,9,48,128]{3,2,1,0:T(8,128)(2,1)}) custom-call(s32[1]{0:T(128)} %bitcast.4.lat, bf16[45,24,128]{2,1,0:T(8,128)(2,1)} %state_tile.1, s32[24,45]{1,0:T(8,128)} %bitcast.49, bf16[45,24,128]{2,1,0:T(8,128)(2,1)} %cotangent.1), custom_call_target="tpu_custom_call" | custom-call | tf_op jit(solution)/shard_map/pallas_call | solution.py:621
  2.7 2.9 %collective-permute-start = (bf16[1,9,48,128]{3,2,1,0:T(8,128)(2,1)}, bf16[1,9,48,128]{3,2,1,0:T(8,128)(2,1)S(1)}, u32[]{:S(2)}, u32[]{:S(2)}) collective-permute-start(bf16[1,9,48,128]{3,2,1,0:T(8,128)(2,1)} %get-tuple-element.29), channel_id=1, source_target_pairs={{0,1},{1,0},{2,3},{3,2},{4,5},{5,4},{6,7},{7,6},{8,9},{9,8},{10,11... | collective-permute-start | bytes 331784 | tf_op jit(solution)/shard_map/ppermute | solution.py:530
  5.8 3.1 %collective-permute-done.lat_pieces = bf16[1,9,48,128]{3,2,1,0:T(8,128)(2,1)S(1)} collective-permute-done((bf16[1,9,48,128]{3,2,1,0:T(8,128)(2,1)}, bf16[1,9,48,128]{3,2,1,0:T(8,128)(2,1)S(1)}, u32[]{:S(2)}, u32[]{:S(2)}) %collective-permute-start) | collective-permute-done | bytes 110624 | tf_op jit(solution)/shard_map/ppermute | solution.py:530
  9.1 3.4 %collective-permute-start.2 = (bf16[54,15,128]{2,1,0:T(8,128)(2,1)S(1)}, bf16[54,15,128]{2,1,0:T(8,128)(2,1)S(1)}, u32[]{:S(2)}, u32[]{:S(2)}) collective-permute-start(bf16[54,15,128]{2,1,0:T(8,128)(2,1)S(1)} %maximum_select_fusion.2), channel_id=1, source_target_pairs={{0,30},{2,0},{4,2},{6,4},{8,6},{10,8},{12,10},{14,12},{16,14},{18,... | collective-permute-start | bytes 622088 | tf_op jit(solution)/shard_map/ppermute | solution.py:516
  12.7 0.7 copy-done.10
  13.5 2.4 %collective-permute-done.2.east = bf16[54,15,128]{2,1,0:T(8,128)(2,1)S(1)} collective-permute-done((bf16[54,15,128]{2,1,0:T(8,128)(2,1)S(1)}, bf16[54,15,128]{2,1,0:T(8,128)(2,1)S(1)}, u32[]{:S(2)}, u32[]{:S(2)}) %collective-permute-start.2) | collective-permute-done | bytes 207392 | tf_op jit(solution)/shard_map/ppermute | solution.py:516
  15.9 4.8 %collective-permute-done.1.west = bf16[54,15,128]{2,1,0:T(8,128)(2,1)S(1)} collective-permute-done((bf16[54,15,128]{2,1,0:T(8,128)(2,1)S(1)}, bf16[54,15,128]{2,1,0:T(8,128)(2,1)S(1)}, u32[]{:S(2)}, u32[]{:S(2)}) %collective-permute-start.1) | collective-permute-done | bytes 207392 | tf_op jit(solution)/shard_map/ppermute | solution.py:516
  20.8 19.7 %shard_map.204 = (bf16[45,24,128]{2,1,0:T(8,128)(2,1)}, bf16[45,24,128]{2,1,0:T(8,128)(2,1)S(1)}, bf16[45,24,128]{2,1,0:T(8,128)(2,1)S(1)}, bf16[2176,128]{1,0:T(8,128)(2,1)S(1)}) custom-call(s32[4]{0:T(128)S(1)} %pad_add_fusion.starts, bf16[45,24,128]{2,1,0:T(8,128)(2,1)S(1)} %copy-done, bf16[45,24,128]{2,1,0:T(8,128)(2,1)S(1)} %copy-done.1, ...), custom_call_target="tpu_custom_call" | custom-call | flops 2013265920 | bytes 2211840 | tf_op jit(solution)/shard_map/pallas_call | solution.py:695
  41.2 4.0 %collective-permute-start.14 = (bf16[45,3,128]{2,1,0:T(4,128)(2,1)S(1)}, bf16[45,3,128]{2,1,0:T(4,128)(2,1)S(1)}, u32[]{:S(2)}, u32[]{:S(2)}) collective-permute-start(bf16[45,3,128]{2,1,0:T(4,128)(2,1)S(1)} %get-tuple-element.53), channel_id=1, source_target_pairs={{0,30},{2,0},{4,2},{6,4},{8,6},{10,8},{12,10},{14,12},{16,14},{18,... | collective-permute-start | bytes 103688 | tf_op jit(solution)/shard_map/ppermute | solution.py:516
  45.3 1.6 %collective-permute-done.13 = bf16[45,3,128]{2,1,0:T(4,128)(2,1)S(1)} collective-permute-done((bf16[45,3,128]{2,1,0:T(4,128)(2,1)S(1)}, bf16[45,3,128]{2,1,0:T(4,128)(2,1)S(1)}, u32[]{:S(2)}, u32[]{:S(2)}) %collective-permute-start.13) | collective-permute-done | bytes 34592 | tf_op jit(solution)/shard_map/ppermute | solution.py:516
  46.9 1.9 %collective-permute-start.15 = (bf16[3,30,128]{2,1,0:T(8,128)(2,1)S(1)}, bf16[3,30,128]{2,1,0:T(8,128)(2,1)S(1)}, u32[]{:S(2)}, u32[]{:S(2)}) collective-permute-start(bf16[3,30,128]{2,1,0:T(8,128)(2,1)S(1)} %fusion.4), channel_id=1, source_target_pairs={{0,1},{1,0},{2,3},{3,2},{4,5},{5,4},{6,7},{7,6},{8,9},{9,8},{10,11... | collective-permute-start | bytes 69128 | tf_op jit(solution)/shard_map/ppermute | solution.py:536
  49.2 3.3 %collective-permute-start.6 = (bf16[272,128]{1,0:T(8,128)(2,1)S(1)}, bf16[272,128]{1,0:T(8,128)(2,1)S(1)}, u32[]{:S(2)}, u32[]{:S(2)}) collective-permute-start(bf16[272,128]{1,0:T(8,128)(2,1)S(1)} %get-tuple-element.50), channel_id=1, source_target_pairs={{0,5},{1,4},{2,7},{3,6},{4,1},{5,0},{6,3},{7,2},{8,13},{9,12},{10,... | collective-permute-start | bytes 208904 | tf_op jit(solution)/shard_map/ppermute | solution.py:530
  52.7 0.6 collective-permute-done.4
  53.5 1.3 %collective-permute-done.6 = bf16[272,128]{1,0:T(8,128)(2,1)S(1)} collective-permute-done((bf16[272,128]{1,0:T(8,128)(2,1)S(1)}, bf16[272,128]{1,0:T(8,128)(2,1)S(1)}, u32[]{:S(2)}, u32[]{:S(2)}) %collective-permute-start.6) | collective-permute-done | bytes 69664 | tf_op jit(solution)/shard_map/ppermute | solution.py:530
  55.0 4.2 %collective-permute-start.9 = (bf16[272,128]{1,0:T(8,128)(2,1)S(1)}, bf16[272,128]{1,0:T(8,128)(2,1)S(1)}, u32[]{:S(2)}, u32[]{:S(2)}) collective-permute-start(bf16[272,128]{1,0:T(8,128)(2,1)S(1)} %fusion.3), channel_id=1, source_target_pairs={{0,24},{1,25},{2,26},{3,27},{4,28},{5,29},{6,30},{7,31},{8,16},{9,... | collective-permute-start | bytes 208904 | tf_op jit(solution)/shard_map/ppermute | solution.py:530
  59.4 4.5 %collective-permute-done.8 = bf16[272,128]{1,0:T(8,128)(2,1)S(1)} collective-permute-done((bf16[272,128]{1,0:T(8,128)(2,1)S(1)}, bf16[272,128]{1,0:T(8,128)(2,1)S(1)}, u32[]{:S(2)}, u32[]{:S(2)}) %collective-permute-start.8) | collective-permute-done | bytes 69664 | tf_op jit(solution)/shard_map/ppermute | solution.py:530
  63.9 1.5 %collective-permute-start.10 = (bf16[272,128]{1,0:T(8,128)(2,1)S(1)}, bf16[272,128]{1,0:T(8,128)(2,1)S(1)}, u32[]{:S(2)}, u32[]{:S(2)}) collective-permute-start(bf16[272,128]{1,0:T(8,128)(2,1)S(1)} %add_convert_fusion), channel_id=1, source_target_pairs={{0,1},{1,0},{2,3},{3,2},{4,5},{5,4},{6,7},{7,6},{8,9},{9,8},{10,11... | collective-permute-start | bytes 208904 | tf_op jit(solution)/shard_map/ppermute | solution.py:530
  65.4 1.3 %collective-permute-start.11 = (bf16[272,128]{1,0:T(8,128)(2,1)S(1)}, bf16[272,128]{1,0:T(8,128)(2,1)S(1)}, u32[]{:S(2)}, u32[]{:S(2)}) collective-permute-start(bf16[272,128]{1,0:T(8,128)(2,1)S(1)} %add_convert_fusion), channel_id=1, source_target_pairs={{0,4},{1,5},{2,6},{3,7},{4,0},{5,1},{6,2},{7,3},{8,12},{9,13},{10,... | collective-permute-start | bytes 208904 | tf_op jit(solution)/shard_map/ppermute | solution.py:530
  66.7 0.8 %collective-permute-start.12 = (bf16[272,128]{1,0:T(8,128)(2,1)S(1)}, bf16[272,128]{1,0:T(8,128)(2,1)S(1)}, u32[]{:S(2)}, u32[]{:S(2)}) collective-permute-start(bf16[272,128]{1,0:T(8,128)(2,1)S(1)} %add_convert_fusion), channel_id=1, source_target_pairs={{0,5},{1,4},{2,7},{3,6},{4,1},{5,0},{6,3},{7,2},{8,13},{9,12},{10,... | collective-permute-start | bytes 208904 | tf_op jit(solution)/shard_map/ppermute | solution.py:530
  67.5 2.1 %shard_map.205 = bf16[45,24,128]{2,1,0:T(8,128)(2,1)} custom-call(bf16[52,32,128]{2,1,0:T(8,128)(2,1)S(1)} %pad.6.window, bf16[45,24,128]{2,1,0:T(8,128)(2,1)S(1)} %get-tuple-element.33.masked, bf16[49,128]{1,0:T(8,128)(2,1)S(1)} %squeeze.39.dw_in), custom_call_target="tpu_custom_call" | custom-call | flops 4000000000 | bytes 8000000 | tf_op jit(solution)/shard_map/pallas_call | solution.py:725
  69.6 0.9 %collective-permute-done.11 = bf16[272,128]{1,0:T(8,128)(2,1)S(1)} collective-permute-done((bf16[272,128]{1,0:T(8,128)(2,1)S(1)}, bf16[272,128]{1,0:T(8,128)(2,1)S(1)}, u32[]{:S(2)}, u32[]{:S(2)}) %collective-permute-start.11) | collective-permute-done | bytes 69664 | tf_op jit(solution)/shard_map/ppermute | solution.py:530
  70.5 1.4 %collective-permute-done.12 = bf16[272,128]{1,0:T(8,128)(2,1)S(1)} collective-permute-done((bf16[272,128]{1,0:T(8,128)(2,1)S(1)}, bf16[272,128]{1,0:T(8,128)(2,1)S(1)}, u32[]{:S(2)}, u32[]{:S(2)}) %collective-permute-start.12) | collective-permute-done | bytes 69664 | tf_op jit(solution)/shard_map/ppermute | solution.py:530
  72.1 1.5 %collective-permute-done.16.other = bf16[1088,128]{1,0:T(8,128)(2,1)S(1)} collective-permute-done((bf16[1088,128]{1,0:T(8,128)(2,1)S(1)}, bf16[1088,128]{1,0:T(8,128)(2,1)S(1)}, u32[]{:S(2)}, u32[]{:S(2)}) %collective-permute-start.16) | collective-permute-done | bytes 278560 | tf_op jit(solution)/shard_map/ppermute | solution.py:530
  73.7 1.1 %shard_map.206 = (f32[7,7,2,128]{3,2,1,0:T(2,128)}, f32[2,128]{1,0:T(2,128)}, f32[2,128]{1,0:T(2,128)}, f32[2,128]{1,0:T(2,128)}, f32[2,128,512]{2,1,0:T(8,128)}...) custom-call(s32[1]{0:T(128)} %bitcast.24.held, ...), custom_call_target="tpu_custom_call" | custom-call | tf_op jit(solution)/shard_map/pallas_call | solution.py:739
  (59 shorter events, 2.7 us)
Async XLA Ops:
  2.7 6.2 %collective-permute-start = (bf16[1,9,48,128]{3,2,1,0:T(8,128)(2,1)}, bf16[1,9,48,128]{3,2,1,0:T(8,128)(2,1)S(1)}, u32[]{:S(2)}, u32[]{:S(2)}) collective-permute-start(bf16[1,9,48,128]{3,2,1,0:T(8,128)(2,1)} %get-tuple-element.29), channel_id=1, source_target_pairs={{0,1},{1,0},{2,3},{3,2},{4,5},{5,4},{6,7},{7,6},{8,9},{9,8},{10,11... | collective-permute-start | bytes 331784 | tf_op jit(solution)/shard_map/ppermute | solution.py:530
  9.1 6.9 %collective-permute-start.2 = (bf16[54,15,128]{2,1,0:T(8,128)(2,1)S(1)}, bf16[54,15,128]{2,1,0:T(8,128)(2,1)S(1)}, u32[]{:S(2)}, u32[]{:S(2)}) collective-permute-start(bf16[54,15,128]{2,1,0:T(8,128)(2,1)S(1)} %maximum_select_fusion.2), channel_id=1, source_target_pairs={{0,30},{2,0},{4,2},{6,4},{8,6},{10,8},{12,10},{14,12},{16,14},{18,... | collective-permute-start | bytes 622088 | tf_op jit(solution)/shard_map/ppermute | solution.py:516
  12.5 8.2 %copy-start.2 = (bf16[2,128,512]{2,1,0:T(8,128)(2,1)S(1)}, bf16[2,128,512]{2,1,0:T(8,128)(2,1)}, u32[]{:S(2)}) copy-start(bf16[2,128,512]{2,1,0:T(8,128)(2,1)} %weight_in.1) | copy-start | bytes 786436
  12.5 8.2 %copy-start.3 = (bf16[2,512,128]{2,1,0:T(8,128)(2,1)S(1)}, bf16[2,512,128]{2,1,0:T(8,128)(2,1)}, u32[]{:S(2)}) copy-start(bf16[2,512,128]{2,1,0:T(8,128)(2,1)} %weight_out.1) | copy-start | bytes 786436
  12.6 8.1 %collective-permute-start.1 = (bf16[54,15,128]{2,1,0:T(8,128)(2,1)S(1)}, bf16[54,15,128]{2,1,0:T(8,128)(2,1)S(1)}, u32[]{:S(2)}, u32[]{:S(2)}) collective-permute-start(bf16[54,15,128]{2,1,0:T(8,128)(2,1)S(1)} %maximum_select_fusion.1), channel_id=1, source_target_pairs={{0,2},{2,4},{4,6},{6,8},{8,10},{10,12},{12,14},{14,16},{16,18},{18... | collective-permute-start | bytes 622088 | tf_op jit(solution)/shard_map/ppermute | solution.py:516
  13.4 7.3 %copy-start.7 = (f32[2,128]{1,0:T(2,128)S(1)}, f32[2,128]{1,0:T(2,128)}, u32[]{:S(2)}) copy-start(f32[2,128]{1,0:T(2,128)} %norm_bias.1) | copy-start | bytes 3076
  13.4 7.3 %copy-start.8 = (f32[2,128]{1,0:T(2,128)S(1)}, f32[2,128]{1,0:T(2,128)}, u32[]{:S(2)}) copy-start(f32[2,128]{1,0:T(2,128)} %bias_out.1) | copy-start | bytes 3076
  13.4 7.3 %copy-start.9 = (f32[2,128]{1,0:T(2,128)S(1)}, f32[2,128]{1,0:T(2,128)}, u32[]{:S(2)}) copy-start(f32[2,128]{1,0:T(2,128)} %layer_scale.1) | copy-start | bytes 3076
  13.4 7.3 %copy-start.4 = (f32[2,512]{1,0:T(2,128)S(1)}, f32[2,512]{1,0:T(2,128)}, u32[]{:S(2)}) copy-start(f32[2,512]{1,0:T(2,128)} %bias_in.1) | copy-start | bytes 12292
  13.4 7.3 %copy-start.5 = (f32[2,128]{1,0:T(2,128)S(1)}, f32[2,128]{1,0:T(2,128)}, u32[]{:S(2)}) copy-start(f32[2,128]{1,0:T(2,128)} %conv_bias.1) | copy-start | bytes 3076
  40.5 8.3 %collective-permute-start.3 = (bf16[1088,128]{1,0:T(8,128)(2,1)S(1)}, bf16[1088,128]{1,0:T(8,128)(2,1)S(1)}, u32[]{:S(2)}, u32[]{:S(2)}) collective-permute-start(bf16[1088,128]{1,0:T(8,128)(2,1)S(1)} %dynamic-slice_bitcast_fusion), channel_id=1, source_target_pairs={{0,2},{1,3},{2,0},{3,1},{4,6},{5,7},{6,4},{7,5},{8,10},{9,11},{10,... | collective-permute-start | bytes 835592 | tf_op jit(solution)/shard_map/ppermute | solution.py:530
  40.6 6.2 %collective-permute-start.13 = (bf16[45,3,128]{2,1,0:T(4,128)(2,1)S(1)}, bf16[45,3,128]{2,1,0:T(4,128)(2,1)S(1)}, u32[]{:S(2)}, u32[]{:S(2)}) collective-permute-start(bf16[45,3,128]{2,1,0:T(4,128)(2,1)S(1)} %get-tuple-element.52), channel_id=1, source_target_pairs={{0,2},{2,4},{4,6},{6,8},{8,10},{10,12},{12,14},{14,16},{16,18},{18... | collective-permute-start | bytes 103688 | tf_op jit(solution)/shard_map/ppermute | solution.py:516
  41.2 5.7 %collective-permute-start.14 = (bf16[45,3,128]{2,1,0:T(4,128)(2,1)S(1)}, bf16[45,3,128]{2,1,0:T(4,128)(2,1)S(1)}, u32[]{:S(2)}, u32[]{:S(2)}) collective-permute-start(bf16[45,3,128]{2,1,0:T(4,128)(2,1)S(1)} %get-tuple-element.53), channel_id=1, source_target_pairs={{0,30},{2,0},{4,2},{6,4},{8,6},{10,8},{12,10},{14,12},{16,14},{18,... | collective-permute-start | bytes 103688 | tf_op jit(solution)/shard_map/ppermute | solution.py:516
  46.9 5.6 %collective-permute-start.15 = (bf16[3,30,128]{2,1,0:T(8,128)(2,1)S(1)}, bf16[3,30,128]{2,1,0:T(8,128)(2,1)S(1)}, u32[]{:S(2)}, u32[]{:S(2)}) collective-permute-start(bf16[3,30,128]{2,1,0:T(8,128)(2,1)S(1)} %fusion.4), channel_id=1, source_target_pairs={{0,1},{1,0},{2,3},{3,2},{4,5},{5,4},{6,7},{7,6},{8,9},{9,8},{10,11... | collective-permute-start | bytes 69128 | tf_op jit(solution)/shard_map/ppermute | solution.py:536
  48.9 4.4 %collective-permute-start.4 = (bf16[272,128]{1,0:T(8,128)(2,1)S(1)}, bf16[272,128]{1,0:T(8,128)(2,1)S(1)}, u32[]{:S(2)}, u32[]{:S(2)}) collective-permute-start(bf16[272,128]{1,0:T(8,128)(2,1)S(1)} %get-tuple-element.49), channel_id=1, source_target_pairs={{0,1},{1,0},{2,3},{3,2},{4,5},{5,4},{6,7},{7,6},{8,9},{9,8},{10,11... | collective-permute-start | bytes 208904 | tf_op jit(solution)/shard_map/ppermute | solution.py:530
  49.2 4.3 %collective-permute-start.5 = (bf16[272,128]{1,0:T(8,128)(2,1)S(1)}, bf16[272,128]{1,0:T(8,128)(2,1)S(1)}, u32[]{:S(2)}, u32[]{:S(2)}) collective-permute-start(bf16[272,128]{1,0:T(8,128)(2,1)S(1)} %get-tuple-element.51), channel_id=1, source_target_pairs={{0,4},{1,5},{2,6},{3,7},{4,0},{5,1},{6,2},{7,3},{8,12},{9,13},{10,... | collective-permute-start | bytes 208904 | tf_op jit(solution)/shard_map/ppermute | solution.py:530
  49.2 5.6 %collective-permute-start.6 = (bf16[272,128]{1,0:T(8,128)(2,1)S(1)}, bf16[272,128]{1,0:T(8,128)(2,1)S(1)}, u32[]{:S(2)}, u32[]{:S(2)}) collective-permute-start(bf16[272,128]{1,0:T(8,128)(2,1)S(1)} %get-tuple-element.50), channel_id=1, source_target_pairs={{0,5},{1,4},{2,7},{3,6},{4,1},{5,0},{6,3},{7,2},{8,13},{9,12},{10,... | collective-permute-start | bytes 208904 | tf_op jit(solution)/shard_map/ppermute | solution.py:530
  54.8 4.6 %collective-permute-start.7 = (bf16[272,128]{1,0:T(8,128)(2,1)S(1)}, bf16[272,128]{1,0:T(8,128)(2,1)S(1)}, u32[]{:S(2)}, u32[]{:S(2)}) collective-permute-start(bf16[272,128]{1,0:T(8,128)(2,1)S(1)} %fusion.3), channel_id=1, source_target_pairs={{0,8},{1,9},{2,10},{3,11},{4,12},{5,13},{6,14},{7,15},{8,0},{9,1},... | collective-permute-start | bytes 208904 | tf_op jit(solution)/shard_map/ppermute | solution.py:530
  54.9 9.0 %collective-permute-start.8 = (bf16[272,128]{1,0:T(8,128)(2,1)S(1)}, bf16[272,128]{1,0:T(8,128)(2,1)S(1)}, u32[]{:S(2)}, u32[]{:S(2)}) collective-permute-start(bf16[272,128]{1,0:T(8,128)(2,1)S(1)} %fusion.3), channel_id=1, source_target_pairs={{0,16},{1,17},{2,18},{3,19},{4,20},{5,21},{6,22},{7,23},{8,24},{9,... | collective-permute-start | bytes 208904 | tf_op jit(solution)/shard_map/ppermute | solution.py:530
  55.0 8.9 %collective-permute-start.9 = (bf16[272,128]{1,0:T(8,128)(2,1)S(1)}, bf16[272,128]{1,0:T(8,128)(2,1)S(1)}, u32[]{:S(2)}, u32[]{:S(2)}) collective-permute-start(bf16[272,128]{1,0:T(8,128)(2,1)S(1)} %fusion.3), channel_id=1, source_target_pairs={{0,24},{1,25},{2,26},{3,27},{4,28},{5,29},{6,30},{7,31},{8,16},{9,... | collective-permute-start | bytes 208904 | tf_op jit(solution)/shard_map/ppermute | solution.py:530
  63.9 5.7 %collective-permute-start.10 = (bf16[272,128]{1,0:T(8,128)(2,1)S(1)}, bf16[272,128]{1,0:T(8,128)(2,1)S(1)}, u32[]{:S(2)}, u32[]{:S(2)}) collective-permute-start(bf16[272,128]{1,0:T(8,128)(2,1)S(1)} %add_convert_fusion), channel_id=1, source_target_pairs={{0,1},{1,0},{2,3},{3,2},{4,5},{5,4},{6,7},{7,6},{8,9},{9,8},{10,11... | collective-permute-start | bytes 208904 | tf_op jit(solution)/shard_map/ppermute | solution.py:530
  65.4 5.1 %collective-permute-start.11 = (bf16[272,128]{1,0:T(8,128)(2,1)S(1)}, bf16[272,128]{1,0:T(8,128)(2,1)S(1)}, u32[]{:S(2)}, u32[]{:S(2)}) collective-permute-start(bf16[272,128]{1,0:T(8,128)(2,1)S(1)} %add_convert_fusion), channel_id=1, source_target_pairs={{0,4},{1,5},{2,6},{3,7},{4,0},{5,1},{6,2},{7,3},{8,12},{9,13},{10,... | collective-permute-start | bytes 208904 | tf_op jit(solution)/shard_map/ppermute | solution.py:530
  66.7 5.2 %collective-permute-start.12 = (bf16[272,128]{1,0:T(8,128)(2,1)S(1)}, bf16[272,128]{1,0:T(8,128)(2,1)S(1)}, u32[]{:S(2)}, u32[]{:S(2)}) collective-permute-start(bf16[272,128]{1,0:T(8,128)(2,1)S(1)} %add_convert_fusion), channel_id=1, source_target_pairs={{0,5},{1,4},{2,7},{3,6},{4,1},{5,0},{6,3},{7,2},{8,13},{9,12},{10,... | collective-permute-start | bytes 208904 | tf_op jit(solution)/shard_map/ppermute | solution.py:530
  72.0 1.6 %collective-permute-start.16 = (bf16[1088,128]{1,0:T(8,128)(2,1)S(1)}, bf16[1088,128]{1,0:T(8,128)(2,1)S(1)}, u32[]{:S(2)}, u32[]{:S(2)}) collective-permute-start(bf16[1088,128]{1,0:T(8,128)(2,1)S(1)} %pad_maximum_fusion.1.own), channel_id=1, source_target_pairs={{0,2},{1,3},{2,0},{3,1},{4,6},{5,7},{6,4},{7,5},{8,10},{9,11},{10,... | collective-permute-start | bytes 835592 | tf_op jit(solution)/shard_map/ppermute | solution.py:530
  (4 other events, 16.1 us)

commit v5 on v4

--- a/solution.py
+++ b/solution.py
@@ -160,14 +160,83 @@
                 out[pl.ds(tap_row * KSIZE + tap_col, 1), :] = total
 
 
+def fill_windows(sizes, starts, sources, state, coded, edges):
+    height, breadth, window_rows = sizes
+    state_tile, cotangent, land_sea, lat_pieces, within, across = sources
+    channels = state.shape[2]
+    pad = MARGIN
+    own = pad + starts[0]
+    lower = starts[3] == 0
+    state[pl.ds(pad, window_rows)] = jnp.zeros((window_rows,) + state.shape[1:], F32)
+    coded[pl.ds(pad, window_rows)] = jnp.zeros((window_rows,) + coded.shape[1:], F32)
+
+    def spread(marks, column):
+        return jnp.broadcast_to(marks[:, column : column + 1], (marks.shape[0], channels))
+
+    state[pl.ds(own, height), pl.ds(STATE_AT, breadth), :] = state_tile[...].astype(F32)
+    ocean = jnp.where(land_sea[...] != 0, 1.0, 0.0).astype(F32)
+    for row in range(height):
+        value = jnp.where(spread(ocean, row) > 0.5, cotangent[row].astype(F32), LAND)
+        coded[own + row, pl.ds(FIELD_AT, breadth), :] = value
+
+    sides = lat_pieces.shape[0]
+    far, near = WIDE * breadth, MARGIN * breadth
+    for side in range(sides):
+        first = pad + starts[4 + side]
+        closest = pad + starts[4 + sides + side]
+        piece = lat_pieces[side].astype(F32)
+        marks = piece[far + near : far + near + breadth]
+        for row in range(WIDE):
+            spots = pl.ds(row * breadth, breadth)
+            state[first + row, pl.ds(STATE_AT, breadth), :] = lat_pieces[side, spots].astype(F32)
+            value = jnp.where(spread(marks, row) > 0.5, 0.0, LAND)
+            coded[first + row, pl.ds(FIELD_AT, breadth), :] = value
+        for row in range(MARGIN):
+            value = piece[far + row * breadth : far + (row + 1) * breadth]
+            old = coded[closest + row, pl.ds(FIELD_AT, breadth), :]
+            value = jnp.where(old > LAND_BOUND, LAND, value)
+            coded[closest + row, pl.ds(FIELD_AT, breadth), :] = value
+
+    group = WIDE + MARGIN
+
+    def fill_columns(source, west):
+        edges[...] = source[...].astype(F32)
+        state_at = STATE_AT - WIDE if west else STATE_AT + breadth
+        mark_at = FIELD_AT - NARROW if west else FIELD_AT + breadth
+        value_at = FIELD_AT - MARGIN if west else FIELD_AT + breadth
+        shown = slice(NARROW - MARGIN, NARROW) if west else slice(0, MARGIN)
+        spans = [(own - pad, height, 0)] + [(starts[4 + side], WIDE, side + 1) for side in range(sides)]
+        for first, count, place in spans:
+            marks = edges[pl.ds(window_rows * group + place * 8, 8), :]
+            for row in range(count):
+                at = pad + first + row
+                lines = (first + row) * group
+                state[at, pl.ds(state_at, WIDE), :] = edges[pl.ds(lines, WIDE), :]
+                mark = spread(marks, row)[:NARROW]
+                coded[at, pl.ds(mark_at, NARROW), :] = jnp.where(mark > 0.5, 0.0, LAND)
+                value = jnp.where(mark[shown] > 0.5, edges[pl.ds(lines + WIDE, MARGIN), :], LAND)
+                coded[at, pl.ds(value_at, MARGIN), :] = value
+
+    @pl.when(lower)
+    def _():
+        fill_columns(across, True)
+        fill_columns(within, False)
+
+    @pl.when(jnp.logical_not(lower))
+    def _():
+        fill_columns(within, True)
+        fill_columns(across, False)
+
+
 def tile_kernel(
     sizes,
     starts,
     state_tile,
-    coded_tile,
+    cotangent,
+    land_sea,
     lat_pieces,
-    west,
-    east,
+    within,
+    across,
     dw_in,
     conv_bias,
     norm_gain,
@@ -180,6 +249,7 @@
     output,
     mixed_out,
     masked_out,
+    edges_out,
     grads_out,
     state,
     coded,
@@ -203,6 +273,8 @@
     sums,
     hidden_sums,
     taps,
+    edges,
+    mixed_edges,
 ):
     height, breadth, first_rows, second_rows, window_rows = sizes
     channels = state.shape[2]
@@ -220,20 +292,14 @@
     state[pl.ds(pad, window_rows)] = jnp.zeros((window_rows,) + state.shape[1:], F32)
     coded[pl.ds(pad, window_rows)] = jnp.zeros((window_rows,) + coded.shape[1:], F32)
 
-    def place(window, at, values):
-        window[at[0], pl.ds(at[1], values.shape[1]), :] = values.astype(F32)
-
-    place(state, (pl.ds(pad + own_start, height), STATE_AT), state_tile[...])
-    place(coded, (pl.ds(pad + own_start, height), FIELD_AT), coded_tile[...])
-    for index in range(lat_pieces.shape[0]):
-        spots = pl.ds(pad + starts[3 + index], WIDE)
-        place(state, (spots, STATE_AT), lat_pieces[index, :, :breadth])
-        place(coded, (spots, FIELD_AT), lat_pieces[index, :, breadth:])
-    spots = pl.ds(pad, window_rows)
-    place(state, (spots, STATE_AT - WIDE), west[:, :WIDE])
-    place(state, (spots, STATE_AT + breadth), east[:, :WIDE])
-    place(coded, (spots, FIELD_AT - NARROW), west[:, WIDE:])
-    place(coded, (spots, FIELD_AT + breadth), east[:, WIDE:])
+    fill_windows(
+        (height, breadth, window_rows),
+        starts,
+        (state_tile, cotangent, land_sea, lat_pieces, within, across),
+        state,
+        coded,
+        edges,
+    )
     kernels[...] = dw_in[...].astype(F32)
     sums[...] = jnp.zeros_like(sums)
     hidden_sums[...] = jnp.zeros_like(hidden_sums)
@@ -371,6 +437,16 @@
         return carry
 
     lax.fori_loop(0, height // back_step, backward_first, 0)
+
+    mixed_edges[...] = jnp.zeros_like(mixed_edges)
+    lower = starts[3] == 0
+    for row in range(height):
+        first = mixed_own[row, pl.ds(0, MARGIN), :]
+        last = mixed_own[row, pl.ds(breadth - MARGIN, MARGIN), :]
+        spots = pl.ds(row * MARGIN, MARGIN)
+        mixed_edges[0, spots] = jnp.where(lower, last, first)
+        mixed_edges[1, spots] = jnp.where(lower, first, last)
+    edges_out[...] = mixed_edges[...].astype(BF16)
 
     hidden_units = weight_in.shape[2]
     groups = hidden_units // channels
@@ -444,10 +520,41 @@
         grads_out[pl.ds(at, small), :] = taps[pl.ds(layer * small, small), :].astype(BF16)
 
 
-def state_kernel(window, masked, dw_in, out, wide, kernels):
+def state_kernel(starts, mixed, within, across, lat_pieces, masked, dw_in, out, wide, kernels, edges):
     height, breadth, channels = masked.shape
-    wide[...] = window[...].astype(F32)
+    wide[...] = jnp.zeros_like(wide)
     kernels[...] = dw_in[...].astype(F32)
+    wide[pl.ds(MARGIN, height), pl.ds(MARGIN, breadth), :] = mixed[...].astype(F32)
+    sides = lat_pieces.shape[0]
+    inner = MARGIN * breadth
+    beside = MARGIN * MARGIN
+    for side in range(sides):
+        first = starts[1 + side]
+        piece = lat_pieces[side].astype(F32)
+        for row in range(MARGIN):
+            spots = slice(row * breadth, (row + 1) * breadth)
+            wide[first + row, pl.ds(MARGIN, breadth), :] = piece[spots]
+
+    def fill_columns(source, place, west):
+        column = 0 if west else MARGIN + breadth
+        edges[...] = source[...].astype(F32)
+        for row in range(height):
+            wide[MARGIN + row, pl.ds(column, MARGIN), :] = edges[pl.ds(row * MARGIN, MARGIN), :]
+        for side in range(sides):
+            piece = lat_pieces[side].astype(F32)
+            for row in range(MARGIN):
+                at = inner + place * beside + row * MARGIN
+                wide[starts[1 + side] + row, pl.ds(column, MARGIN), :] = piece[at : at + MARGIN]
+
+    @pl.when(starts[0] == 0)
+    def _():
+        fill_columns(within, 0, False)
+        fill_columns(across, 1, True)
+
+    @pl.when(starts[0] != 0)
+    def _():
+        fill_columns(within, 0, True)
+        fill_columns(across, 1, False)
 
     rows = divisor(height, BACK_STEP)
 
@@ -460,18 +567,6 @@
         return carry
 
     lax.fori_loop(0, height // rows, advance, 0)
-
-
-def code_kernel(lat, state, land_sea, cotangent, coded, edge):
-    height, breadth, channels = state.shape
-    ocean = jnp.where(land_sea[...] != 0, 1.0, 0.0).astype(F32)
-    for row in range(height):
-        wide = jnp.broadcast_to(ocean[:, row : row + 1], (breadth, channels))
-        coded[row] = jnp.where(wide > 0.5, cotangent[row].astype(F32), LAND).astype(BF16)
-    for side in range(edge.shape[0]):
-        first = (1 - lat[0]) * (height - WIDE) if edge.shape[0] == 1 else (1 - side) * (height - WIDE)
-        edge[side, :, :breadth] = state[pl.ds(first, WIDE)]
-        edge[side, :, breadth:] = coded[pl.ds(first, WIDE)]
 
 
 def gradient_kernel(grad_norm, held, own, other, *outs):
@@ -511,15 +606,23 @@
         self.lat = mesh.shape["lat"]
         self.axes = ("lon", "lat")
 
-    def shift_lon(self, values, by):
-        pairs = [(place, (place + by) % self.lon) for place in range(self.lon)]
-        return lax.ppermute(values, "lon", pairs)
+    def lon_neighbours(self, within, across):
+        there = [place + 1 if place % 2 else place - 1 for place in range(self.lon)]
+        pairs = [(place, other % self.lon) for place, other in enumerate(there)]
+        across = lax.ppermute(across, "lon", pairs)
+        return self.swap(within, 1, 0), across
 
     def shift_lat(self, values, by):
         pairs = [
             (place, place + by) for place in range(self.lat) if 0 <= place + by < self.lat
         ]
         return lax.ppermute(values, "lat", pairs)
+
+    def lat_neighbours(self, last, first):
+        if self.lat == 2:
+            mine = jnp.where(lax.axis_index("lat") == 0, last, first)
+            return self.swap(mine, 0, 1)[None]
+        return jnp.stack([self.shift_lat(last, 1), self.shift_lat(first, -1)])
 
     def swap(self, values, lon_bits, lat_bits):
         pairs = []
@@ -528,20 +631,6 @@
                 there = (lon ^ lon_bits) * self.lat + (lat ^ lat_bits)
                 pairs.append((lon * self.lat + lat, there))
         return lax.ppermute(values, self.axes, pairs)
-
-    def extend_lat(self, field, width, outside):
-        place = lax.axis_index("lat")
-        if self.lat == 2:
-            mine = jnp.where(place == 0, field[-width:], field[:width])
-            other = lax.ppermute(mine, "lat", [(0, 1), (1, 0)])
-            below = jnp.concatenate([field, other], axis=0)
-            above = jnp.concatenate([other, field], axis=0)
-            return jnp.where(place == 0, below, above)
-        before = self.shift_lat(field[-width:], 1)
-        after = self.shift_lat(field[:width], -1)
-        before = jnp.where(place == 0, outside, before)
-        after = jnp.where(place == self.lat - 1, outside, after)
-        return jnp.concatenate([before, field, after], axis=0)
 
     def sum_all(self, rows, beside):
         lon = lax.axis_index("lon")
@@ -615,47 +704,72 @@
         skipped = WIDE - margin
         return lat * skipped if sides == 1 else jnp.int32(skipped)
 
+    core = lax.axis_index("lon") % 2
     vmem = pl.BlockSpec(memory_space=pltpu.VMEM)
     smem = pl.BlockSpec(memory_space=pltpu.SMEM)
     tile = (height, breadth, channels)
-    coded, edges = pl.pallas_call(
-        code_kernel,
-        out_shape=(
-            jax.ShapeDtypeStruct(tile, BF16),
-            jax.ShapeDtypeStruct((sides, WIDE, 2 * breadth, channels), BF16),
-        ),
-        in_specs=[smem, vmem, vmem, vmem],
-        out_specs=(vmem, vmem),
-    )(lat.reshape(1), state, land_sea.T, cotangent)
+
+    def flat(values):
+        return values.reshape(-1, channels)
+
+    def whole_rows(values, rows):
+        return jnp.pad(values, ((0, rows - values.shape[0]), (0, channels - values.shape[1])))
+
+    land = land_sea.T
+    marks = (land != 0).astype(BF16)
+
+    def lat_rows(far, near):
+        return jnp.concatenate(
+            [flat(state[far]), flat(cotangent[near]), whole_rows(marks[:, far], breadth)]
+        )
+
+    pieces = links.lat_neighbours(
+        lat_rows(slice(height - WIDE, height), slice(height - MARGIN, height)),
+        lat_rows(slice(0, WIDE), slice(0, MARGIN)),
+    )
+    far, near = WIDE * breadth, MARGIN * breadth
+    piece_states = pieces[:, :far].reshape(sides, WIDE, breadth, channels)
+    piece_cotangents = pieces[:, far : far + near].reshape(sides, MARGIN, breadth, channels)
+    piece_marks = pieces[:, far + near :]
+
+    def lon_columns(wide, narrow, margin):
+        own = jnp.concatenate([state[:, wide], cotangent[:, margin]], axis=1)
+
+        def ends(side, above):
+            empty = ((NARROW, 0) if above else (0, NARROW), (0, 0), (0, 0))
+            near_rows = jnp.pad(piece_cotangents[side][:, margin], empty)
+            return jnp.concatenate([piece_states[side][:, wide], near_rows], axis=1)
+
+        if sides == 1:
+            rows = jnp.where(
+                lat == 0,
+                jnp.concatenate([own, ends(0, False)]),
+                jnp.concatenate([ends(0, True), own]),
+            )
+        else:
+            rows = jnp.concatenate([ends(0, True), own, ends(1, False)])
+        kept = [whole_rows(marks[narrow], 8)]
+        kept += [jnp.pad(piece_marks[side][narrow], ((0, 8 - NARROW), (0, 0))) for side in range(sides)]
+        return jnp.concatenate([flat(rows), *kept])
+
+    first_columns = lon_columns(slice(0, WIDE), slice(0, NARROW), slice(0, MARGIN))
+    last_columns = lon_columns(
+        slice(breadth - WIDE, breadth),
+        slice(breadth - NARROW, breadth),
+        slice(breadth - MARGIN, breadth),
+    )
+    within, across = links.lon_neighbours(
+        jnp.where(core == 0, last_columns, first_columns),
+        jnp.where(core == 0, first_columns, last_columns),
+    )
     if sides == 1:
-        pieces = links.swap(edges, 0, 1)
         places = [(1 - lat) * height]
+        closest = [jnp.where(lat == 0, height, WIDE - MARGIN)]
     else:
-        outside = jnp.concatenate(
-            [jnp.zeros((1, breadth, 1), BF16), jnp.full((1, breadth, 1), LAND, BF16)], axis=1
-        )
-        above = jnp.where(lat == 0, outside, links.shift_lat(edges[0], 1))
-        below = jnp.where(lat == links.lat - 1, outside, links.shift_lat(edges[1], -1))
-        pieces = jnp.stack([above, below])
-        places = [jnp.int32(0), jnp.int32(WIDE + height)]
-
-    def edge(tile_cols):
-        own = jnp.concatenate([state[:, tile_cols[0]], coded[:, tile_cols[1]]], axis=1)
-        ends = [
-            jnp.concatenate(
-                [piece[:, :breadth][:, tile_cols[0]], piece[:, breadth:][:, tile_cols[1]]], axis=1
-            )
-            for piece in pieces
-        ]
-        if sides == 2:
-            return jnp.concatenate([ends[0], own, ends[1]], axis=0)
-        after = jnp.concatenate([own, ends[0]], axis=0)
-        before = jnp.concatenate([ends[0], own], axis=0)
-        return jnp.where(lat == 0, after, before)
-
-    west = links.shift_lon(edge((slice(-WIDE, None), slice(-NARROW, None))), 1)
-    east = links.shift_lon(edge((slice(WIDE), slice(NARROW))), -1)
-    starts = jnp.stack([start(0), start(MARGIN), start(NARROW), *places]).astype(jnp.int32)
+        places = [0, WIDE + height]
+        closest = [WIDE - MARGIN, WIDE + height]
+    starts = [start(0), start(MARGIN), start(NARROW), core, *places, *closest]
+    starts = jnp.stack([jnp.asarray(entry, jnp.int32) for entry in starts])
     state_pitch, field_pitch, inner_pitch = (
         round_up(breadth + size, 8) for size in (STATE_AT + WIDE, FIELD_AT + NARROW, NARROW)
     )
@@ -666,6 +780,7 @@
     small_rows = BLOCKS * (layer_rows - 2 * hidden_units)
     grad_rows = BLOCKS * layer_rows
     own_rows = (window_rows, breadth)
+    edge_rows = round_up(height * MARGIN, 8)
     scratch = [
         pltpu.VMEM((padded_rows, state_pitch, channels), F32),
         pltpu.VMEM((padded_rows, field_pitch, channels), F32),
@@ -689,19 +804,22 @@
         pltpu.VMEM((BLOCKS, 5, 8, channels), F32),
         pltpu.VMEM((BLOCKS, 8, hidden_units), F32),
         pltpu.VMEM((small_rows, channels), F32),
+        pltpu.VMEM(within.shape, F32),
+        pltpu.VMEM((2, edge_rows, channels), F32),
     ]
     sizes = (height, breadth, first_rows, second_rows, window_rows)
     taps_in = dw_kernel.reshape(BLOCKS, TAPS, channels)
-    output, grad_mixed, masked, grads = pl.pallas_call(
+    output, grad_mixed, masked, mixed_edges, grads = pl.pallas_call(
         functools.partial(tile_kernel, sizes),
         out_shape=(
             jax.ShapeDtypeStruct(tile, BF16),
             jax.ShapeDtypeStruct(tile, BF16),
             jax.ShapeDtypeStruct(tile, BF16),
+            jax.ShapeDtypeStruct((2, edge_rows, channels), BF16),
             jax.ShapeDtypeStruct((grad_rows, channels), BF16),
         ),
-        in_specs=[smem] + [vmem] * 14,
-        out_specs=(vmem,) * 4,
+        in_specs=[smem] + [vmem] * 15,
+        out_specs=(vmem,) * 5,
         scratch_shapes=scratch,
         compiler_params=pltpu.CompilerParams(vmem_limit_bytes=48 * 1024 * 1024),
         cost_estimate=pl.CostEstimate(
@@ -709,30 +827,41 @@
             bytes_accessed=4 * height * breadth * channels * 4,
             transcendentals=0,
         ),
-    )(starts, state, coded, pieces, west, east, taps_in, *params[1:])
-
-    before = links.shift_lon(grad_mixed[:, -MARGIN:], 1)
-    after = links.shift_lon(grad_mixed[:, :MARGIN], -1)
-    beside = jnp.concatenate([before, grad_mixed, after], axis=1)
-    spread = links.extend_lat(beside, MARGIN, jnp.zeros((1, 1, 1), BF16))
+    )(starts, state, cotangent, land, pieces, within, across, taps_in, *params[1:])
+
+    within, across = links.lon_neighbours(mixed_edges[0], mixed_edges[1])
+    corner = MARGIN * MARGIN
+
+    def corner_rows(rows, first):
+        beside = slice(first * MARGIN, first * MARGIN + corner)
+        parts = jnp.concatenate([flat(grad_mixed[rows]), within[beside], across[beside]])
+        return jnp.pad(parts, ((0, -parts.shape[0] % 16), (0, 0)))
+
+    pieces = links.lat_neighbours(
+        corner_rows(slice(height - MARGIN, height), height - MARGIN),
+        corner_rows(slice(0, MARGIN), 0),
+    )
     if sides == 1:
-        empty = jnp.zeros((MARGIN,) + spread.shape[1:], BF16)
-        first = jnp.concatenate([empty, spread], axis=0)
-        last = jnp.concatenate([spread, empty], axis=0)
-        spread = jnp.where(lat == 0, first, last)
-    pitch = round_up(spread.shape[1], 8)
-    spread = jnp.pad(spread, ((0, 1), (0, pitch - spread.shape[1]), (0, 0)))
+        places = [(1 - lat) * (MARGIN + height)]
+    else:
+        places = [0, MARGIN + height]
+    starts = jnp.stack([jnp.asarray(entry, jnp.int32) for entry in (core, *places)])
+    wide = (height + 2 * MARGIN + 1, round_up(breadth + 2 * MARGIN, 8), channels)
     grad_state = pl.pallas_call(
         state_kernel,
         out_shape=jax.ShapeDtypeStruct(tile, BF16),
-        in_specs=[vmem] * 3,
+        in_specs=[smem] + [vmem] * 6,
         out_specs=vmem,
-        scratch_shapes=[pltpu.VMEM(spread.shape, F32), pltpu.VMEM((TAPS, channels), F32)],
+        scratch_shapes=[
+            pltpu.VMEM(wide, F32),
+            pltpu.VMEM((TAPS, channels), F32),
+            pltpu.VMEM((edge_rows, channels), F32),
+        ],
         compiler_params=pltpu.CompilerParams(vmem_limit_bytes=16 * 1024 * 1024),
         cost_estimate=pl.CostEstimate(
             flops=4_000_000_000, bytes_accessed=8_000_000, transcendentals=0
         ),
-    )(spread, masked, taps_in[0])
+    )(starts, grad_mixed, within, across, pieces, masked, taps_in[0])
 
     held, own, other, grad_state = links.sum_all(grads, grad_state)
     shapes = [(KSIZE, KSIZE, BLOCKS, channels)] + [member.shape for member in params[1:]]

time: 74.9 us -> 69.3 us (0.925)
  waiting for transfers between devices: 22.3 us -> 16.8 us
  local copies, waits for them, and re-layouts: 1.16 us -> 2.32 us
  Pallas kernels: 25 us -> 24 us
  starting transfers between devices: 24.5 us -> 23.5 us
    ppermute x5 -> x2, waiting for transfers between devices: 8.74 us -> 5.65 us  [lon_neighbours(): across = lax.ppermute(across, 'lon', pairs)]
    ppermute x5 -> x2, starting transfers between devices: 9.87 us -> 6.93 us  [lon_neighbours(): across = lax.ppermute(across, 'lon', pairs)]
    ppermute x12 -> x15, waiting for transfers between devices: 13.6 us -> 11.2 us  [swap(): return lax.ppermute(values, self.axes, pairs)]
    pallas_call x1 -> x0, Pallas kernels: 2.05 us -> none  [on_device(): pl.pallas_call(code_kernel, out_shape=(jax.ShapeDtypeStruct(tile, BF16),...]
    ppermute x12 -> x15, starting transfers between devices: 14.6 us -> 16.5 us  [swap(): return lax.ppermute(values, self.axes, pairs)]
    slice x5 -> x14, local copies, waits for them, and re-layouts: 0.18 us -> 1.9 us  [the longest x1 0.85 us: lat_rows(): state[far]]
  transfers between devices with their start and end apart: 17 -> 17, of which waited for: 11 -> 9; matrix products, arithmetic and copies ran while one was open for 1% -> 1% of each run, Pallas kernels for 3% -> 4%
where the time goes in v5:
time: 69.3 us; the launch traced here: 69.1 us
  Pallas kernels  24 us (35%)
  starting transfers between devices  23.5 us (34%)
  waiting for transfers between devices  16.8 us (24%)
  local copies, waits for them, and re-layouts  2.32 us (3%)
  other arithmetic  1.37 us (2%)
  between operations  1.09 us (2%)
    pallas_call x1, Pallas kernels, on_device(): pl.pallas_call(functools.partial(tile_kernel, sizes), out_shape=(jax.Shap...  20.1 us
    ppermute x15, starting transfers between devices, swap(): return lax.ppermute(values, self.axes, pairs)  16.5 us
    ppermute x15, waiting for transfers between devices, swap(): return lax.ppermute(values, self.axes, pairs)  11.2 us
    ppermute x2, starting transfers between devices, lon_neighbours(): across = lax.ppermute(across, 'lon', pairs)  6.93 us
    ppermute x2, waiting for transfers between devices, lon_neighbours(): across = lax.ppermute(across, 'lon', pairs)  5.65 us
    pallas_call x1, Pallas kernels, on_device(): pl.pallas_call(state_kernel, out_shape=jax.ShapeDtypeStruct(tile, BF16),...  2.75 us
  transfers between devices with their start and end apart: 17, of which 9 were waited for; matrix products, arithmetic and copies ran while one was open for 1% of the time, Pallas kernels for 4%

profile of v5, /device:TPU:0, one launch (start us, length us, event | category | flops | bytes accessed | tf_op | source)
XLA Modules:
  0.0 69.1 jit_solution(15017924454719547420)
XLA Ops:
  1.4 0.8 %fusion.53 = (bf16[3,24,128]{2,1,0:T(8,128)(2,1)S(1)}, bf16[3,24,128]{2,1,0:T(8,128)(2,1)S(1)}) fusion(bf16[45,24,128]{2,1,0:T(8,128)(2,1)} %cotangent.1), kind=kLoop, calls=%fused_computation.83 | loop fusion | bytes 73728 | tf_op jit(solution)/shard_map/slice | solution.py:723
  2.2 0.9 %fusion.52 = (bf16[9,24,128]{2,1,0:T(8,128)(2,1)S(1)}, bf16[9,24,128]{2,1,0:T(8,128)(2,1)S(1)}) fusion(bf16[45,24,128]{2,1,0:T(8,128)(2,1)} %state_tile.1), kind=kLoop, calls=%fused_computation.82 | loop fusion | bytes 221184 | tf_op jit(solution)/shard_map/slice | solution.py:723
  3.1 3.0 %collective-permute-start = (bf16[312,128]{1,0:T(8,128)(2,1)S(1)}, bf16[312,128]{1,0:T(8,128)(2,1)S(1)}, u32[]{:S(2)}, u32[]{:S(2)}) collective-permute-start(bf16[312,128]{1,0:T(8,128)(2,1)S(1)} %fusion.36), channel_id=1, source_target_pairs={{0,1},{1,0},{2,3},{3,2},{4,5},{5,4},{6,7},{7,6},{8,9},{9,8},{10,11... | collective-permute-start | bytes 239624 | tf_op jit(solution)/shard_map/ppermute | solution.py:633
  6.3 2.2 %collective-permute-done = bf16[312,128]{1,0:T(8,128)(2,1)S(1)} collective-permute-done((bf16[312,128]{1,0:T(8,128)(2,1)S(1)}, bf16[312,128]{1,0:T(8,128)(2,1)S(1)}, u32[]{:S(2)}, u32[]{:S(2)}) %collective-permute-start) | collective-permute-done | bytes 79904 | tf_op jit(solution)/shard_map/ppermute | solution.py:633
  9.1 3.4 %collective-permute-start.2 = (bf16[664,128]{1,0:T(8,128)(2,1)S(1)}, bf16[664,128]{1,0:T(8,128)(2,1)S(1)}, u32[]{:S(2)}, u32[]{:S(2)}) collective-permute-start(bf16[664,128]{1,0:T(8,128)(2,1)S(1)} %get-tuple-element.43), channel_id=1, source_target_pairs={{0,30},{2,4},{4,2},{6,8},{8,6},{10,12},{12,10},{14,16},{16,14},{18... | collective-permute-start | bytes 509960 | tf_op jit(solution)/shard_map/ppermute | solution.py:612
  13.0 3.7 %collective-permute-done.2.across = bf16[664,128]{1,0:T(8,128)(2,1)S(1)} collective-permute-done((bf16[664,128]{1,0:T(8,128)(2,1)S(1)}, bf16[664,128]{1,0:T(8,128)(2,1)S(1)}, u32[]{:S(2)}, u32[]{:S(2)}) %collective-permute-start.2) | collective-permute-done | bytes 170016 | tf_op jit(solution)/shard_map/ppermute | solution.py:612
  16.7 20.1 %shard_map.203 = (bf16[45,24,128]{2,1,0:T(8,128)(2,1)}, bf16[45,24,128]{2,1,0:T(8,128)(2,1)S(1)}, bf16[45,24,128]{2,1,0:T(8,128)(2,1)S(1)}, bf16[2,136,128]{2,1,0:T(8,128)(2,1)S(1)}, bf16[2176,128]{1,0:T(8,128)(2,1)S(1)}) custom-call(s32[6]{0:T(128)S(1)} %stack.49.starts, bf16[45,24,128]{2,1,0:T(8,128)(2,1)S(1)} %copy-done, ...), custom_call_target="tpu_custom_call" | custom-call | flops 2013265920 | bytes 2211840 | tf_op jit(solution)/shard_map/pallas_call | solution.py:812
  36.9 3.5 %collective-permute-start.14 = (bf16[136,128]{1,0:T(8,128)(2,1)S(1)}, bf16[136,128]{1,0:T(8,128)(2,1)S(1)}, u32[]{:S(2)}, u32[]{:S(2)}) collective-permute-start(bf16[136,128]{1,0:T(8,128)(2,1)S(1)} %get-tuple-element.64), channel_id=1, source_target_pairs={{0,30},{2,4},{4,2},{6,8},{8,6},{10,12},{12,10},{14,16},{16,14},{18... | collective-permute-start | bytes 104456 | tf_op jit(solution)/shard_map/ppermute | solution.py:612
  40.9 2.0 %collective-permute-done.14.across = bf16[136,128]{1,0:T(8,128)(2,1)S(1)} collective-permute-done((bf16[136,128]{1,0:T(8,128)(2,1)S(1)}, bf16[136,128]{1,0:T(8,128)(2,1)S(1)}, u32[]{:S(2)}, u32[]{:S(2)}) %collective-permute-start.14) | collective-permute-done | bytes 34848 | tf_op jit(solution)/shard_map/ppermute | solution.py:612
  43.0 2.5 %collective-permute-start.4 = (bf16[272,128]{1,0:T(8,128)(2,1)S(1)}, bf16[272,128]{1,0:T(8,128)(2,1)S(1)}, u32[]{:S(2)}, u32[]{:S(2)}) collective-permute-start(bf16[272,128]{1,0:T(8,128)(2,1)S(1)} %get-tuple-element.49), channel_id=1, source_target_pairs={{0,1},{1,0},{2,3},{3,2},{4,5},{5,4},{6,7},{7,6},{8,9},{9,8},{10,11... | collective-permute-start | bytes 208904 | tf_op jit(solution)/shard_map/ppermute | solution.py:633
  45.5 1.5 %collective-permute-start.5 = (bf16[272,128]{1,0:T(8,128)(2,1)S(1)}, bf16[272,128]{1,0:T(8,128)(2,1)S(1)}, u32[]{:S(2)}, u32[]{:S(2)}) collective-permute-start(bf16[272,128]{1,0:T(8,128)(2,1)S(1)} %get-tuple-element.51), channel_id=1, source_target_pairs={{0,4},{1,5},{2,6},{3,7},{4,0},{5,1},{6,2},{7,3},{8,12},{9,13},{10,... | collective-permute-start | bytes 208904 | tf_op jit(solution)/shard_map/ppermute | solution.py:633
  47.1 0.7 %collective-permute-done.4 = bf16[272,128]{1,0:T(8,128)(2,1)S(1)} collective-permute-done((bf16[272,128]{1,0:T(8,128)(2,1)S(1)}, bf16[272,128]{1,0:T(8,128)(2,1)S(1)}, u32[]{:S(2)}, u32[]{:S(2)}) %collective-permute-start.4) | collective-permute-done | bytes 69664 | tf_op jit(solution)/shard_map/ppermute | solution.py:633
  47.8 2.9 %collective-permute-done.6 = bf16[272,128]{1,0:T(8,128)(2,1)S(1)} collective-permute-done((bf16[272,128]{1,0:T(8,128)(2,1)S(1)}, bf16[272,128]{1,0:T(8,128)(2,1)S(1)}, u32[]{:S(2)}, u32[]{:S(2)}) %collective-permute-start.6) | collective-permute-done | bytes 69664 | tf_op jit(solution)/shard_map/ppermute | solution.py:633
  50.8 2.2 %collective-permute-start.9 = (bf16[272,128]{1,0:T(8,128)(2,1)S(1)}, bf16[272,128]{1,0:T(8,128)(2,1)S(1)}, u32[]{:S(2)}, u32[]{:S(2)}) collective-permute-start(bf16[272,128]{1,0:T(8,128)(2,1)S(1)} %fusion.34), channel_id=1, source_target_pairs={{0,24},{1,25},{2,26},{3,27},{4,28},{5,29},{6,30},{7,31},{8,16},{9,... | collective-permute-start | bytes 208904 | tf_op jit(solution)/shard_map/ppermute | solution.py:633
  53.0 2.2 %collective-permute-start.7 = (bf16[272,128]{1,0:T(8,128)(2,1)S(1)}, bf16[272,128]{1,0:T(8,128)(2,1)S(1)}, u32[]{:S(2)}, u32[]{:S(2)}) collective-permute-start(bf16[272,128]{1,0:T(8,128)(2,1)S(1)} %fusion.34), channel_id=1, source_target_pairs={{0,8},{1,9},{2,10},{3,11},{4,12},{5,13},{6,14},{7,15},{8,0},{9,1},... | collective-permute-start | bytes 208904 | tf_op jit(solution)/shard_map/ppermute | solution.py:633
  55.3 0.9 %collective-permute-start.15 = (bf16[96,128]{1,0:T(8,128)(2,1)S(1)}, bf16[96,128]{1,0:T(8,128)(2,1)S(1)}, u32[]{:S(2)}, u32[]{:S(2)}) collective-permute-start(bf16[96,128]{1,0:T(8,128)(2,1)S(1)} %fusion.46), channel_id=1, source_target_pairs={{0,1},{1,0},{2,3},{3,2},{4,5},{5,4},{6,7},{7,6},{8,9},{9,8},{10,11... | collective-permute-start | bytes 73736 | tf_op jit(solution)/shard_map/ppermute | solution.py:633
  56.1 0.9 %collective-permute-done.9 = bf16[272,128]{1,0:T(8,128)(2,1)S(1)} collective-permute-done((bf16[272,128]{1,0:T(8,128)(2,1)S(1)}, bf16[272,128]{1,0:T(8,128)(2,1)S(1)}, u32[]{:S(2)}, u32[]{:S(2)}) %collective-permute-start.9) | collective-permute-done | bytes 69664 | tf_op jit(solution)/shard_map/ppermute | solution.py:633
  57.0 2.1 %collective-permute-done.8 = bf16[272,128]{1,0:T(8,128)(2,1)S(1)} collective-permute-done((bf16[272,128]{1,0:T(8,128)(2,1)S(1)}, bf16[272,128]{1,0:T(8,128)(2,1)S(1)}, u32[]{:S(2)}, u32[]{:S(2)}) %collective-permute-start.8) | collective-permute-done | bytes 69664 | tf_op jit(solution)/shard_map/ppermute | solution.py:633
  59.2 1.5 %collective-permute-start.12 = (bf16[272,128]{1,0:T(8,128)(2,1)S(1)}, bf16[272,128]{1,0:T(8,128)(2,1)S(1)}, u32[]{:S(2)}, u32[]{:S(2)}) collective-permute-start(bf16[272,128]{1,0:T(8,128)(2,1)S(1)} %add_convert_fusion), channel_id=1, source_target_pairs={{0,5},{1,4},{2,7},{3,6},{4,1},{5,0},{6,3},{7,2},{8,13},{9,12},{10,... | collective-permute-start | bytes 208904 | tf_op jit(solution)/shard_map/ppermute | solution.py:633
  60.7 1.2 %collective-permute-start.11 = (bf16[272,128]{1,0:T(8,128)(2,1)S(1)}, bf16[272,128]{1,0:T(8,128)(2,1)S(1)}, u32[]{:S(2)}, u32[]{:S(2)}) collective-permute-start(bf16[272,128]{1,0:T(8,128)(2,1)S(1)} %add_convert_fusion), channel_id=1, source_target_pairs={{0,4},{1,5},{2,6},{3,7},{4,0},{5,1},{6,2},{7,3},{8,12},{9,13},{10,... | collective-permute-start | bytes 208904 | tf_op jit(solution)/shard_map/ppermute | solution.py:633
  61.9 0.9 %collective-permute-start.10 = (bf16[272,128]{1,0:T(8,128)(2,1)S(1)}, bf16[272,128]{1,0:T(8,128)(2,1)S(1)}, u32[]{:S(2)}, u32[]{:S(2)}) collective-permute-start(bf16[272,128]{1,0:T(8,128)(2,1)S(1)} %add_convert_fusion), channel_id=1, source_target_pairs={{0,1},{1,0},{2,3},{3,2},{4,5},{5,4},{6,7},{7,6},{8,9},{9,8},{10,11... | collective-permute-start | bytes 208904 | tf_op jit(solution)/shard_map/ppermute | solution.py:633
  62.8 2.7 %shard_map.204 = bf16[45,24,128]{2,1,0:T(8,128)(2,1)} custom-call(s32[2]{0:T(128)S(1)} %pad_add_fusion.starts, bf16[45,24,128]{2,1,0:T(8,128)(2,1)S(1)} %get-tuple-element.29.mixed, bf16[136,128]{1,0:T(8,128)(2,1)S(1)} %collective-permute-done.13.within, bf16[136,128]{1,0:T(8,128)(2,1)S(1)} %collective-permute-done.14.across, ...), custom_call_target="tpu_custom_call" | custom-call | flops 4000000000 | bytes 8000000 | tf_op jit(solution)/shard_map/pallas_call | solution.py:850
  66.4 1.5 %collective-permute-done.16.other = bf16[1088,128]{1,0:T(8,128)(2,1)S(1)} collective-permute-done((bf16[1088,128]{1,0:T(8,128)(2,1)S(1)}, bf16[1088,128]{1,0:T(8,128)(2,1)S(1)}, u32[]{:S(2)}, u32[]{:S(2)}) %collective-permute-start.16) | collective-permute-done | bytes 278560 | tf_op jit(solution)/shard_map/ppermute | solution.py:633
  67.9 1.1 %shard_map.205 = (f32[7,7,2,128]{3,2,1,0:T(2,128)}, f32[2,128]{1,0:T(2,128)}, f32[2,128]{1,0:T(2,128)}, f32[2,128]{1,0:T(2,128)}, f32[2,128,512]{2,1,0:T(8,128)}...) custom-call(s32[1]{0:T(128)} %bitcast.3.held, ...), custom_call_target="tpu_custom_call" | custom-call | tf_op jit(solution)/shard_map/pallas_call | solution.py:868
  (72 shorter events, 3.3 us)
Async XLA Ops:
  1.4 4.7 %copy-start.1 = (bf16[45,24,128]{2,1,0:T(8,128)(2,1)S(1)}, bf16[45,24,128]{2,1,0:T(8,128)(2,1)}, u32[]{:S(2)}) copy-start(bf16[45,24,128]{2,1,0:T(8,128)(2,1)} %cotangent.1) | copy-start | bytes 829444
  3.1 5.4 %collective-permute-start = (bf16[312,128]{1,0:T(8,128)(2,1)S(1)}, bf16[312,128]{1,0:T(8,128)(2,1)S(1)}, u32[]{:S(2)}, u32[]{:S(2)}) collective-permute-start(bf16[312,128]{1,0:T(8,128)(2,1)S(1)} %fusion.36), channel_id=1, source_target_pairs={{0,1},{1,0},{2,3},{3,2},{4,5},{5,4},{6,7},{7,6},{8,9},{9,8},{10,11... | collective-permute-start | bytes 239624 | tf_op jit(solution)/shard_map/ppermute | solution.py:633
  9.0 7.7 %copy-start.3 = (bf16[2,128,512]{2,1,0:T(8,128)(2,1)S(1)}, bf16[2,128,512]{2,1,0:T(8,128)(2,1)}, u32[]{:S(2)}) copy-start(bf16[2,128,512]{2,1,0:T(8,128)(2,1)} %weight_in.1) | copy-start | bytes 786436
  9.0 7.7 %copy-start.4 = (bf16[2,512,128]{2,1,0:T(8,128)(2,1)S(1)}, bf16[2,512,128]{2,1,0:T(8,128)(2,1)}, u32[]{:S(2)}) copy-start(bf16[2,512,128]{2,1,0:T(8,128)(2,1)} %weight_out.1) | copy-start | bytes 786436
  9.1 7.6 %collective-permute-start.2 = (bf16[664,128]{1,0:T(8,128)(2,1)S(1)}, bf16[664,128]{1,0:T(8,128)(2,1)S(1)}, u32[]{:S(2)}, u32[]{:S(2)}) collective-permute-start(bf16[664,128]{1,0:T(8,128)(2,1)S(1)} %get-tuple-element.43), channel_id=1, source_target_pairs={{0,30},{2,4},{4,2},{6,8},{8,6},{10,12},{12,10},{14,16},{16,14},{18... | collective-permute-start | bytes 509960 | tf_op jit(solution)/shard_map/ppermute | solution.py:612
  12.5 4.1 %collective-permute-start.1 = (bf16[664,128]{1,0:T(8,128)(2,1)S(1)}, bf16[664,128]{1,0:T(8,128)(2,1)S(1)}, u32[]{:S(2)}, u32[]{:S(2)}) collective-permute-start(bf16[664,128]{1,0:T(8,128)(2,1)S(1)} %get-tuple-element.44), channel_id=1, source_target_pairs={{0,2},{1,3},{2,0},{3,1},{4,6},{5,7},{6,4},{7,5},{8,10},{9,11},{10,... | collective-permute-start | bytes 509960 | tf_op jit(solution)/shard_map/ppermute | solution.py:633
  12.7 3.9 %copy-start.2 = (s32[45,24]{0,1:T(8,128)S(1)}, s32[45,24]{0,1:T(8,128)}, u32[]{:S(2)}) copy-start(s32[45,24]{0,1:T(8,128)} %param.13) | copy-start | bytes 12964
  12.8 3.9 %copy-start.5 = (f32[2,512]{1,0:T(2,128)S(1)}, f32[2,512]{1,0:T(2,128)}, u32[]{:S(2)}) copy-start(f32[2,512]{1,0:T(2,128)} %bias_in.1) | copy-start | bytes 12292
  12.9 3.8 %copy-start.7 = (f32[2,128]{1,0:T(2,128)S(1)}, f32[2,128]{1,0:T(2,128)}, u32[]{:S(2)}) copy-start(f32[2,128]{1,0:T(2,128)} %norm_gain.1) | copy-start | bytes 3076
  12.9 3.8 %copy-start.8 = (f32[2,128]{1,0:T(2,128)S(1)}, f32[2,128]{1,0:T(2,128)}, u32[]{:S(2)}) copy-start(f32[2,128]{1,0:T(2,128)} %norm_bias.1) | copy-start | bytes 3076
  36.9 6.1 %collective-permute-start.14 = (bf16[136,128]{1,0:T(8,128)(2,1)S(1)}, bf16[136,128]{1,0:T(8,128)(2,1)S(1)}, u32[]{:S(2)}, u32[]{:S(2)}) collective-permute-start(bf16[136,128]{1,0:T(8,128)(2,1)S(1)} %get-tuple-element.64), channel_id=1, source_target_pairs={{0,30},{2,4},{4,2},{6,8},{8,6},{10,12},{12,10},{14,16},{16,14},{18... | collective-permute-start | bytes 104456 | tf_op jit(solution)/shard_map/ppermute | solution.py:612
  40.4 2.6 %collective-permute-start.3 = (bf16[1088,128]{1,0:T(8,128)(2,1)S(1)}, bf16[1088,128]{1,0:T(8,128)(2,1)S(1)}, u32[]{:S(2)}, u32[]{:S(2)}) collective-permute-start(bf16[1088,128]{1,0:T(8,128)(2,1)S(1)} %dynamic-slice_bitcast_fusion), channel_id=1, source_target_pairs={{0,2},{1,3},{2,0},{3,1},{4,6},{5,7},{6,4},{7,5},{8,10},{9,11},{10,... | collective-permute-start | bytes 835592 | tf_op jit(solution)/shard_map/ppermute | solution.py:633
  40.5 6.6 %collective-permute-start.13 = (bf16[136,128]{1,0:T(8,128)(2,1)S(1)}, bf16[136,128]{1,0:T(8,128)(2,1)S(1)}, u32[]{:S(2)}, u32[]{:S(2)}) collective-permute-start(bf16[136,128]{1,0:T(8,128)(2,1)S(1)} %get-tuple-element.65), channel_id=1, source_target_pairs={{0,2},{1,3},{2,0},{3,1},{4,6},{5,7},{6,4},{7,5},{8,10},{9,11},{10,... | collective-permute-start | bytes 104456 | tf_op jit(solution)/shard_map/ppermute | solution.py:633
  43.0 4.8 %collective-permute-start.4 = (bf16[272,128]{1,0:T(8,128)(2,1)S(1)}, bf16[272,128]{1,0:T(8,128)(2,1)S(1)}, u32[]{:S(2)}, u32[]{:S(2)}) collective-permute-start(bf16[272,128]{1,0:T(8,128)(2,1)S(1)} %get-tuple-element.49), channel_id=1, source_target_pairs={{0,1},{1,0},{2,3},{3,2},{4,5},{5,4},{6,7},{7,6},{8,9},{9,8},{10,11... | collective-permute-start | bytes 208904 | tf_op jit(solution)/shard_map/ppermute | solution.py:633
  45.5 5.2 %collective-permute-start.6 = (bf16[272,128]{1,0:T(8,128)(2,1)S(1)}, bf16[272,128]{1,0:T(8,128)(2,1)S(1)}, u32[]{:S(2)}, u32[]{:S(2)}) collective-permute-start(bf16[272,128]{1,0:T(8,128)(2,1)S(1)} %get-tuple-element.50), channel_id=1, source_target_pairs={{0,5},{1,4},{2,7},{3,6},{4,1},{5,0},{6,3},{7,2},{8,13},{9,12},{10,... | collective-permute-start | bytes 208904 | tf_op jit(solution)/shard_map/ppermute | solution.py:633
  45.5 5.2 %collective-permute-start.5 = (bf16[272,128]{1,0:T(8,128)(2,1)S(1)}, bf16[272,128]{1,0:T(8,128)(2,1)S(1)}, u32[]{:S(2)}, u32[]{:S(2)}) collective-permute-start(bf16[272,128]{1,0:T(8,128)(2,1)S(1)} %get-tuple-element.51), channel_id=1, source_target_pairs={{0,4},{1,5},{2,6},{3,7},{4,0},{5,1},{6,2},{7,3},{8,12},{9,13},{10,... | collective-permute-start | bytes 208904 | tf_op jit(solution)/shard_map/ppermute | solution.py:633
  50.8 6.3 %collective-permute-start.9 = (bf16[272,128]{1,0:T(8,128)(2,1)S(1)}, bf16[272,128]{1,0:T(8,128)(2,1)S(1)}, u32[]{:S(2)}, u32[]{:S(2)}) collective-permute-start(bf16[272,128]{1,0:T(8,128)(2,1)S(1)} %fusion.34), channel_id=1, source_target_pairs={{0,24},{1,25},{2,26},{3,27},{4,28},{5,29},{6,30},{7,31},{8,16},{9,... | collective-permute-start | bytes 208904 | tf_op jit(solution)/shard_map/ppermute | solution.py:633
  53.0 6.2 %collective-permute-start.8 = (bf16[272,128]{1,0:T(8,128)(2,1)S(1)}, bf16[272,128]{1,0:T(8,128)(2,1)S(1)}, u32[]{:S(2)}, u32[]{:S(2)}) collective-permute-start(bf16[272,128]{1,0:T(8,128)(2,1)S(1)} %fusion.34), channel_id=1, source_target_pairs={{0,16},{1,17},{2,18},{3,19},{4,20},{5,21},{6,22},{7,23},{8,24},{9,... | collective-permute-start | bytes 208904 | tf_op jit(solution)/shard_map/ppermute | solution.py:633
  53.0 6.2 %collective-permute-start.7 = (bf16[272,128]{1,0:T(8,128)(2,1)S(1)}, bf16[272,128]{1,0:T(8,128)(2,1)S(1)}, u32[]{:S(2)}, u32[]{:S(2)}) collective-permute-start(bf16[272,128]{1,0:T(8,128)(2,1)S(1)} %fusion.34), channel_id=1, source_target_pairs={{0,8},{1,9},{2,10},{3,11},{4,12},{5,13},{6,14},{7,15},{8,0},{9,1},... | collective-permute-start | bytes 208904 | tf_op jit(solution)/shard_map/ppermute | solution.py:633
  55.3 7.5 %collective-permute-start.15 = (bf16[96,128]{1,0:T(8,128)(2,1)S(1)}, bf16[96,128]{1,0:T(8,128)(2,1)S(1)}, u32[]{:S(2)}, u32[]{:S(2)}) collective-permute-start(bf16[96,128]{1,0:T(8,128)(2,1)S(1)} %fusion.46), channel_id=1, source_target_pairs={{0,1},{1,0},{2,3},{3,2},{4,5},{5,4},{6,7},{7,6},{8,9},{9,8},{10,11... | collective-permute-start | bytes 73736 | tf_op jit(solution)/shard_map/ppermute | solution.py:633
  59.2 6.3 %collective-permute-start.12 = (bf16[272,128]{1,0:T(8,128)(2,1)S(1)}, bf16[272,128]{1,0:T(8,128)(2,1)S(1)}, u32[]{:S(2)}, u32[]{:S(2)}) collective-permute-start(bf16[272,128]{1,0:T(8,128)(2,1)S(1)} %add_convert_fusion), channel_id=1, source_target_pairs={{0,5},{1,4},{2,7},{3,6},{4,1},{5,0},{6,3},{7,2},{8,13},{9,12},{10,... | collective-permute-start | bytes 208904 | tf_op jit(solution)/shard_map/ppermute | solution.py:633
  60.7 4.8 %collective-permute-start.11 = (bf16[272,128]{1,0:T(8,128)(2,1)S(1)}, bf16[272,128]{1,0:T(8,128)(2,1)S(1)}, u32[]{:S(2)}, u32[]{:S(2)}) collective-permute-start(bf16[272,128]{1,0:T(8,128)(2,1)S(1)} %add_convert_fusion), channel_id=1, source_target_pairs={{0,4},{1,5},{2,6},{3,7},{4,0},{5,1},{6,2},{7,3},{8,12},{9,13},{10,... | collective-permute-start | bytes 208904 | tf_op jit(solution)/shard_map/ppermute | solution.py:633
  61.9 4.3 %collective-permute-start.10 = (bf16[272,128]{1,0:T(8,128)(2,1)S(1)}, bf16[272,128]{1,0:T(8,128)(2,1)S(1)}, u32[]{:S(2)}, u32[]{:S(2)}) collective-permute-start(bf16[272,128]{1,0:T(8,128)(2,1)S(1)} %add_convert_fusion), channel_id=1, source_target_pairs={{0,1},{1,0},{2,3},{3,2},{4,5},{5,4},{6,7},{7,6},{8,9},{9,8},{10,11... | collective-permute-start | bytes 208904 | tf_op jit(solution)/shard_map/ppermute | solution.py:633
  66.3 1.6 %collective-permute-start.16 = (bf16[1088,128]{1,0:T(8,128)(2,1)S(1)}, bf16[1088,128]{1,0:T(8,128)(2,1)S(1)}, u32[]{:S(2)}, u32[]{:S(2)}) collective-permute-start(bf16[1088,128]{1,0:T(8,128)(2,1)S(1)} %pad_maximum_fusion.1.own), channel_id=1, source_target_pairs={{0,2},{1,3},{2,0},{3,1},{4,6},{5,7},{6,4},{7,5},{8,10},{9,11},{10,... | collective-permute-start | bytes 835592 | tf_op jit(solution)/shard_map/ppermute | solution.py:633
  (5 other events, 18.1 us)

commit v6 on v5

--- a/solution.py
+++ b/solution.py
@@ -158,6 +158,26 @@
             for tap_row in range(KSIZE):
                 total = jnp.sum(sums[place * KSIZE + tap_row], axis=0, keepdims=True)
                 out[pl.ds(tap_row * KSIZE + tap_col, 1), :] = total
+
+
+def pack_kernel(lat, state, cotangent, land_sea, out, rows):
+    height, breadth, channels = state.shape
+    sides = out.shape[0]
+    rows[...] = jnp.zeros_like(rows)
+    ocean = jnp.where(land_sea[...] != 0, 1.0, 0.0).astype(F32)
+    far, near = WIDE * breadth, MARGIN * breadth
+    for side in range(sides):
+        last = lat[0] == 0 if sides == 1 else side == 0
+        first = jnp.where(last, height - WIDE, 0)
+        closest = jnp.where(last, height - MARGIN, 0)
+        for row in range(WIDE):
+            rows[side, pl.ds(row * breadth, breadth), :] = state[first + row].astype(F32)
+        for row in range(MARGIN):
+            spots = pl.ds(far + row * breadth, breadth)
+            rows[side, spots, :] = cotangent[closest + row].astype(F32)
+        marks = jnp.where(last, ocean[:, height - WIDE :], ocean[:, :WIDE])
+        rows[side, pl.ds(far + near, breadth), pl.ds(0, WIDE)] = marks
+    out[...] = rows[...].astype(BF16)
 
 
 def fill_windows(sizes, starts, sources, state, coded, edges):
@@ -620,8 +640,7 @@
 
     def lat_neighbours(self, last, first):
         if self.lat == 2:
-            mine = jnp.where(lax.axis_index("lat") == 0, last, first)
-            return self.swap(mine, 0, 1)[None]
+            return self.swap(last, 0, 1)[None]
         return jnp.stack([self.shift_lat(last, 1), self.shift_lat(first, -1)])
 
     def swap(self, values, lon_bits, lat_bits):
@@ -632,7 +651,7 @@
                 pairs.append((lon * self.lat + lat, there))
         return lax.ppermute(values, self.axes, pairs)
 
-    def sum_all(self, rows, beside):
+    def sum_all(self, rows, edges, finish):
         lon = lax.axis_index("lon")
         lat = lax.axis_index("lat")
         bits = [(1 << bit, 0) for bit in range(self.lon.bit_length() - 1)]
@@ -655,9 +674,15 @@
             pieces = values.reshape(count, -1, values.shape[1])
             here = code(group)
             total = lax.dynamic_index_in_dim(pieces, here, 0, False).astype(F32)
+            arrived = []
             for choice in range(1, count):
                 sent = lax.dynamic_index_in_dim(pieces, here ^ choice, 0, False)
-                total = total + self.swap(sent, *merged(group, choice)).astype(F32)
+                arrived.append(self.swap(sent, *merged(group, choice)))
+            return total, arrived
+
+        def summed(total, arrived):
+            for values in arrived:
+                total = total + values.astype(F32)
             return total.astype(BF16)
 
         def exchange(values, group):
@@ -679,7 +704,11 @@
             return jnp.concatenate(ordered, axis=0)
 
         pair, quad, rest = bits[:1], bits[1:3], bits[3:]
-        values = scatter(scatter(rows, pair), quad)
+        values = summed(*scatter(rows, pair))
+        total, arrived = scatter(values, quad)
+        arrived[0], edges = lax.optimization_barrier((arrived[0], edges))
+        beside = finish(edges)
+        values = summed(total, arrived)
         while rest:
             values = exchange(values, rest[:2])
             rest = rest[2:]
@@ -718,19 +747,21 @@
     land = land_sea.T
     marks = (land != 0).astype(BF16)
 
-    def lat_rows(far, near):
-        return jnp.concatenate(
-            [flat(state[far]), flat(cotangent[near]), whole_rows(marks[:, far], breadth)]
-        )
-
-    pieces = links.lat_neighbours(
-        lat_rows(slice(height - WIDE, height), slice(height - MARGIN, height)),
-        lat_rows(slice(0, WIDE), slice(0, MARGIN)),
-    )
+    packed_rows = round_up((WIDE + MARGIN + 1) * breadth, 16)
+    packed = (sides, packed_rows, channels)
+    packed = pl.pallas_call(
+        pack_kernel,
+        out_shape=jax.ShapeDtypeStruct(packed, BF16),
+        in_specs=[smem] + [vmem] * 3,
+        out_specs=vmem,
+        scratch_shapes=[pltpu.VMEM(packed, F32)],
+        compiler_params=pltpu.CompilerParams(vmem_limit_bytes=8 * 1024 * 1024),
+    )(lat.reshape(1), state, cotangent, land)
+    pieces = links.lat_neighbours(packed[0], packed[-1])
     far, near = WIDE * breadth, MARGIN * breadth
     piece_states = pieces[:, :far].reshape(sides, WIDE, breadth, channels)
     piece_cotangents = pieces[:, far : far + near].reshape(sides, MARGIN, breadth, channels)
-    piece_marks = pieces[:, far + near :]
+    piece_marks = pieces[:, far + near : far + near + breadth]
 
     def lon_columns(wide, narrow, margin):
         own = jnp.concatenate([state[:, wide], cotangent[:, margin]], axis=1)
@@ -829,41 +860,43 @@
         ),
     )(starts, state, cotangent, land, pieces, within, across, taps_in, *params[1:])
 
-    within, across = links.lon_neighbours(mixed_edges[0], mixed_edges[1])
-    corner = MARGIN * MARGIN
-
-    def corner_rows(rows, first):
-        beside = slice(first * MARGIN, first * MARGIN + corner)
-        parts = jnp.concatenate([flat(grad_mixed[rows]), within[beside], across[beside]])
-        return jnp.pad(parts, ((0, -parts.shape[0] % 16), (0, 0)))
-
-    pieces = links.lat_neighbours(
-        corner_rows(slice(height - MARGIN, height), height - MARGIN),
-        corner_rows(slice(0, MARGIN), 0),
-    )
-    if sides == 1:
-        places = [(1 - lat) * (MARGIN + height)]
-    else:
-        places = [0, MARGIN + height]
-    starts = jnp.stack([jnp.asarray(entry, jnp.int32) for entry in (core, *places)])
-    wide = (height + 2 * MARGIN + 1, round_up(breadth + 2 * MARGIN, 8), channels)
-    grad_state = pl.pallas_call(
-        state_kernel,
-        out_shape=jax.ShapeDtypeStruct(tile, BF16),
-        in_specs=[smem] + [vmem] * 6,
-        out_specs=vmem,
-        scratch_shapes=[
-            pltpu.VMEM(wide, F32),
-            pltpu.VMEM((TAPS, channels), F32),
-            pltpu.VMEM((edge_rows, channels), F32),
-        ],
-        compiler_params=pltpu.CompilerParams(vmem_limit_bytes=16 * 1024 * 1024),
-        cost_estimate=pl.CostEstimate(
-            flops=4_000_000_000, bytes_accessed=8_000_000, transcendentals=0
-        ),
-    )(starts, grad_mixed, within, across, pieces, masked, taps_in[0])
-
-    held, own, other, grad_state = links.sum_all(grads, grad_state)
+    def finish(mixed_edges):
+        within, across = links.lon_neighbours(mixed_edges[0], mixed_edges[1])
+        corner = MARGIN * MARGIN
+
+        def corner_rows(rows, first):
+            beside = slice(first * MARGIN, first * MARGIN + corner)
+            parts = jnp.concatenate([flat(grad_mixed[rows]), within[beside], across[beside]])
+            return jnp.pad(parts, ((0, -parts.shape[0] % 16), (0, 0)))
+
+        last = corner_rows(slice(height - MARGIN, height), height - MARGIN)
+        first = corner_rows(slice(0, MARGIN), 0)
+        if sides == 1:
+            last = first = jnp.where(lat == 0, last, first)
+        pieces = links.lat_neighbours(last, first)
+        if sides == 1:
+            places = [(1 - lat) * (MARGIN + height)]
+        else:
+            places = [0, MARGIN + height]
+        starts = jnp.stack([jnp.asarray(entry, jnp.int32) for entry in (core, *places)])
+        wide = (height + 2 * MARGIN + 1, round_up(breadth + 2 * MARGIN, 8), channels)
+        return pl.pallas_call(
+            state_kernel,
+            out_shape=jax.ShapeDtypeStruct(tile, BF16),
+            in_specs=[smem] + [vmem] * 6,
+            out_specs=vmem,
+            scratch_shapes=[
+                pltpu.VMEM(wide, F32),
+                pltpu.VMEM((TAPS, channels), F32),
+                pltpu.VMEM((edge_rows, channels), F32),
+            ],
+            compiler_params=pltpu.CompilerParams(vmem_limit_bytes=16 * 1024 * 1024),
+            cost_estimate=pl.CostEstimate(
+                flops=4_000_000_000, bytes_accessed=8_000_000, transcendentals=0
+            ),
+        )(starts, grad_mixed, within, across, pieces, masked, taps_in[0])
+
+    held, own, other, grad_state = links.sum_all(grads, mixed_edges, finish)
     shapes = [(KSIZE, KSIZE, BLOCKS, channels)] + [member.shape for member in params[1:]]
     grad_kernel, *gradients = pl.pallas_call(
         functools.partial(gradient_kernel, grad_norm),

time: 69.3 us -> 66.6 us (0.961)
  waiting for transfers between devices: 16.8 us -> 14.7 us
  local copies, waits for them, and re-layouts: 2.32 us -> 3.21 us
  starting transfers between devices: 23.5 us -> 22.7 us
  other arithmetic: 1.37 us -> 0.63 us
    unnamed x24 -> x30, local copies, waits for them, and re-layouts: 0.06 us -> 2.67 us
    slice x4 -> x1, local copies, waits for them, and re-layouts: 1.81 us -> 0.08 us  [finish(): taps_in[0]]
    ppermute x2, waiting for transfers between devices: 5.65 us -> 3.97 us  [lon_neighbours(): across = lax.ppermute(across, 'lon', pairs)]
    ppermute x2, starting transfers between devices: 6.93 us -> 6.15 us  [lon_neighbours(): across = lax.ppermute(across, 'lon', pairs)]
    convert_element_type x1, other arithmetic: 0.71 us -> 0.01 us  [on_device(): marks = (land != 0).astype(BF16)]
    pallas_call x1 -> x2, Pallas kernels: 2.75 us -> 2.91 us  [the longest x1 2.76 us: finish(): pl.pallas_call(state_kernel, out_shape=jax.ShapeDtypeStruct(tile, BF16),...]
where the time goes in v6:
time: 66.6 us; the launch traced here: 66.3 us
  Pallas kernels  24 us (36%)
  starting transfers between devices  22.7 us (34%)
  waiting for transfers between devices  14.7 us (22%)
  local copies, waits for them, and re-layouts  3.21 us (5%)
  between operations  1.07 us (2%)
    pallas_call x1, Pallas kernels, on_device(): pl.pallas_call(functools.partial(tile_kernel, sizes), out_shape=(jax.Shap...  20 us
    ppermute x15, starting transfers between devices, swap(): return lax.ppermute(values, self.axes, pairs)  16.5 us
    ppermute x15, waiting for transfers between devices, swap(): return lax.ppermute(values, self.axes, pairs)  10.7 us
    ppermute x2, starting transfers between devices, lon_neighbours(): across = lax.ppermute(across, 'lon', pairs)  6.15 us
    ppermute x2, waiting for transfers between devices, lon_neighbours(): across = lax.ppermute(across, 'lon', pairs)  3.97 us
    pallas_call x1, Pallas kernels, finish(): pl.pallas_call(state_kernel, out_shape=jax.ShapeDtypeStruct(tile, BF16),...  2.76 us
    unnamed x30, local copies, waits for them, and re-layouts  2.67 us
  transfers between devices with their start and end apart: 17, of which 9 were waited for; matrix products, arithmetic and copies ran while one was open for 1% of the time, Pallas kernels for 4%

profile of v6, /device:TPU:0, one launch (start us, length us, event | category | flops | bytes accessed | tf_op | source)
XLA Modules:
  0.0 66.3 jit_solution(18013333038814553555)
XLA Ops:
  0.7 0.9 %copy-done = bf16[45,24,128]{2,1,0:T(8,128)(2,1)S(1)} copy-done((bf16[45,24,128]{2,1,0:T(8,128)(2,1)S(1)}, bf16[45,24,128]{2,1,0:T(8,128)(2,1)}, u32[]{:S(2)}) %copy-start) | copy-done | bytes 276504
  1.6 1.0 %copy-done.2 = bf16[45,24,128]{2,1,0:T(8,128)(2,1)S(1)} copy-done((bf16[45,24,128]{2,1,0:T(8,128)(2,1)S(1)}, bf16[45,24,128]{2,1,0:T(8,128)(2,1)}, u32[]{:S(2)}) %copy-start.2) | copy-done | bytes 276504
  2.6 0.7 %copy-done.4 = s32[45,24]{0,1:T(8,128)S(1)} copy-done((s32[45,24]{0,1:T(8,128)S(1)}, s32[45,24]{0,1:T(8,128)}, u32[]{:S(2)}) %copy-start.4) | copy-done | bytes 4344
  3.4 2.9 %collective-permute-start = (bf16[320,128]{1,0:T(8,128)(2,1)S(1)}, bf16[320,128]{1,0:T(8,128)(2,1)S(1)}, u32[]{:S(2)}, u32[]{:S(2)}) collective-permute-start(bf16[320,128]{1,0:T(8,128)(2,1)S(1)} %bitcast.57), channel_id=1, source_target_pairs={{0,1},{1,0},{2,3},{3,2},{4,5},{5,4},{6,7},{7,6},{8,9},{9,8},{10,11... | collective-permute-start | bytes 245768 | tf_op jit(solution)/shard_map/ppermute | solution.py:652
  6.5 2.3 %collective-permute-done = bf16[320,128]{1,0:T(8,128)(2,1)S(1)} collective-permute-done((bf16[320,128]{1,0:T(8,128)(2,1)S(1)}, bf16[320,128]{1,0:T(8,128)(2,1)S(1)}, u32[]{:S(2)}, u32[]{:S(2)}) %collective-permute-start) | collective-permute-done | bytes 81952 | tf_op jit(solution)/shard_map/ppermute | solution.py:652
  9.3 3.4 %collective-permute-start.2 = (bf16[664,128]{1,0:T(8,128)(2,1)S(1)}, bf16[664,128]{1,0:T(8,128)(2,1)S(1)}, u32[]{:S(2)}, u32[]{:S(2)}) collective-permute-start(bf16[664,128]{1,0:T(8,128)(2,1)S(1)} %get-tuple-element.47), channel_id=1, source_target_pairs={{0,30},{2,4},{4,2},{6,8},{8,6},{10,12},{12,10},{14,16},{16,14},{18... | collective-permute-start | bytes 509960 | tf_op jit(solution)/shard_map/ppermute | solution.py:632
  12.9 4.0 %collective-permute-done.2.across = bf16[664,128]{1,0:T(8,128)(2,1)S(1)} collective-permute-done((bf16[664,128]{1,0:T(8,128)(2,1)S(1)}, bf16[664,128]{1,0:T(8,128)(2,1)S(1)}, u32[]{:S(2)}, u32[]{:S(2)}) %collective-permute-start.2) | collective-permute-done | bytes 170016 | tf_op jit(solution)/shard_map/ppermute | solution.py:632
  17.0 20.0 %shard_map.204 = (bf16[45,24,128]{2,1,0:T(8,128)(2,1)}, bf16[45,24,128]{2,1,0:T(8,128)(2,1)S(1)}, bf16[45,24,128]{2,1,0:T(8,128)(2,1)S(1)}, bf16[2,136,128]{2,1,0:T(8,128)(2,1)S(1)}, bf16[2176,128]{1,0:T(8,128)(2,1)S(1)}) custom-call(s32[6]{0:T(128)S(1)} %stack.49.starts, bf16[45,24,128]{2,1,0:T(8,128)(2,1)S(1)} %copy-done.1, ...), custom_call_target="tpu_custom_call" | custom-call | flops 2013265920 | bytes 2211840 | tf_op jit(solution)/shard_map/pallas_call | solution.py:843
  37.4 1.3 %collective-permute-done.3 = bf16[1088,128]{1,0:T(8,128)(2,1)S(1)} collective-permute-done((bf16[1088,128]{1,0:T(8,128)(2,1)S(1)}, bf16[1088,128]{1,0:T(8,128)(2,1)S(1)}, u32[]{:S(2)}, u32[]{:S(2)}) %collective-permute-start.3) | collective-permute-done | bytes 278560 | tf_op jit(solution)/shard_map/ppermute | solution.py:652
  38.7 2.5 %collective-permute-start.4 = (bf16[272,128]{1,0:T(8,128)(2,1)S(1)}, bf16[272,128]{1,0:T(8,128)(2,1)S(1)}, u32[]{:S(2)}, u32[]{:S(2)}) collective-permute-start(bf16[272,128]{1,0:T(8,128)(2,1)S(1)} %get-tuple-element.53), channel_id=1, source_target_pairs={{0,1},{1,0},{2,3},{3,2},{4,5},{5,4},{6,7},{7,6},{8,9},{9,8},{10,11... | collective-permute-start | bytes 208904 | tf_op jit(solution)/shard_map/ppermute | solution.py:652
  41.4 1.3 %collective-permute-start.5 = (bf16[272,128]{1,0:T(8,128)(2,1)S(1)}, bf16[272,128]{1,0:T(8,128)(2,1)S(1)}, u32[]{:S(2)}, u32[]{:S(2)}) collective-permute-start(bf16[272,128]{1,0:T(8,128)(2,1)S(1)} %get-tuple-element.55), channel_id=1, source_target_pairs={{0,4},{1,5},{2,6},{3,7},{4,0},{5,1},{6,2},{7,3},{8,12},{9,13},{10,... | collective-permute-start | bytes 208904 | tf_op jit(solution)/shard_map/ppermute | solution.py:652
  42.8 1.0 %collective-permute-done.4 = bf16[272,128]{1,0:T(8,128)(2,1)S(1)} collective-permute-done((bf16[272,128]{1,0:T(8,128)(2,1)S(1)}, bf16[272,128]{1,0:T(8,128)(2,1)S(1)}, u32[]{:S(2)}, u32[]{:S(2)}) %collective-permute-start.4) | collective-permute-done | bytes 69664 | tf_op jit(solution)/shard_map/ppermute | solution.py:652
  43.7 2.7 %collective-permute-start.14 = (bf16[136,128]{1,0:T(8,128)(2,1)S(1)}, bf16[136,128]{1,0:T(8,128)(2,1)S(1)}, u32[]{:S(2)}, u32[]{:S(2)}) collective-permute-start(bf16[136,128]{1,0:T(8,128)(2,1)S(1)} %get-tuple-element.64), channel_id=1, source_target_pairs={{0,30},{2,4},{4,2},{6,8},{8,6},{10,12},{12,10},{14,16},{16,14},{18... | collective-permute-start | bytes 104456 | tf_op jit(solution)/shard_map/ppermute | solution.py:632
  46.9 3.8 %collective-permute-start.9 = (bf16[272,128]{1,0:T(8,128)(2,1)S(1)}, bf16[272,128]{1,0:T(8,128)(2,1)S(1)}, u32[]{:S(2)}, u32[]{:S(2)}) collective-permute-start(bf16[272,128]{1,0:T(8,128)(2,1)S(1)} %fusion.32), channel_id=1, source_target_pairs={{0,24},{1,25},{2,26},{3,27},{4,28},{5,29},{6,30},{7,31},{8,16},{9,... | collective-permute-start | bytes 208904 | tf_op jit(solution)/shard_map/ppermute | solution.py:652
  51.3 1.2 %collective-permute-done.13.within = bf16[136,128]{1,0:T(8,128)(2,1)S(1)} collective-permute-done((bf16[136,128]{1,0:T(8,128)(2,1)S(1)}, bf16[136,128]{1,0:T(8,128)(2,1)S(1)}, u32[]{:S(2)}, u32[]{:S(2)}) %collective-permute-start.13) | collective-permute-done | bytes 34848 | tf_op jit(solution)/shard_map/ppermute | solution.py:652
  52.5 1.4 %collective-permute-start.15 = (bf16[96,128]{1,0:T(8,128)(2,1)S(1)}, bf16[96,128]{1,0:T(8,128)(2,1)S(1)}, u32[]{:S(2)}, u32[]{:S(2)}) collective-permute-start(bf16[96,128]{1,0:T(8,128)(2,1)S(1)} %fusion.41), channel_id=1, source_target_pairs={{0,1},{1,0},{2,3},{3,2},{4,5},{5,4},{6,7},{7,6},{8,9},{9,8},{10,11... | collective-permute-start | bytes 73736 | tf_op jit(solution)/shard_map/ppermute | solution.py:652
  54.0 2.3 %collective-permute-done.8 = bf16[272,128]{1,0:T(8,128)(2,1)S(1)} collective-permute-done((bf16[272,128]{1,0:T(8,128)(2,1)S(1)}, bf16[272,128]{1,0:T(8,128)(2,1)S(1)}, u32[]{:S(2)}, u32[]{:S(2)}) %collective-permute-start.8) | collective-permute-done | bytes 69664 | tf_op jit(solution)/shard_map/ppermute | solution.py:652
  56.4 1.8 %collective-permute-start.12 = (bf16[272,128]{1,0:T(8,128)(2,1)S(1)}, bf16[272,128]{1,0:T(8,128)(2,1)S(1)}, u32[]{:S(2)}, u32[]{:S(2)}) collective-permute-start(bf16[272,128]{1,0:T(8,128)(2,1)S(1)} %add_convert_fusion), channel_id=1, source_target_pairs={{0,5},{1,4},{2,7},{3,6},{4,1},{5,0},{6,3},{7,2},{8,13},{9,12},{10,... | collective-permute-start | bytes 208904 | tf_op jit(solution)/shard_map/ppermute | solution.py:652
  58.1 1.0 %collective-permute-start.11 = (bf16[272,128]{1,0:T(8,128)(2,1)S(1)}, bf16[272,128]{1,0:T(8,128)(2,1)S(1)}, u32[]{:S(2)}, u32[]{:S(2)}) collective-permute-start(bf16[272,128]{1,0:T(8,128)(2,1)S(1)} %add_convert_fusion), channel_id=1, source_target_pairs={{0,4},{1,5},{2,6},{3,7},{4,0},{5,1},{6,2},{7,3},{8,12},{9,13},{10,... | collective-permute-start | bytes 208904 | tf_op jit(solution)/shard_map/ppermute | solution.py:652
  59.1 0.8 %collective-permute-start.10 = (bf16[272,128]{1,0:T(8,128)(2,1)S(1)}, bf16[272,128]{1,0:T(8,128)(2,1)S(1)}, u32[]{:S(2)}, u32[]{:S(2)}) collective-permute-start(bf16[272,128]{1,0:T(8,128)(2,1)S(1)} %add_convert_fusion), channel_id=1, source_target_pairs={{0,1},{1,0},{2,3},{3,2},{4,5},{5,4},{6,7},{7,6},{8,9},{9,8},{10,11... | collective-permute-start | bytes 208904 | tf_op jit(solution)/shard_map/ppermute | solution.py:652
  59.9 2.8 %shard_map.205 = bf16[45,24,128]{2,1,0:T(8,128)(2,1)} custom-call(s32[2]{0:T(128)S(1)} %pad_add_fusion.starts, bf16[45,24,128]{2,1,0:T(8,128)(2,1)S(1)} %get-tuple-element.33.mixed, bf16[136,128]{1,0:T(8,128)(2,1)S(1)} %collective-permute-done.13.within, bf16[136,128]{1,0:T(8,128)(2,1)S(1)} %collective-permute-done.14.across, ...), custom_call_target="tpu_custom_call" | custom-call | flops 4000000000 | bytes 8000000 | tf_op jit(solution)/shard_map/pallas_call | solution.py:883
  62.7 0.8 %collective-permute-done.10 = bf16[272,128]{1,0:T(8,128)(2,1)S(1)} collective-permute-done((bf16[272,128]{1,0:T(8,128)(2,1)S(1)}, bf16[272,128]{1,0:T(8,128)(2,1)S(1)}, u32[]{:S(2)}, u32[]{:S(2)}) %collective-permute-start.10) | collective-permute-done | bytes 69664 | tf_op jit(solution)/shard_map/ppermute | solution.py:652
  63.6 1.5 %collective-permute-done.16.other = bf16[1088,128]{1,0:T(8,128)(2,1)S(1)} collective-permute-done((bf16[1088,128]{1,0:T(8,128)(2,1)S(1)}, bf16[1088,128]{1,0:T(8,128)(2,1)S(1)}, u32[]{:S(2)}, u32[]{:S(2)}) %collective-permute-start.16) | collective-permute-done | bytes 278560 | tf_op jit(solution)/shard_map/ppermute | solution.py:652
  65.2 1.1 %shard_map.206 = (f32[7,7,2,128]{3,2,1,0:T(2,128)}, f32[2,128]{1,0:T(2,128)}, f32[2,128]{1,0:T(2,128)}, f32[2,128]{1,0:T(2,128)}, f32[2,128,512]{2,1,0:T(8,128)}...) custom-call(s32[1]{0:T(128)} %bitcast.3.held, ...), custom_call_target="tpu_custom_call" | custom-call | tf_op jit(solution)/shard_map/pallas_call | solution.py:901
  (75 shorter events, 2.8 us)
Async XLA Ops:
  3.4 5.4 %collective-permute-start = (bf16[320,128]{1,0:T(8,128)(2,1)S(1)}, bf16[320,128]{1,0:T(8,128)(2,1)S(1)}, u32[]{:S(2)}, u32[]{:S(2)}) collective-permute-start(bf16[320,128]{1,0:T(8,128)(2,1)S(1)} %bitcast.57), channel_id=1, source_target_pairs={{0,1},{1,0},{2,3},{3,2},{4,5},{5,4},{6,7},{7,6},{8,9},{9,8},{10,11... | collective-permute-start | bytes 245768 | tf_op jit(solution)/shard_map/ppermute | solution.py:652
  9.2 7.7 %copy-start.6 = (bf16[2,128,512]{2,1,0:T(8,128)(2,1)S(1)}, bf16[2,128,512]{2,1,0:T(8,128)(2,1)}, u32[]{:S(2)}) copy-start(bf16[2,128,512]{2,1,0:T(8,128)(2,1)} %weight_in.1) | copy-start | bytes 786436
  9.2 7.7 %copy-start.7 = (bf16[2,512,128]{2,1,0:T(8,128)(2,1)S(1)}, bf16[2,512,128]{2,1,0:T(8,128)(2,1)}, u32[]{:S(2)}) copy-start(bf16[2,512,128]{2,1,0:T(8,128)(2,1)} %weight_out.1) | copy-start | bytes 786436
  9.3 7.6 %collective-permute-start.2 = (bf16[664,128]{1,0:T(8,128)(2,1)S(1)}, bf16[664,128]{1,0:T(8,128)(2,1)S(1)}, u32[]{:S(2)}, u32[]{:S(2)}) collective-permute-start(bf16[664,128]{1,0:T(8,128)(2,1)S(1)} %get-tuple-element.47), channel_id=1, source_target_pairs={{0,30},{2,4},{4,2},{6,8},{8,6},{10,12},{12,10},{14,16},{16,14},{18... | collective-permute-start | bytes 509960 | tf_op jit(solution)/shard_map/ppermute | solution.py:632
  12.7 4.2 %collective-permute-start.1 = (bf16[664,128]{1,0:T(8,128)(2,1)S(1)}, bf16[664,128]{1,0:T(8,128)(2,1)S(1)}, u32[]{:S(2)}, u32[]{:S(2)}) collective-permute-start(bf16[664,128]{1,0:T(8,128)(2,1)S(1)} %get-tuple-element.48), channel_id=1, source_target_pairs={{0,2},{1,3},{2,0},{3,1},{4,6},{5,7},{6,4},{7,5},{8,10},{9,11},{10,... | collective-permute-start | bytes 509960 | tf_op jit(solution)/shard_map/ppermute | solution.py:652
  12.7 4.2 %copy-start.9 = (f32[2,128]{1,0:T(2,128)S(1)}, f32[2,128]{1,0:T(2,128)}, u32[]{:S(2)}) copy-start(f32[2,128]{1,0:T(2,128)} %conv_bias.1) | copy-start | bytes 3076
  12.7 4.2 %copy-start.10 = (f32[2,128]{1,0:T(2,128)S(1)}, f32[2,128]{1,0:T(2,128)}, u32[]{:S(2)}) copy-start(f32[2,128]{1,0:T(2,128)} %norm_gain.1) | copy-start | bytes 3076
  12.8 4.2 %copy-start.11 = (f32[2,128]{1,0:T(2,128)S(1)}, f32[2,128]{1,0:T(2,128)}, u32[]{:S(2)}) copy-start(f32[2,128]{1,0:T(2,128)} %norm_bias.1) | copy-start | bytes 3076
  12.8 4.2 %copy-start.12 = (f32[2,128]{1,0:T(2,128)S(1)}, f32[2,128]{1,0:T(2,128)}, u32[]{:S(2)}) copy-start(f32[2,128]{1,0:T(2,128)} %bias_out.1) | copy-start | bytes 3076
  12.8 4.2 %copy-start.13 = (f32[2,128]{1,0:T(2,128)S(1)}, f32[2,128]{1,0:T(2,128)}, u32[]{:S(2)}) copy-start(f32[2,128]{1,0:T(2,128)} %layer_scale.1) | copy-start | bytes 3076
  37.0 1.6 %collective-permute-start.3 = (bf16[1088,128]{1,0:T(8,128)(2,1)S(1)}, bf16[1088,128]{1,0:T(8,128)(2,1)S(1)}, u32[]{:S(2)}, u32[]{:S(2)}) collective-permute-start(bf16[1088,128]{1,0:T(8,128)(2,1)S(1)} %dynamic-slice_bitcast_fusion), channel_id=1, source_target_pairs={{0,2},{1,3},{2,0},{3,1},{4,6},{5,7},{6,4},{7,5},{8,10},{9,11},{10,... | collective-permute-start | bytes 835592 | tf_op jit(solution)/shard_map/ppermute | solution.py:652
  38.7 5.0 %collective-permute-start.4 = (bf16[272,128]{1,0:T(8,128)(2,1)S(1)}, bf16[272,128]{1,0:T(8,128)(2,1)S(1)}, u32[]{:S(2)}, u32[]{:S(2)}) collective-permute-start(bf16[272,128]{1,0:T(8,128)(2,1)S(1)} %get-tuple-element.53), channel_id=1, source_target_pairs={{0,1},{1,0},{2,3},{3,2},{4,5},{5,4},{6,7},{7,6},{8,9},{9,8},{10,11... | collective-permute-start | bytes 208904 | tf_op jit(solution)/shard_map/ppermute | solution.py:652
  41.2 5.3 %collective-permute-start.6 = (bf16[272,128]{1,0:T(8,128)(2,1)S(1)}, bf16[272,128]{1,0:T(8,128)(2,1)S(1)}, u32[]{:S(2)}, u32[]{:S(2)}) collective-permute-start(bf16[272,128]{1,0:T(8,128)(2,1)S(1)} %get-tuple-element.54), channel_id=1, source_target_pairs={{0,5},{1,4},{2,7},{3,6},{4,1},{5,0},{6,3},{7,2},{8,13},{9,12},{10,... | collective-permute-start | bytes 208904 | tf_op jit(solution)/shard_map/ppermute | solution.py:652
  41.4 5.4 %collective-permute-start.5 = (bf16[272,128]{1,0:T(8,128)(2,1)S(1)}, bf16[272,128]{1,0:T(8,128)(2,1)S(1)}, u32[]{:S(2)}, u32[]{:S(2)}) collective-permute-start(bf16[272,128]{1,0:T(8,128)(2,1)S(1)} %get-tuple-element.55), channel_id=1, source_target_pairs={{0,4},{1,5},{2,6},{3,7},{4,0},{5,1},{6,2},{7,3},{8,12},{9,13},{10,... | collective-permute-start | bytes 208904 | tf_op jit(solution)/shard_map/ppermute | solution.py:652
  43.7 7.6 %collective-permute-start.14 = (bf16[136,128]{1,0:T(8,128)(2,1)S(1)}, bf16[136,128]{1,0:T(8,128)(2,1)S(1)}, u32[]{:S(2)}, u32[]{:S(2)}) collective-permute-start(bf16[136,128]{1,0:T(8,128)(2,1)S(1)} %get-tuple-element.64), channel_id=1, source_target_pairs={{0,30},{2,4},{4,2},{6,8},{8,6},{10,12},{12,10},{14,16},{16,14},{18... | collective-permute-start | bytes 104456 | tf_op jit(solution)/shard_map/ppermute | solution.py:632
  46.9 7.1 %collective-permute-start.9 = (bf16[272,128]{1,0:T(8,128)(2,1)S(1)}, bf16[272,128]{1,0:T(8,128)(2,1)S(1)}, u32[]{:S(2)}, u32[]{:S(2)}) collective-permute-start(bf16[272,128]{1,0:T(8,128)(2,1)S(1)} %fusion.32), channel_id=1, source_target_pairs={{0,24},{1,25},{2,26},{3,27},{4,28},{5,29},{6,30},{7,31},{8,16},{9,... | collective-permute-start | bytes 208904 | tf_op jit(solution)/shard_map/ppermute | solution.py:652
  50.7 5.6 %collective-permute-start.8 = (bf16[272,128]{1,0:T(8,128)(2,1)S(1)}, bf16[272,128]{1,0:T(8,128)(2,1)S(1)}, u32[]{:S(2)}, u32[]{:S(2)}) collective-permute-start(bf16[272,128]{1,0:T(8,128)(2,1)S(1)} %fusion.32), channel_id=1, source_target_pairs={{0,16},{1,17},{2,18},{3,19},{4,20},{5,21},{6,22},{7,23},{8,24},{9,... | collective-permute-start | bytes 208904 | tf_op jit(solution)/shard_map/ppermute | solution.py:652
  50.7 5.6 %collective-permute-start.7 = (bf16[272,128]{1,0:T(8,128)(2,1)S(1)}, bf16[272,128]{1,0:T(8,128)(2,1)S(1)}, u32[]{:S(2)}, u32[]{:S(2)}) collective-permute-start(bf16[272,128]{1,0:T(8,128)(2,1)S(1)} %fusion.32), channel_id=1, source_target_pairs={{0,8},{1,9},{2,10},{3,11},{4,12},{5,13},{6,14},{7,15},{8,0},{9,1},... | collective-permute-start | bytes 208904 | tf_op jit(solution)/shard_map/ppermute | solution.py:652
  51.3 1.2 %collective-permute-start.13 = (bf16[136,128]{1,0:T(8,128)(2,1)S(1)}, bf16[136,128]{1,0:T(8,128)(2,1)S(1)}, u32[]{:S(2)}, u32[]{:S(2)}) collective-permute-start(bf16[136,128]{1,0:T(8,128)(2,1)S(1)} %get-tuple-element.65), channel_id=1, source_target_pairs={{0,2},{1,3},{2,0},{3,1},{4,6},{5,7},{6,4},{7,5},{8,10},{9,11},{10,... | collective-permute-start | bytes 104456 | tf_op jit(solution)/shard_map/ppermute | solution.py:652
  52.5 7.4 %collective-permute-start.15 = (bf16[96,128]{1,0:T(8,128)(2,1)S(1)}, bf16[96,128]{1,0:T(8,128)(2,1)S(1)}, u32[]{:S(2)}, u32[]{:S(2)}) collective-permute-start(bf16[96,128]{1,0:T(8,128)(2,1)S(1)} %fusion.41), channel_id=1, source_target_pairs={{0,1},{1,0},{2,3},{3,2},{4,5},{5,4},{6,7},{7,6},{8,9},{9,8},{10,11... | collective-permute-start | bytes 73736 | tf_op jit(solution)/shard_map/ppermute | solution.py:652
  56.4 6.3 %collective-permute-start.12 = (bf16[272,128]{1,0:T(8,128)(2,1)S(1)}, bf16[272,128]{1,0:T(8,128)(2,1)S(1)}, u32[]{:S(2)}, u32[]{:S(2)}) collective-permute-start(bf16[272,128]{1,0:T(8,128)(2,1)S(1)} %add_convert_fusion), channel_id=1, source_target_pairs={{0,5},{1,4},{2,7},{3,6},{4,1},{5,0},{6,3},{7,2},{8,13},{9,12},{10,... | collective-permute-start | bytes 208904 | tf_op jit(solution)/shard_map/ppermute | solution.py:652
  58.1 4.6 %collective-permute-start.11 = (bf16[272,128]{1,0:T(8,128)(2,1)S(1)}, bf16[272,128]{1,0:T(8,128)(2,1)S(1)}, u32[]{:S(2)}, u32[]{:S(2)}) collective-permute-start(bf16[272,128]{1,0:T(8,128)(2,1)S(1)} %add_convert_fusion), channel_id=1, source_target_pairs={{0,4},{1,5},{2,6},{3,7},{4,0},{5,1},{6,2},{7,3},{8,12},{9,13},{10,... | collective-permute-start | bytes 208904 | tf_op jit(solution)/shard_map/ppermute | solution.py:652
  59.1 4.3 %collective-permute-start.10 = (bf16[272,128]{1,0:T(8,128)(2,1)S(1)}, bf16[272,128]{1,0:T(8,128)(2,1)S(1)}, u32[]{:S(2)}, u32[]{:S(2)}) collective-permute-start(bf16[272,128]{1,0:T(8,128)(2,1)S(1)} %add_convert_fusion), channel_id=1, source_target_pairs={{0,1},{1,0},{2,3},{3,2},{4,5},{5,4},{6,7},{7,6},{8,9},{9,8},{10,11... | collective-permute-start | bytes 208904 | tf_op jit(solution)/shard_map/ppermute | solution.py:652
  63.6 1.6 %collective-permute-start.16 = (bf16[1088,128]{1,0:T(8,128)(2,1)S(1)}, bf16[1088,128]{1,0:T(8,128)(2,1)S(1)}, u32[]{:S(2)}, u32[]{:S(2)}) collective-permute-start(bf16[1088,128]{1,0:T(8,128)(2,1)S(1)} %pad_maximum_fusion.1.own), channel_id=1, source_target_pairs={{0,2},{1,3},{2,0},{3,1},{4,6},{5,7},{6,4},{7,5},{8,10},{9,11},{10,... | collective-permute-start | bytes 835592 | tf_op jit(solution)/shard_map/ppermute | solution.py:652
  (8 other events, 20.7 us)

commit v7 on v6

--- a/solution.py
+++ b/solution.py
@@ -17,6 +17,8 @@
 INV_ROOT_TWO_PI = 0.3989422804014327
 LAND = 1024.0
 LAND_BOUND = 512.0
+VMEM_LIMIT = 48 * 1024 * 1024
+PACK_LIMIT = 62 * 1024 * 1024
 F32 = jnp.float32
 BF16 = jnp.bfloat16
 FIRST_STEP = 19
@@ -160,21 +162,34 @@
                 out[pl.ds(tap_row * KSIZE + tap_col, 1), :] = total
 
 
-def pack_kernel(lat, state, cotangent, land_sea, out, rows):
-    height, breadth, channels = state.shape
+def pack_kernel(lat, state, cotangent, land_sea, out, rows, far_rows, near_rows, land, arrived):
+    height, breadth = state.shape[:2]
     sides = out.shape[0]
-    rows[...] = jnp.zeros_like(rows)
-    ocean = jnp.where(land_sea[...] != 0, 1.0, 0.0).astype(F32)
-    far, near = WIDE * breadth, MARGIN * breadth
+    copies = [pltpu.make_async_copy(land_sea, land, arrived.at[0])]
     for side in range(sides):
         last = lat[0] == 0 if sides == 1 else side == 0
         first = jnp.where(last, height - WIDE, 0)
         closest = jnp.where(last, height - MARGIN, 0)
+        source = state.at[pl.ds(first, WIDE)]
+        copies.append(pltpu.make_async_copy(source, far_rows.at[side], arrived.at[1 + side]))
+        source = cotangent.at[pl.ds(closest, MARGIN)]
+        copies.append(
+            pltpu.make_async_copy(source, near_rows.at[side], arrived.at[1 + sides + side])
+        )
+    for copy in copies:
+        copy.start()
+    rows[...] = jnp.zeros_like(rows)
+    for copy in copies:
+        copy.wait()
+    ocean = jnp.where(land[...] != 0, 1.0, 0.0).astype(F32)
+    far, near = WIDE * breadth, MARGIN * breadth
+    for side in range(sides):
+        last = lat[0] == 0 if sides == 1 else side == 0
         for row in range(WIDE):
-            rows[side, pl.ds(row * breadth, breadth), :] = state[first + row].astype(F32)
+            rows[side, pl.ds(row * breadth, breadth), :] = far_rows[side, row].astype(F32)
         for row in range(MARGIN):
             spots = pl.ds(far + row * breadth, breadth)
-            rows[side, spots, :] = cotangent[closest + row].astype(F32)
+            rows[side, spots, :] = near_rows[side, row].astype(F32)
         marks = jnp.where(last, ocean[:, height - WIDE :], ocean[:, :WIDE])
         rows[side, pl.ds(far + near, breadth), pl.ds(0, WIDE)] = marks
     out[...] = rows[...].astype(BF16)
@@ -752,10 +767,16 @@
     packed = pl.pallas_call(
         pack_kernel,
         out_shape=jax.ShapeDtypeStruct(packed, BF16),
-        in_specs=[smem] + [vmem] * 3,
+        in_specs=[smem] + [pl.BlockSpec(memory_space=pl.ANY)] * 3,
         out_specs=vmem,
-        scratch_shapes=[pltpu.VMEM(packed, F32)],
-        compiler_params=pltpu.CompilerParams(vmem_limit_bytes=8 * 1024 * 1024),
+        scratch_shapes=[
+            pltpu.VMEM(packed, F32),
+            pltpu.VMEM((sides, WIDE, breadth, channels), BF16),
+            pltpu.VMEM((sides, MARGIN, breadth, channels), BF16),
+            pltpu.VMEM((breadth, height), jnp.int32),
+            pltpu.SemaphoreType.DMA((1 + 2 * sides,)),
+        ],
+        compiler_params=pltpu.CompilerParams(vmem_limit_bytes=PACK_LIMIT),
     )(lat.reshape(1), state, cotangent, land)
     pieces = links.lat_neighbours(packed[0], packed[-1])
     far, near = WIDE * breadth, MARGIN * breadth
@@ -852,7 +873,7 @@
         in_specs=[smem] + [vmem] * 15,
         out_specs=(vmem,) * 5,
         scratch_shapes=scratch,
-        compiler_params=pltpu.CompilerParams(vmem_limit_bytes=48 * 1024 * 1024),
+        compiler_params=pltpu.CompilerParams(vmem_limit_bytes=VMEM_LIMIT),
         cost_estimate=pl.CostEstimate(
             flops=20 * all_cells * channels * hidden_units,
             bytes_accessed=4 * height * breadth * channels * 4,

time: 66.6 us -> 65.8 us (0.988)
  local copies, waits for them, and re-layouts: 3.21 us -> 0.6 us
  Pallas kernels: 24 us -> 25.7 us
    unnamed x30 -> x24, local copies, waits for them, and re-layouts: 2.67 us -> 0.06 us
    pallas_call x1, Pallas kernels: 0.15 us -> 1.7 us  [on_device(): pl.pallas_call(pack_kernel, out_shape=jax.ShapeDtypeStruct(packed, BF16),...]
  transfers between devices with their start and end apart: 17 -> 17, of which waited for: 9 -> 10; matrix products, arithmetic and copies ran while one was open for 1% -> 1% of each run, Pallas kernels for 4% -> 4%
where the time goes in v7:
time: 65.8 us; the launch traced here: 65.7 us
  Pallas kernels  25.7 us (39%)
  starting transfers between devices  22.7 us (34%)
  waiting for transfers between devices  14.9 us (23%)
  between operations  1.09 us (2%)
    pallas_call x1, Pallas kernels, on_device(): pl.pallas_call(functools.partial(tile_kernel, sizes), out_shape=(jax.Shap...  20.1 us
    ppermute x15, starting transfers between devices, swap(): return lax.ppermute(values, self.axes, pairs)  16.6 us
    ppermute x15, waiting for transfers between devices, swap(): return lax.ppermute(values, self.axes, pairs)  10.9 us
    ppermute x2, starting transfers between devices, lon_neighbours(): across = lax.ppermute(across, 'lon', pairs)  6.14 us
    ppermute x2, waiting for transfers between devices, lon_neighbours(): across = lax.ppermute(across, 'lon', pairs)  3.98 us
    pallas_call x1, Pallas kernels, finish(): pl.pallas_call(state_kernel, out_shape=jax.ShapeDtypeStruct(tile, BF16),...  2.75 us
    pallas_call x1, Pallas kernels, on_device(): pl.pallas_call(pack_kernel, out_shape=jax.ShapeDtypeStruct(packed, BF16),...  1.7 us
  transfers between devices with their start and end apart: 17, of which 10 were waited for; matrix products, arithmetic and copies ran while one was open for 1% of the time, Pallas kernels for 4%

profile of v7, /device:TPU:0, one launch (start us, length us, event | category | flops | bytes accessed | tf_op | source)
XLA Modules:
  0.0 65.7 jit_solution(349474938982986629)
XLA Ops:
  0.7 1.7 %shard_map.203 = bf16[1,320,128]{2,1,0:T(8,128)(2,1)} custom-call(s32[1]{0:T(128)} %bitcast.7.lat, bf16[45,24,128]{2,1,0:T(8,128)(2,1)} %state_tile.1, bf16[45,24,128]{2,1,0:T(8,128)(2,1)} %cotangent.3, s32[24,45]{1,0:T(8,128)} %bitcast.61), custom_call_target="tpu_custom_call" | custom-call | tf_op jit(solution)/shard_map/pallas_call | solution.py:767
  2.4 3.0 %collective-permute-start = (bf16[320,128]{1,0:T(8,128)(2,1)}, bf16[320,128]{1,0:T(8,128)(2,1)S(1)}, u32[]{:S(2)}, u32[]{:S(2)}) collective-permute-start(bf16[320,128]{1,0:T(8,128)(2,1)} %bitcast.69), channel_id=1, source_target_pairs={{0,1},{1,0},{2,3},{3,2},{4,5},{5,4},{6,7},{7,6},{8,9},{9,8},{10,11... | collective-permute-start | bytes 245768 | tf_op jit(solution)/shard_map/ppermute | solution.py:667
  5.6 2.5 %collective-permute-done = bf16[320,128]{1,0:T(8,128)(2,1)S(1)} collective-permute-done((bf16[320,128]{1,0:T(8,128)(2,1)}, bf16[320,128]{1,0:T(8,128)(2,1)S(1)}, u32[]{:S(2)}, u32[]{:S(2)}) %collective-permute-start) | collective-permute-done | bytes 81952 | tf_op jit(solution)/shard_map/ppermute | solution.py:667
  8.6 3.4 %collective-permute-start.2 = (bf16[664,128]{1,0:T(8,128)(2,1)S(1)}, bf16[664,128]{1,0:T(8,128)(2,1)S(1)}, u32[]{:S(2)}, u32[]{:S(2)}) collective-permute-start(bf16[664,128]{1,0:T(8,128)(2,1)S(1)} %get-tuple-element.47), channel_id=1, source_target_pairs={{0,30},{2,4},{4,2},{6,8},{8,6},{10,12},{12,10},{14,16},{16,14},{18... | collective-permute-start | bytes 509960 | tf_op jit(solution)/shard_map/ppermute | solution.py:647
  12.2 4.0 %collective-permute-done.2.across = bf16[664,128]{1,0:T(8,128)(2,1)S(1)} collective-permute-done((bf16[664,128]{1,0:T(8,128)(2,1)S(1)}, bf16[664,128]{1,0:T(8,128)(2,1)S(1)}, u32[]{:S(2)}, u32[]{:S(2)}) %collective-permute-start.2) | collective-permute-done | bytes 170016 | tf_op jit(solution)/shard_map/ppermute | solution.py:647
  16.2 20.1 %shard_map.204 = (bf16[45,24,128]{2,1,0:T(8,128)(2,1)}, bf16[45,24,128]{2,1,0:T(8,128)(2,1)S(1)}, bf16[45,24,128]{2,1,0:T(8,128)(2,1)S(1)}, bf16[2,136,128]{2,1,0:T(8,128)(2,1)S(1)}, bf16[2176,128]{1,0:T(8,128)(2,1)S(1)}) custom-call(s32[6]{0:T(128)S(1)} %stack.49.starts, bf16[45,24,128]{2,1,0:T(8,128)(2,1)S(1)} %copy-done, ...), custom_call_target="tpu_custom_call" | custom-call | flops 2013265920 | bytes 2211840 | tf_op jit(solution)/shard_map/pallas_call | solution.py:864
  36.7 1.3 %collective-permute-done.3 = bf16[1088,128]{1,0:T(8,128)(2,1)S(1)} collective-permute-done((bf16[1088,128]{1,0:T(8,128)(2,1)S(1)}, bf16[1088,128]{1,0:T(8,128)(2,1)S(1)}, u32[]{:S(2)}, u32[]{:S(2)}) %collective-permute-start.3) | collective-permute-done | bytes 278560 | tf_op jit(solution)/shard_map/ppermute | solution.py:667
  38.1 2.4 %collective-permute-start.4 = (bf16[272,128]{1,0:T(8,128)(2,1)S(1)}, bf16[272,128]{1,0:T(8,128)(2,1)S(1)}, u32[]{:S(2)}, u32[]{:S(2)}) collective-permute-start(bf16[272,128]{1,0:T(8,128)(2,1)S(1)} %get-tuple-element.53), channel_id=1, source_target_pairs={{0,1},{1,0},{2,3},{3,2},{4,5},{5,4},{6,7},{7,6},{8,9},{9,8},{10,11... | collective-permute-start | bytes 208904 | tf_op jit(solution)/shard_map/ppermute | solution.py:667
  40.8 1.3 %collective-permute-start.5 = (bf16[272,128]{1,0:T(8,128)(2,1)S(1)}, bf16[272,128]{1,0:T(8,128)(2,1)S(1)}, u32[]{:S(2)}, u32[]{:S(2)}) collective-permute-start(bf16[272,128]{1,0:T(8,128)(2,1)S(1)} %get-tuple-element.55), channel_id=1, source_target_pairs={{0,4},{1,5},{2,6},{3,7},{4,0},{5,1},{6,2},{7,3},{8,12},{9,13},{10,... | collective-permute-start | bytes 208904 | tf_op jit(solution)/shard_map/ppermute | solution.py:667
  42.1 1.0 %collective-permute-done.4 = bf16[272,128]{1,0:T(8,128)(2,1)S(1)} collective-permute-done((bf16[272,128]{1,0:T(8,128)(2,1)S(1)}, bf16[272,128]{1,0:T(8,128)(2,1)S(1)}, u32[]{:S(2)}, u32[]{:S(2)}) %collective-permute-start.4) | collective-permute-done | bytes 69664 | tf_op jit(solution)/shard_map/ppermute | solution.py:667
  43.0 2.7 %collective-permute-start.14 = (bf16[136,128]{1,0:T(8,128)(2,1)S(1)}, bf16[136,128]{1,0:T(8,128)(2,1)S(1)}, u32[]{:S(2)}, u32[]{:S(2)}) collective-permute-start(bf16[136,128]{1,0:T(8,128)(2,1)S(1)} %get-tuple-element.64), channel_id=1, source_target_pairs={{0,30},{2,4},{4,2},{6,8},{8,6},{10,12},{12,10},{14,16},{16,14},{18... | collective-permute-start | bytes 104456 | tf_op jit(solution)/shard_map/ppermute | solution.py:647
  45.8 0.3 collective-permute-done.5
  46.2 3.8 %collective-permute-start.9 = (bf16[272,128]{1,0:T(8,128)(2,1)S(1)}, bf16[272,128]{1,0:T(8,128)(2,1)S(1)}, u32[]{:S(2)}, u32[]{:S(2)}) collective-permute-start(bf16[272,128]{1,0:T(8,128)(2,1)S(1)} %fusion.32), channel_id=1, source_target_pairs={{0,24},{1,25},{2,26},{3,27},{4,28},{5,29},{6,30},{7,31},{8,16},{9,... | collective-permute-start | bytes 208904 | tf_op jit(solution)/shard_map/ppermute | solution.py:667
  50.0 0.6 collective-permute-start.7
  50.7 1.2 %collective-permute-done.13.within = bf16[136,128]{1,0:T(8,128)(2,1)S(1)} collective-permute-done((bf16[136,128]{1,0:T(8,128)(2,1)S(1)}, bf16[136,128]{1,0:T(8,128)(2,1)S(1)}, u32[]{:S(2)}, u32[]{:S(2)}) %collective-permute-start.13) | collective-permute-done | bytes 34848 | tf_op jit(solution)/shard_map/ppermute | solution.py:667
  51.9 1.4 %collective-permute-start.15 = (bf16[96,128]{1,0:T(8,128)(2,1)S(1)}, bf16[96,128]{1,0:T(8,128)(2,1)S(1)}, u32[]{:S(2)}, u32[]{:S(2)}) collective-permute-start(bf16[96,128]{1,0:T(8,128)(2,1)S(1)} %fusion.41), channel_id=1, source_target_pairs={{0,1},{1,0},{2,3},{3,2},{4,5},{5,4},{6,7},{7,6},{8,9},{9,8},{10,11... | collective-permute-start | bytes 73736 | tf_op jit(solution)/shard_map/ppermute | solution.py:667
  53.3 2.3 %collective-permute-done.8 = bf16[272,128]{1,0:T(8,128)(2,1)S(1)} collective-permute-done((bf16[272,128]{1,0:T(8,128)(2,1)S(1)}, bf16[272,128]{1,0:T(8,128)(2,1)S(1)}, u32[]{:S(2)}, u32[]{:S(2)}) %collective-permute-start.8) | collective-permute-done | bytes 69664 | tf_op jit(solution)/shard_map/ppermute | solution.py:667
  55.7 1.7 %collective-permute-start.12 = (bf16[272,128]{1,0:T(8,128)(2,1)S(1)}, bf16[272,128]{1,0:T(8,128)(2,1)S(1)}, u32[]{:S(2)}, u32[]{:S(2)}) collective-permute-start(bf16[272,128]{1,0:T(8,128)(2,1)S(1)} %add_convert_fusion), channel_id=1, source_target_pairs={{0,5},{1,4},{2,7},{3,6},{4,1},{5,0},{6,3},{7,2},{8,13},{9,12},{10,... | collective-permute-start | bytes 208904 | tf_op jit(solution)/shard_map/ppermute | solution.py:667
  57.4 1.0 %collective-permute-start.11 = (bf16[272,128]{1,0:T(8,128)(2,1)S(1)}, bf16[272,128]{1,0:T(8,128)(2,1)S(1)}, u32[]{:S(2)}, u32[]{:S(2)}) collective-permute-start(bf16[272,128]{1,0:T(8,128)(2,1)S(1)} %add_convert_fusion), channel_id=1, source_target_pairs={{0,4},{1,5},{2,6},{3,7},{4,0},{5,1},{6,2},{7,3},{8,12},{9,13},{10,... | collective-permute-start | bytes 208904 | tf_op jit(solution)/shard_map/ppermute | solution.py:667
  58.5 0.8 %collective-permute-start.10 = (bf16[272,128]{1,0:T(8,128)(2,1)S(1)}, bf16[272,128]{1,0:T(8,128)(2,1)S(1)}, u32[]{:S(2)}, u32[]{:S(2)}) collective-permute-start(bf16[272,128]{1,0:T(8,128)(2,1)S(1)} %add_convert_fusion), channel_id=1, source_target_pairs={{0,1},{1,0},{2,3},{3,2},{4,5},{5,4},{6,7},{7,6},{8,9},{9,8},{10,11... | collective-permute-start | bytes 208904 | tf_op jit(solution)/shard_map/ppermute | solution.py:667
  59.3 2.8 %shard_map.205 = bf16[45,24,128]{2,1,0:T(8,128)(2,1)} custom-call(s32[2]{0:T(128)S(1)} %pad_add_fusion.starts, bf16[45,24,128]{2,1,0:T(8,128)(2,1)S(1)} %get-tuple-element.33.mixed, bf16[136,128]{1,0:T(8,128)(2,1)S(1)} %collective-permute-done.13.within, bf16[136,128]{1,0:T(8,128)(2,1)S(1)} %collective-permute-done.14.across, ...), custom_call_target="tpu_custom_call" | custom-call | flops 4000000000 | bytes 8000000 | tf_op jit(solution)/shard_map/pallas_call | solution.py:904
  62.0 0.8 %collective-permute-done.10 = bf16[272,128]{1,0:T(8,128)(2,1)S(1)} collective-permute-done((bf16[272,128]{1,0:T(8,128)(2,1)S(1)}, bf16[272,128]{1,0:T(8,128)(2,1)S(1)}, u32[]{:S(2)}, u32[]{:S(2)}) %collective-permute-start.10) | collective-permute-done | bytes 69664 | tf_op jit(solution)/shard_map/ppermute | solution.py:667
  63.0 1.5 %collective-permute-done.16.other = bf16[1088,128]{1,0:T(8,128)(2,1)S(1)} collective-permute-done((bf16[1088,128]{1,0:T(8,128)(2,1)S(1)}, bf16[1088,128]{1,0:T(8,128)(2,1)S(1)}, u32[]{:S(2)}, u32[]{:S(2)}) %collective-permute-start.16) | collective-permute-done | bytes 278560 | tf_op jit(solution)/shard_map/ppermute | solution.py:667
  64.5 1.1 %shard_map.206 = (f32[7,7,2,128]{3,2,1,0:T(2,128)}, f32[2,128]{1,0:T(2,128)}, f32[2,128]{1,0:T(2,128)}, f32[2,128]{1,0:T(2,128)}, f32[2,128,512]{2,1,0:T(8,128)}...) custom-call(s32[1]{0:T(128)} %bitcast.3.held, ...), custom_call_target="tpu_custom_call" | custom-call | tf_op jit(solution)/shard_map/pallas_call | solution.py:922
  (69 shorter events, 1.7 us)
Async XLA Ops:
  0.6 4.7 %copy-start.2 = (s32[45,24]{0,1:T(8,128)S(1)}, s32[45,24]{0,1:T(8,128)}, u32[]{:S(2)}) copy-start(s32[45,24]{0,1:T(8,128)} %param.13) | copy-start | bytes 12964
  0.7 4.7 %copy-start.1 = (bf16[45,24,128]{2,1,0:T(8,128)(2,1)S(1)}, bf16[45,24,128]{2,1,0:T(8,128)(2,1)}, u32[]{:S(2)}) copy-start(bf16[45,24,128]{2,1,0:T(8,128)(2,1)} %cotangent.3) | copy-start | bytes 829444
  0.7 4.8 %copy-start = (bf16[45,24,128]{2,1,0:T(8,128)(2,1)S(1)}, bf16[45,24,128]{2,1,0:T(8,128)(2,1)}, u32[]{:S(2)}) copy-start(bf16[45,24,128]{2,1,0:T(8,128)(2,1)} %state_tile.1) | copy-start | bytes 829444
  2.4 5.7 %collective-permute-start = (bf16[320,128]{1,0:T(8,128)(2,1)}, bf16[320,128]{1,0:T(8,128)(2,1)S(1)}, u32[]{:S(2)}, u32[]{:S(2)}) collective-permute-start(bf16[320,128]{1,0:T(8,128)(2,1)} %bitcast.69), channel_id=1, source_target_pairs={{0,1},{1,0},{2,3},{3,2},{4,5},{5,4},{6,7},{7,6},{8,9},{9,8},{10,11... | collective-permute-start | bytes 245768 | tf_op jit(solution)/shard_map/ppermute | solution.py:667
  8.5 7.7 %copy-start.3 = (bf16[2,128,512]{2,1,0:T(8,128)(2,1)S(1)}, bf16[2,128,512]{2,1,0:T(8,128)(2,1)}, u32[]{:S(2)}) copy-start(bf16[2,128,512]{2,1,0:T(8,128)(2,1)} %weight_in.1) | copy-start | bytes 786436
  8.5 7.7 %copy-start.4 = (bf16[2,512,128]{2,1,0:T(8,128)(2,1)S(1)}, bf16[2,512,128]{2,1,0:T(8,128)(2,1)}, u32[]{:S(2)}) copy-start(bf16[2,512,128]{2,1,0:T(8,128)(2,1)} %weight_out.1) | copy-start | bytes 786436
  8.6 7.6 %collective-permute-start.2 = (bf16[664,128]{1,0:T(8,128)(2,1)S(1)}, bf16[664,128]{1,0:T(8,128)(2,1)S(1)}, u32[]{:S(2)}, u32[]{:S(2)}) collective-permute-start(bf16[664,128]{1,0:T(8,128)(2,1)S(1)} %get-tuple-element.47), channel_id=1, source_target_pairs={{0,30},{2,4},{4,2},{6,8},{8,6},{10,12},{12,10},{14,16},{16,14},{18... | collective-permute-start | bytes 509960 | tf_op jit(solution)/shard_map/ppermute | solution.py:647
  12.0 4.2 %collective-permute-start.1 = (bf16[664,128]{1,0:T(8,128)(2,1)S(1)}, bf16[664,128]{1,0:T(8,128)(2,1)S(1)}, u32[]{:S(2)}, u32[]{:S(2)}) collective-permute-start(bf16[664,128]{1,0:T(8,128)(2,1)S(1)} %get-tuple-element.48), channel_id=1, source_target_pairs={{0,2},{1,3},{2,0},{3,1},{4,6},{5,7},{6,4},{7,5},{8,10},{9,11},{10,... | collective-permute-start | bytes 509960 | tf_op jit(solution)/shard_map/ppermute | solution.py:667
  12.0 4.2 %copy-start.9 = (f32[2,128]{1,0:T(2,128)S(1)}, f32[2,128]{1,0:T(2,128)}, u32[]{:S(2)}) copy-start(f32[2,128]{1,0:T(2,128)} %bias_out.1) | copy-start | bytes 3076
  12.0 4.2 %copy-start.10 = (f32[2,128]{1,0:T(2,128)S(1)}, f32[2,128]{1,0:T(2,128)}, u32[]{:S(2)}) copy-start(f32[2,128]{1,0:T(2,128)} %layer_scale.1) | copy-start | bytes 3076
  36.3 1.6 %collective-permute-start.3 = (bf16[1088,128]{1,0:T(8,128)(2,1)S(1)}, bf16[1088,128]{1,0:T(8,128)(2,1)S(1)}, u32[]{:S(2)}, u32[]{:S(2)}) collective-permute-start(bf16[1088,128]{1,0:T(8,128)(2,1)S(1)} %dynamic-slice_bitcast_fusion), channel_id=1, source_target_pairs={{0,2},{1,3},{2,0},{3,1},{4,6},{5,7},{6,4},{7,5},{8,10},{9,11},{10,... | collective-permute-start | bytes 835592 | tf_op jit(solution)/shard_map/ppermute | solution.py:667
  38.1 5.0 %collective-permute-start.4 = (bf16[272,128]{1,0:T(8,128)(2,1)S(1)}, bf16[272,128]{1,0:T(8,128)(2,1)S(1)}, u32[]{:S(2)}, u32[]{:S(2)}) collective-permute-start(bf16[272,128]{1,0:T(8,128)(2,1)S(1)} %get-tuple-element.53), channel_id=1, source_target_pairs={{0,1},{1,0},{2,3},{3,2},{4,5},{5,4},{6,7},{7,6},{8,9},{9,8},{10,11... | collective-permute-start | bytes 208904 | tf_op jit(solution)/shard_map/ppermute | solution.py:667
  40.5 5.3 %collective-permute-start.6 = (bf16[272,128]{1,0:T(8,128)(2,1)S(1)}, bf16[272,128]{1,0:T(8,128)(2,1)S(1)}, u32[]{:S(2)}, u32[]{:S(2)}) collective-permute-start(bf16[272,128]{1,0:T(8,128)(2,1)S(1)} %get-tuple-element.54), channel_id=1, source_target_pairs={{0,5},{1,4},{2,7},{3,6},{4,1},{5,0},{6,3},{7,2},{8,13},{9,12},{10,... | collective-permute-start | bytes 208904 | tf_op jit(solution)/shard_map/ppermute | solution.py:667
  40.8 5.4 %collective-permute-start.5 = (bf16[272,128]{1,0:T(8,128)(2,1)S(1)}, bf16[272,128]{1,0:T(8,128)(2,1)S(1)}, u32[]{:S(2)}, u32[]{:S(2)}) collective-permute-start(bf16[272,128]{1,0:T(8,128)(2,1)S(1)} %get-tuple-element.55), channel_id=1, source_target_pairs={{0,4},{1,5},{2,6},{3,7},{4,0},{5,1},{6,2},{7,3},{8,12},{9,13},{10,... | collective-permute-start | bytes 208904 | tf_op jit(solution)/shard_map/ppermute | solution.py:667
  43.0 7.6 %collective-permute-start.14 = (bf16[136,128]{1,0:T(8,128)(2,1)S(1)}, bf16[136,128]{1,0:T(8,128)(2,1)S(1)}, u32[]{:S(2)}, u32[]{:S(2)}) collective-permute-start(bf16[136,128]{1,0:T(8,128)(2,1)S(1)} %get-tuple-element.64), channel_id=1, source_target_pairs={{0,30},{2,4},{4,2},{6,8},{8,6},{10,12},{12,10},{14,16},{16,14},{18... | collective-permute-start | bytes 104456 | tf_op jit(solution)/shard_map/ppermute | solution.py:647
  46.2 7.1 %collective-permute-start.9 = (bf16[272,128]{1,0:T(8,128)(2,1)S(1)}, bf16[272,128]{1,0:T(8,128)(2,1)S(1)}, u32[]{:S(2)}, u32[]{:S(2)}) collective-permute-start(bf16[272,128]{1,0:T(8,128)(2,1)S(1)} %fusion.32), channel_id=1, source_target_pairs={{0,24},{1,25},{2,26},{3,27},{4,28},{5,29},{6,30},{7,31},{8,16},{9,... | collective-permute-start | bytes 208904 | tf_op jit(solution)/shard_map/ppermute | solution.py:667
  50.0 5.6 %collective-permute-start.8 = (bf16[272,128]{1,0:T(8,128)(2,1)S(1)}, bf16[272,128]{1,0:T(8,128)(2,1)S(1)}, u32[]{:S(2)}, u32[]{:S(2)}) collective-permute-start(bf16[272,128]{1,0:T(8,128)(2,1)S(1)} %fusion.32), channel_id=1, source_target_pairs={{0,16},{1,17},{2,18},{3,19},{4,20},{5,21},{6,22},{7,23},{8,24},{9,... | collective-permute-start | bytes 208904 | tf_op jit(solution)/shard_map/ppermute | solution.py:667
  50.0 5.7 %collective-permute-start.7 = (bf16[272,128]{1,0:T(8,128)(2,1)S(1)}, bf16[272,128]{1,0:T(8,128)(2,1)S(1)}, u32[]{:S(2)}, u32[]{:S(2)}) collective-permute-start(bf16[272,128]{1,0:T(8,128)(2,1)S(1)} %fusion.32), channel_id=1, source_target_pairs={{0,8},{1,9},{2,10},{3,11},{4,12},{5,13},{6,14},{7,15},{8,0},{9,1},... | collective-permute-start | bytes 208904 | tf_op jit(solution)/shard_map/ppermute | solution.py:667
  50.6 1.2 %collective-permute-start.13 = (bf16[136,128]{1,0:T(8,128)(2,1)S(1)}, bf16[136,128]{1,0:T(8,128)(2,1)S(1)}, u32[]{:S(2)}, u32[]{:S(2)}) collective-permute-start(bf16[136,128]{1,0:T(8,128)(2,1)S(1)} %get-tuple-element.65), channel_id=1, source_target_pairs={{0,2},{1,3},{2,0},{3,1},{4,6},{5,7},{6,4},{7,5},{8,10},{9,11},{10,... | collective-permute-start | bytes 104456 | tf_op jit(solution)/shard_map/ppermute | solution.py:667
  51.9 7.4 %collective-permute-start.15 = (bf16[96,128]{1,0:T(8,128)(2,1)S(1)}, bf16[96,128]{1,0:T(8,128)(2,1)S(1)}, u32[]{:S(2)}, u32[]{:S(2)}) collective-permute-start(bf16[96,128]{1,0:T(8,128)(2,1)S(1)} %fusion.41), channel_id=1, source_target_pairs={{0,1},{1,0},{2,3},{3,2},{4,5},{5,4},{6,7},{7,6},{8,9},{9,8},{10,11... | collective-permute-start | bytes 73736 | tf_op jit(solution)/shard_map/ppermute | solution.py:667
  55.7 6.3 %collective-permute-start.12 = (bf16[272,128]{1,0:T(8,128)(2,1)S(1)}, bf16[272,128]{1,0:T(8,128)(2,1)S(1)}, u32[]{:S(2)}, u32[]{:S(2)}) collective-permute-start(bf16[272,128]{1,0:T(8,128)(2,1)S(1)} %add_convert_fusion), channel_id=1, source_target_pairs={{0,5},{1,4},{2,7},{3,6},{4,1},{5,0},{6,3},{7,2},{8,13},{9,12},{10,... | collective-permute-start | bytes 208904 | tf_op jit(solution)/shard_map/ppermute | solution.py:667
  57.4 4.6 %collective-permute-start.11 = (bf16[272,128]{1,0:T(8,128)(2,1)S(1)}, bf16[272,128]{1,0:T(8,128)(2,1)S(1)}, u32[]{:S(2)}, u32[]{:S(2)}) collective-permute-start(bf16[272,128]{1,0:T(8,128)(2,1)S(1)} %add_convert_fusion), channel_id=1, source_target_pairs={{0,4},{1,5},{2,6},{3,7},{4,0},{5,1},{6,2},{7,3},{8,12},{9,13},{10,... | collective-permute-start | bytes 208904 | tf_op jit(solution)/shard_map/ppermute | solution.py:667
  58.5 4.3 %collective-permute-start.10 = (bf16[272,128]{1,0:T(8,128)(2,1)S(1)}, bf16[272,128]{1,0:T(8,128)(2,1)S(1)}, u32[]{:S(2)}, u32[]{:S(2)}) collective-permute-start(bf16[272,128]{1,0:T(8,128)(2,1)S(1)} %add_convert_fusion), channel_id=1, source_target_pairs={{0,1},{1,0},{2,3},{3,2},{4,5},{5,4},{6,7},{7,6},{8,9},{9,8},{10,11... | collective-permute-start | bytes 208904 | tf_op jit(solution)/shard_map/ppermute | solution.py:667
  62.9 1.6 %collective-permute-start.16 = (bf16[1088,128]{1,0:T(8,128)(2,1)S(1)}, bf16[1088,128]{1,0:T(8,128)(2,1)S(1)}, u32[]{:S(2)}, u32[]{:S(2)}) collective-permute-start(bf16[1088,128]{1,0:T(8,128)(2,1)S(1)} %pad_maximum_fusion.1.own), channel_id=1, source_target_pairs={{0,2},{1,3},{2,0},{3,1},{4,6},{5,7},{6,4},{7,5},{8,10},{9,11},{10,... | collective-permute-start | bytes 835592 | tf_op jit(solution)/shard_map/ppermute | solution.py:667
  (5 other events, 20.1 us)

commit v8 on v7

--- a/solution.py
+++ b/solution.py
@@ -21,7 +21,7 @@
 PACK_LIMIT = 62 * 1024 * 1024
 F32 = jnp.float32
 BF16 = jnp.bfloat16
-FIRST_STEP = 19
+FIRST_STEP = 57
 SECOND_STEP = 17
 BACK_STEP = 45
 TAP_STEP = 9

time: 65.8 us -> 65.9 us (level)
  starting transfers between devices: 22.7 us -> 23.6 us
where the time goes in v8:
time: 65.9 us; the launch traced here: 65.7 us
  Pallas kernels  25.1 us (38%)
  starting transfers between devices  23.6 us (36%)
  waiting for transfers between devices  14.7 us (22%)
  between operations  1.09 us (2%)
    pallas_call x1, Pallas kernels, on_device(): pl.pallas_call(functools.partial(tile_kernel, sizes), out_shape=(jax.Shap...  19.5 us
    ppermute x15, starting transfers between devices, swap(): return lax.ppermute(values, self.axes, pairs)  17.3 us
    ppermute x15, waiting for transfers between devices, swap(): return lax.ppermute(values, self.axes, pairs)  10.8 us
    ppermute x2, starting transfers between devices, lon_neighbours(): across = lax.ppermute(across, 'lon', pairs)  6.31 us
    ppermute x2, waiting for transfers between devices, lon_neighbours(): across = lax.ppermute(across, 'lon', pairs)  3.98 us
    pallas_call x1, Pallas kernels, finish(): pl.pallas_call(state_kernel, out_shape=jax.ShapeDtypeStruct(tile, BF16),...  2.75 us
    pallas_call x1, Pallas kernels, on_device(): pl.pallas_call(pack_kernel, out_shape=jax.ShapeDtypeStruct(packed, BF16),...  1.7 us
  transfers between devices with their start and end apart: 17, of which 10 were waited for; matrix products, arithmetic and copies ran while one was open for 1% of the time, Pallas kernels for 4%

profile of v8, /device:TPU:0, one launch (start us, length us, event | category | flops | bytes accessed | tf_op | source)
XLA Modules:
  0.0 65.7 jit_solution(10332146907913678969)
XLA Ops:
  0.7 1.7 %shard_map.203 = bf16[1,320,128]{2,1,0:T(8,128)(2,1)} custom-call(s32[1]{0:T(128)} %bitcast.7.lat, bf16[45,24,128]{2,1,0:T(8,128)(2,1)} %state_tile.1, bf16[45,24,128]{2,1,0:T(8,128)(2,1)} %cotangent.3, s32[24,45]{1,0:T(8,128)} %bitcast.61), custom_call_target="tpu_custom_call" | custom-call | tf_op jit(solution)/shard_map/pallas_call | solution.py:767
  2.4 3.0 %collective-permute-start = (bf16[320,128]{1,0:T(8,128)(2,1)}, bf16[320,128]{1,0:T(8,128)(2,1)S(1)}, u32[]{:S(2)}, u32[]{:S(2)}) collective-permute-start(bf16[320,128]{1,0:T(8,128)(2,1)} %bitcast.69), channel_id=1, source_target_pairs={{0,1},{1,0},{2,3},{3,2},{4,5},{5,4},{6,7},{7,6},{8,9},{9,8},{10,11... | collective-permute-start | bytes 245768 | tf_op jit(solution)/shard_map/ppermute | solution.py:667
  5.6 2.5 %collective-permute-done = bf16[320,128]{1,0:T(8,128)(2,1)S(1)} collective-permute-done((bf16[320,128]{1,0:T(8,128)(2,1)}, bf16[320,128]{1,0:T(8,128)(2,1)S(1)}, u32[]{:S(2)}, u32[]{:S(2)}) %collective-permute-start) | collective-permute-done | bytes 81952 | tf_op jit(solution)/shard_map/ppermute | solution.py:667
  8.1 0.2 fusion.18
  8.6 3.4 %collective-permute-start.2 = (bf16[664,128]{1,0:T(8,128)(2,1)S(1)}, bf16[664,128]{1,0:T(8,128)(2,1)S(1)}, u32[]{:S(2)}, u32[]{:S(2)}) collective-permute-start(bf16[664,128]{1,0:T(8,128)(2,1)S(1)} %get-tuple-element.47), channel_id=1, source_target_pairs={{0,30},{2,4},{4,2},{6,8},{8,6},{10,12},{12,10},{14,16},{16,14},{18... | collective-permute-start | bytes 509960 | tf_op jit(solution)/shard_map/ppermute | solution.py:647
  12.2 4.0 %collective-permute-done.2.across = bf16[664,128]{1,0:T(8,128)(2,1)S(1)} collective-permute-done((bf16[664,128]{1,0:T(8,128)(2,1)S(1)}, bf16[664,128]{1,0:T(8,128)(2,1)S(1)}, u32[]{:S(2)}, u32[]{:S(2)}) %collective-permute-start.2) | collective-permute-done | bytes 170016 | tf_op jit(solution)/shard_map/ppermute | solution.py:647
  16.2 19.5 %shard_map.204 = (bf16[45,24,128]{2,1,0:T(8,128)(2,1)}, bf16[45,24,128]{2,1,0:T(8,128)(2,1)S(1)}, bf16[45,24,128]{2,1,0:T(8,128)(2,1)S(1)}, bf16[2,136,128]{2,1,0:T(8,128)(2,1)S(1)}, bf16[2176,128]{1,0:T(8,128)(2,1)S(1)}) custom-call(s32[6]{0:T(128)S(1)} %stack.49.starts, bf16[45,24,128]{2,1,0:T(8,128)(2,1)S(1)} %copy-done, ...), custom_call_target="tpu_custom_call" | custom-call | flops 2013265920 | bytes 2211840 | tf_op jit(solution)/shard_map/pallas_call | solution.py:864
  36.1 1.3 %collective-permute-done.3 = bf16[1088,128]{1,0:T(8,128)(2,1)S(1)} collective-permute-done((bf16[1088,128]{1,0:T(8,128)(2,1)S(1)}, bf16[1088,128]{1,0:T(8,128)(2,1)S(1)}, u32[]{:S(2)}, u32[]{:S(2)}) %collective-permute-start.3) | collective-permute-done | bytes 278560 | tf_op jit(solution)/shard_map/ppermute | solution.py:667
  37.5 3.1 %collective-permute-start.4 = (bf16[272,128]{1,0:T(8,128)(2,1)S(1)}, bf16[272,128]{1,0:T(8,128)(2,1)S(1)}, u32[]{:S(2)}, u32[]{:S(2)}) collective-permute-start(bf16[272,128]{1,0:T(8,128)(2,1)S(1)} %get-tuple-element.53), channel_id=1, source_target_pairs={{0,1},{1,0},{2,3},{3,2},{4,5},{5,4},{6,7},{7,6},{8,9},{9,8},{10,11... | collective-permute-start | bytes 208904 | tf_op jit(solution)/shard_map/ppermute | solution.py:667
  40.8 1.4 %collective-permute-start.5 = (bf16[272,128]{1,0:T(8,128)(2,1)S(1)}, bf16[272,128]{1,0:T(8,128)(2,1)S(1)}, u32[]{:S(2)}, u32[]{:S(2)}) collective-permute-start(bf16[272,128]{1,0:T(8,128)(2,1)S(1)} %get-tuple-element.55), channel_id=1, source_target_pairs={{0,4},{1,5},{2,6},{3,7},{4,0},{5,1},{6,2},{7,3},{8,12},{9,13},{10,... | collective-permute-start | bytes 208904 | tf_op jit(solution)/shard_map/ppermute | solution.py:667
  42.2 1.0 %collective-permute-done.4 = bf16[272,128]{1,0:T(8,128)(2,1)S(1)} collective-permute-done((bf16[272,128]{1,0:T(8,128)(2,1)S(1)}, bf16[272,128]{1,0:T(8,128)(2,1)S(1)}, u32[]{:S(2)}, u32[]{:S(2)}) %collective-permute-start.4) | collective-permute-done | bytes 69664 | tf_op jit(solution)/shard_map/ppermute | solution.py:667
  43.1 2.9 %collective-permute-start.14 = (bf16[136,128]{1,0:T(8,128)(2,1)S(1)}, bf16[136,128]{1,0:T(8,128)(2,1)S(1)}, u32[]{:S(2)}, u32[]{:S(2)}) collective-permute-start(bf16[136,128]{1,0:T(8,128)(2,1)S(1)} %get-tuple-element.64), channel_id=1, source_target_pairs={{0,30},{2,4},{4,2},{6,8},{8,6},{10,12},{12,10},{14,16},{16,14},{18... | collective-permute-start | bytes 104456 | tf_op jit(solution)/shard_map/ppermute | solution.py:647
  46.2 3.8 %collective-permute-start.9 = (bf16[272,128]{1,0:T(8,128)(2,1)S(1)}, bf16[272,128]{1,0:T(8,128)(2,1)S(1)}, u32[]{:S(2)}, u32[]{:S(2)}) collective-permute-start(bf16[272,128]{1,0:T(8,128)(2,1)S(1)} %fusion.32), channel_id=1, source_target_pairs={{0,24},{1,25},{2,26},{3,27},{4,28},{5,29},{6,30},{7,31},{8,16},{9,... | collective-permute-start | bytes 208904 | tf_op jit(solution)/shard_map/ppermute | solution.py:667
  50.1 0.6 collective-permute-start.7
  50.7 1.2 %collective-permute-done.13.within = bf16[136,128]{1,0:T(8,128)(2,1)S(1)} collective-permute-done((bf16[136,128]{1,0:T(8,128)(2,1)S(1)}, bf16[136,128]{1,0:T(8,128)(2,1)S(1)}, u32[]{:S(2)}, u32[]{:S(2)}) %collective-permute-start.13) | collective-permute-done | bytes 34848 | tf_op jit(solution)/shard_map/ppermute | solution.py:667
  52.0 1.4 %collective-permute-start.15 = (bf16[96,128]{1,0:T(8,128)(2,1)S(1)}, bf16[96,128]{1,0:T(8,128)(2,1)S(1)}, u32[]{:S(2)}, u32[]{:S(2)}) collective-permute-start(bf16[96,128]{1,0:T(8,128)(2,1)S(1)} %fusion.41), channel_id=1, source_target_pairs={{0,1},{1,0},{2,3},{3,2},{4,5},{5,4},{6,7},{7,6},{8,9},{9,8},{10,11... | collective-permute-start | bytes 73736 | tf_op jit(solution)/shard_map/ppermute | solution.py:667
  53.4 2.3 %collective-permute-done.8 = bf16[272,128]{1,0:T(8,128)(2,1)S(1)} collective-permute-done((bf16[272,128]{1,0:T(8,128)(2,1)S(1)}, bf16[272,128]{1,0:T(8,128)(2,1)S(1)}, u32[]{:S(2)}, u32[]{:S(2)}) %collective-permute-start.8) | collective-permute-done | bytes 69664 | tf_op jit(solution)/shard_map/ppermute | solution.py:667
  55.8 1.7 %collective-permute-start.12 = (bf16[272,128]{1,0:T(8,128)(2,1)S(1)}, bf16[272,128]{1,0:T(8,128)(2,1)S(1)}, u32[]{:S(2)}, u32[]{:S(2)}) collective-permute-start(bf16[272,128]{1,0:T(8,128)(2,1)S(1)} %add_convert_fusion), channel_id=1, source_target_pairs={{0,5},{1,4},{2,7},{3,6},{4,1},{5,0},{6,3},{7,2},{8,13},{9,12},{10,... | collective-permute-start | bytes 208904 | tf_op jit(solution)/shard_map/ppermute | solution.py:667
  57.5 1.0 %collective-permute-start.11 = (bf16[272,128]{1,0:T(8,128)(2,1)S(1)}, bf16[272,128]{1,0:T(8,128)(2,1)S(1)}, u32[]{:S(2)}, u32[]{:S(2)}) collective-permute-start(bf16[272,128]{1,0:T(8,128)(2,1)S(1)} %add_convert_fusion), channel_id=1, source_target_pairs={{0,4},{1,5},{2,6},{3,7},{4,0},{5,1},{6,2},{7,3},{8,12},{9,13},{10,... | collective-permute-start | bytes 208904 | tf_op jit(solution)/shard_map/ppermute | solution.py:667
  58.5 0.8 %collective-permute-start.10 = (bf16[272,128]{1,0:T(8,128)(2,1)S(1)}, bf16[272,128]{1,0:T(8,128)(2,1)S(1)}, u32[]{:S(2)}, u32[]{:S(2)}) collective-permute-start(bf16[272,128]{1,0:T(8,128)(2,1)S(1)} %add_convert_fusion), channel_id=1, source_target_pairs={{0,1},{1,0},{2,3},{3,2},{4,5},{5,4},{6,7},{7,6},{8,9},{9,8},{10,11... | collective-permute-start | bytes 208904 | tf_op jit(solution)/shard_map/ppermute | solution.py:667
  59.3 2.8 %shard_map.205 = bf16[45,24,128]{2,1,0:T(8,128)(2,1)} custom-call(s32[2]{0:T(128)S(1)} %pad_add_fusion.starts, bf16[45,24,128]{2,1,0:T(8,128)(2,1)S(1)} %get-tuple-element.33.mixed, bf16[136,128]{1,0:T(8,128)(2,1)S(1)} %collective-permute-done.13.within, bf16[136,128]{1,0:T(8,128)(2,1)S(1)} %collective-permute-done.14.across, ...), custom_call_target="tpu_custom_call" | custom-call | flops 4000000000 | bytes 8000000 | tf_op jit(solution)/shard_map/pallas_call | solution.py:904
  62.1 0.7 %collective-permute-done.10 = bf16[272,128]{1,0:T(8,128)(2,1)S(1)} collective-permute-done((bf16[272,128]{1,0:T(8,128)(2,1)S(1)}, bf16[272,128]{1,0:T(8,128)(2,1)S(1)}, u32[]{:S(2)}, u32[]{:S(2)}) %collective-permute-start.10) | collective-permute-done | bytes 69664 | tf_op jit(solution)/shard_map/ppermute | solution.py:667
  63.0 1.5 %collective-permute-done.16.other = bf16[1088,128]{1,0:T(8,128)(2,1)S(1)} collective-permute-done((bf16[1088,128]{1,0:T(8,128)(2,1)S(1)}, bf16[1088,128]{1,0:T(8,128)(2,1)S(1)}, u32[]{:S(2)}, u32[]{:S(2)}) %collective-permute-start.16) | collective-permute-done | bytes 278560 | tf_op jit(solution)/shard_map/ppermute | solution.py:667
  64.6 1.1 %shard_map.206 = (f32[7,7,2,128]{3,2,1,0:T(2,128)}, f32[2,128]{1,0:T(2,128)}, f32[2,128]{1,0:T(2,128)}, f32[2,128]{1,0:T(2,128)}, f32[2,128,512]{2,1,0:T(8,128)}...) custom-call(s32[1]{0:T(128)} %bitcast.3.held, ...), custom_call_target="tpu_custom_call" | custom-call | tf_op jit(solution)/shard_map/pallas_call | solution.py:922
  (69 shorter events, 1.6 us)
Async XLA Ops:
  0.6 4.7 %copy-start.2 = (s32[45,24]{0,1:T(8,128)S(1)}, s32[45,24]{0,1:T(8,128)}, u32[]{:S(2)}) copy-start(s32[45,24]{0,1:T(8,128)} %param.13) | copy-start | bytes 12964
  0.7 4.7 %copy-start.1 = (bf16[45,24,128]{2,1,0:T(8,128)(2,1)S(1)}, bf16[45,24,128]{2,1,0:T(8,128)(2,1)}, u32[]{:S(2)}) copy-start(bf16[45,24,128]{2,1,0:T(8,128)(2,1)} %cotangent.3) | copy-start | bytes 829444
  0.7 4.8 %copy-start = (bf16[45,24,128]{2,1,0:T(8,128)(2,1)S(1)}, bf16[45,24,128]{2,1,0:T(8,128)(2,1)}, u32[]{:S(2)}) copy-start(bf16[45,24,128]{2,1,0:T(8,128)(2,1)} %state_tile.1) | copy-start | bytes 829444
  2.4 5.7 %collective-permute-start = (bf16[320,128]{1,0:T(8,128)(2,1)}, bf16[320,128]{1,0:T(8,128)(2,1)S(1)}, u32[]{:S(2)}, u32[]{:S(2)}) collective-permute-start(bf16[320,128]{1,0:T(8,128)(2,1)} %bitcast.69), channel_id=1, source_target_pairs={{0,1},{1,0},{2,3},{3,2},{4,5},{5,4},{6,7},{7,6},{8,9},{9,8},{10,11... | collective-permute-start | bytes 245768 | tf_op jit(solution)/shard_map/ppermute | solution.py:667
  8.5 7.7 %copy-start.3 = (bf16[2,128,512]{2,1,0:T(8,128)(2,1)S(1)}, bf16[2,128,512]{2,1,0:T(8,128)(2,1)}, u32[]{:S(2)}) copy-start(bf16[2,128,512]{2,1,0:T(8,128)(2,1)} %weight_in.1) | copy-start | bytes 786436
  8.5 7.7 %copy-start.4 = (bf16[2,512,128]{2,1,0:T(8,128)(2,1)S(1)}, bf16[2,512,128]{2,1,0:T(8,128)(2,1)}, u32[]{:S(2)}) copy-start(bf16[2,512,128]{2,1,0:T(8,128)(2,1)} %weight_out.1) | copy-start | bytes 786436
  8.6 7.6 %collective-permute-start.2 = (bf16[664,128]{1,0:T(8,128)(2,1)S(1)}, bf16[664,128]{1,0:T(8,128)(2,1)S(1)}, u32[]{:S(2)}, u32[]{:S(2)}) collective-permute-start(bf16[664,128]{1,0:T(8,128)(2,1)S(1)} %get-tuple-element.47), channel_id=1, source_target_pairs={{0,30},{2,4},{4,2},{6,8},{8,6},{10,12},{12,10},{14,16},{16,14},{18... | collective-permute-start | bytes 509960 | tf_op jit(solution)/shard_map/ppermute | solution.py:647
  12.0 4.2 %collective-permute-start.1 = (bf16[664,128]{1,0:T(8,128)(2,1)S(1)}, bf16[664,128]{1,0:T(8,128)(2,1)S(1)}, u32[]{:S(2)}, u32[]{:S(2)}) collective-permute-start(bf16[664,128]{1,0:T(8,128)(2,1)S(1)} %get-tuple-element.48), channel_id=1, source_target_pairs={{0,2},{1,3},{2,0},{3,1},{4,6},{5,7},{6,4},{7,5},{8,10},{9,11},{10,... | collective-permute-start | bytes 509960 | tf_op jit(solution)/shard_map/ppermute | solution.py:667
  12.0 4.2 %copy-start.9 = (f32[2,128]{1,0:T(2,128)S(1)}, f32[2,128]{1,0:T(2,128)}, u32[]{:S(2)}) copy-start(f32[2,128]{1,0:T(2,128)} %bias_out.1) | copy-start | bytes 3076
  12.0 4.2 %copy-start.10 = (f32[2,128]{1,0:T(2,128)S(1)}, f32[2,128]{1,0:T(2,128)}, u32[]{:S(2)}) copy-start(f32[2,128]{1,0:T(2,128)} %layer_scale.1) | copy-start | bytes 3076
  35.8 1.6 %collective-permute-start.3 = (bf16[1088,128]{1,0:T(8,128)(2,1)S(1)}, bf16[1088,128]{1,0:T(8,128)(2,1)S(1)}, u32[]{:S(2)}, u32[]{:S(2)}) collective-permute-start(bf16[1088,128]{1,0:T(8,128)(2,1)S(1)} %dynamic-slice_bitcast_fusion), channel_id=1, source_target_pairs={{0,2},{1,3},{2,0},{3,1},{4,6},{5,7},{6,4},{7,5},{8,10},{9,11},{10,... | collective-permute-start | bytes 835592 | tf_op jit(solution)/shard_map/ppermute | solution.py:667
  37.5 5.6 %collective-permute-start.4 = (bf16[272,128]{1,0:T(8,128)(2,1)S(1)}, bf16[272,128]{1,0:T(8,128)(2,1)S(1)}, u32[]{:S(2)}, u32[]{:S(2)}) collective-permute-start(bf16[272,128]{1,0:T(8,128)(2,1)S(1)} %get-tuple-element.53), channel_id=1, source_target_pairs={{0,1},{1,0},{2,3},{3,2},{4,5},{5,4},{6,7},{7,6},{8,9},{9,8},{10,11... | collective-permute-start | bytes 208904 | tf_op jit(solution)/shard_map/ppermute | solution.py:667
  40.6 5.4 %collective-permute-start.6 = (bf16[272,128]{1,0:T(8,128)(2,1)S(1)}, bf16[272,128]{1,0:T(8,128)(2,1)S(1)}, u32[]{:S(2)}, u32[]{:S(2)}) collective-permute-start(bf16[272,128]{1,0:T(8,128)(2,1)S(1)} %get-tuple-element.54), channel_id=1, source_target_pairs={{0,5},{1,4},{2,7},{3,6},{4,1},{5,0},{6,3},{7,2},{8,13},{9,12},{10,... | collective-permute-start | bytes 208904 | tf_op jit(solution)/shard_map/ppermute | solution.py:667
  40.8 5.4 %collective-permute-start.5 = (bf16[272,128]{1,0:T(8,128)(2,1)S(1)}, bf16[272,128]{1,0:T(8,128)(2,1)S(1)}, u32[]{:S(2)}, u32[]{:S(2)}) collective-permute-start(bf16[272,128]{1,0:T(8,128)(2,1)S(1)} %get-tuple-element.55), channel_id=1, source_target_pairs={{0,4},{1,5},{2,6},{3,7},{4,0},{5,1},{6,2},{7,3},{8,12},{9,13},{10,... | collective-permute-start | bytes 208904 | tf_op jit(solution)/shard_map/ppermute | solution.py:667
  43.1 7.6 %collective-permute-start.14 = (bf16[136,128]{1,0:T(8,128)(2,1)S(1)}, bf16[136,128]{1,0:T(8,128)(2,1)S(1)}, u32[]{:S(2)}, u32[]{:S(2)}) collective-permute-start(bf16[136,128]{1,0:T(8,128)(2,1)S(1)} %get-tuple-element.64), channel_id=1, source_target_pairs={{0,30},{2,4},{4,2},{6,8},{8,6},{10,12},{12,10},{14,16},{16,14},{18... | collective-permute-start | bytes 104456 | tf_op jit(solution)/shard_map/ppermute | solution.py:647
  46.2 7.1 %collective-permute-start.9 = (bf16[272,128]{1,0:T(8,128)(2,1)S(1)}, bf16[272,128]{1,0:T(8,128)(2,1)S(1)}, u32[]{:S(2)}, u32[]{:S(2)}) collective-permute-start(bf16[272,128]{1,0:T(8,128)(2,1)S(1)} %fusion.32), channel_id=1, source_target_pairs={{0,24},{1,25},{2,26},{3,27},{4,28},{5,29},{6,30},{7,31},{8,16},{9,... | collective-permute-start | bytes 208904 | tf_op jit(solution)/shard_map/ppermute | solution.py:667
  50.1 5.6 %collective-permute-start.8 = (bf16[272,128]{1,0:T(8,128)(2,1)S(1)}, bf16[272,128]{1,0:T(8,128)(2,1)S(1)}, u32[]{:S(2)}, u32[]{:S(2)}) collective-permute-start(bf16[272,128]{1,0:T(8,128)(2,1)S(1)} %fusion.32), channel_id=1, source_target_pairs={{0,16},{1,17},{2,18},{3,19},{4,20},{5,21},{6,22},{7,23},{8,24},{9,... | collective-permute-start | bytes 208904 | tf_op jit(solution)/shard_map/ppermute | solution.py:667
  50.1 5.7 %collective-permute-start.7 = (bf16[272,128]{1,0:T(8,128)(2,1)S(1)}, bf16[272,128]{1,0:T(8,128)(2,1)S(1)}, u32[]{:S(2)}, u32[]{:S(2)}) collective-permute-start(bf16[272,128]{1,0:T(8,128)(2,1)S(1)} %fusion.32), channel_id=1, source_target_pairs={{0,8},{1,9},{2,10},{3,11},{4,12},{5,13},{6,14},{7,15},{8,0},{9,1},... | collective-permute-start | bytes 208904 | tf_op jit(solution)/shard_map/ppermute | solution.py:667
  50.7 1.2 %collective-permute-start.13 = (bf16[136,128]{1,0:T(8,128)(2,1)S(1)}, bf16[136,128]{1,0:T(8,128)(2,1)S(1)}, u32[]{:S(2)}, u32[]{:S(2)}) collective-permute-start(bf16[136,128]{1,0:T(8,128)(2,1)S(1)} %get-tuple-element.65), channel_id=1, source_target_pairs={{0,2},{1,3},{2,0},{3,1},{4,6},{5,7},{6,4},{7,5},{8,10},{9,11},{10,... | collective-permute-start | bytes 104456 | tf_op jit(solution)/shard_map/ppermute | solution.py:667
  52.0 7.4 %collective-permute-start.15 = (bf16[96,128]{1,0:T(8,128)(2,1)S(1)}, bf16[96,128]{1,0:T(8,128)(2,1)S(1)}, u32[]{:S(2)}, u32[]{:S(2)}) collective-permute-start(bf16[96,128]{1,0:T(8,128)(2,1)S(1)} %fusion.41), channel_id=1, source_target_pairs={{0,1},{1,0},{2,3},{3,2},{4,5},{5,4},{6,7},{7,6},{8,9},{9,8},{10,11... | collective-permute-start | bytes 73736 | tf_op jit(solution)/shard_map/ppermute | solution.py:667
  55.8 6.3 %collective-permute-start.12 = (bf16[272,128]{1,0:T(8,128)(2,1)S(1)}, bf16[272,128]{1,0:T(8,128)(2,1)S(1)}, u32[]{:S(2)}, u32[]{:S(2)}) collective-permute-start(bf16[272,128]{1,0:T(8,128)(2,1)S(1)} %add_convert_fusion), channel_id=1, source_target_pairs={{0,5},{1,4},{2,7},{3,6},{4,1},{5,0},{6,3},{7,2},{8,13},{9,12},{10,... | collective-permute-start | bytes 208904 | tf_op jit(solution)/shard_map/ppermute | solution.py:667
  57.5 4.6 %collective-permute-start.11 = (bf16[272,128]{1,0:T(8,128)(2,1)S(1)}, bf16[272,128]{1,0:T(8,128)(2,1)S(1)}, u32[]{:S(2)}, u32[]{:S(2)}) collective-permute-start(bf16[272,128]{1,0:T(8,128)(2,1)S(1)} %add_convert_fusion), channel_id=1, source_target_pairs={{0,4},{1,5},{2,6},{3,7},{4,0},{5,1},{6,2},{7,3},{8,12},{9,13},{10,... | collective-permute-start | bytes 208904 | tf_op jit(solution)/shard_map/ppermute | solution.py:667
  58.5 4.3 %collective-permute-start.10 = (bf16[272,128]{1,0:T(8,128)(2,1)S(1)}, bf16[272,128]{1,0:T(8,128)(2,1)S(1)}, u32[]{:S(2)}, u32[]{:S(2)}) collective-permute-start(bf16[272,128]{1,0:T(8,128)(2,1)S(1)} %add_convert_fusion), channel_id=1, source_target_pairs={{0,1},{1,0},{2,3},{3,2},{4,5},{5,4},{6,7},{7,6},{8,9},{9,8},{10,11... | collective-permute-start | bytes 208904 | tf_op jit(solution)/shard_map/ppermute | solution.py:667
  63.0 1.6 %collective-permute-start.16 = (bf16[1088,128]{1,0:T(8,128)(2,1)S(1)}, bf16[1088,128]{1,0:T(8,128)(2,1)S(1)}, u32[]{:S(2)}, u32[]{:S(2)}) collective-permute-start(bf16[1088,128]{1,0:T(8,128)(2,1)S(1)} %pad_maximum_fusion.1.own), channel_id=1, source_target_pairs={{0,2},{1,3},{2,0},{3,1},{4,6},{5,7},{6,4},{7,5},{8,10},{9,11},{10,... | collective-permute-start | bytes 835592 | tf_op jit(solution)/shard_map/ppermute | solution.py:667
  (5 other events, 20.1 us)

commit v9 on v8

--- a/solution.py
+++ b/solution.py
@@ -24,7 +24,7 @@
 FIRST_STEP = 57
 SECOND_STEP = 17
 BACK_STEP = 45
-TAP_STEP = 9
+TAP_STEP = 15
 STATE_AT = 11
 FIELD_AT = 8
 INNER_AT = 3
@@ -421,12 +421,10 @@
         sums[1, 1] += fold(own_branch)
         sums[1, 2] += fold(own_lifted * normed)
         sums[1, 3] += fold(own_lifted)
-        wide = jnp.concatenate([inside] * (hidden.shape[1] // channels), axis=1)
-        hidden_sums[1] += fold(grad_hidden.astype(F32) * wide)
         spots = pl.ds(pl.multiple_of(step * cells, cells), cells)
         active_all[spots] = active
         hidden_all[spots] = grad_hidden
-        lifted_all[spots] = (lifted * inside).astype(BF16)
+        lifted_all[spots] = jnp.concatenate([lifted * inside, inside], axis=1).astype(BF16)
         branch_grad_all[spots] = own_branch.astype(BF16)
         return carry
 
@@ -503,6 +501,9 @@
     for layer, (lifted, grad_hidden, active, grad_branch) in enumerate(operands):
         at = layer * (grads_out.shape[0] // BLOCKS)
         grad_in = dot_rows(lifted, grad_hidden)
+        if layer:
+            hidden_sums[1, 0:1] = grad_in[channels : channels + 1]
+            grad_in = grad_in[:channels]
         for group in range(groups):
             grads_out[pl.ds(at + group * channels, channels), :] = grad_in[
                 :, group * channels : (group + 1) * channels
@@ -851,7 +852,7 @@
         pltpu.VMEM(tile, F32),
         pltpu.VMEM((all_cells, hidden_units), BF16),
         pltpu.VMEM((all_cells, hidden_units), BF16),
-        pltpu.VMEM((all_cells, channels), BF16),
+        pltpu.VMEM((all_cells, 2 * channels), BF16),
         pltpu.VMEM((all_cells, channels), BF16),
         pltpu.VMEM((BLOCKS, 5, 8, channels), F32),
         pltpu.VMEM((BLOCKS, 8, hidden_units), F32),

time: 65.9 us -> 65.5 us (level)
  no operation moved by 1% of the time
where the time goes in v9:
time: 65.5 us; the launch traced here: 65.3 us
  Pallas kernels  24.7 us (38%)
  starting transfers between devices  23.6 us (36%)
  waiting for transfers between devices  14.7 us (22%)
  between operations  1.09 us (2%)
    pallas_call x1, Pallas kernels, on_device(): pl.pallas_call(functools.partial(tile_kernel, sizes), out_shape=(jax.Shap...  19.1 us
    ppermute x15, starting transfers between devices, swap(): return lax.ppermute(values, self.axes, pairs)  17.3 us
    ppermute x15, waiting for transfers between devices, swap(): return lax.ppermute(values, self.axes, pairs)  10.8 us
    ppermute x2, starting transfers between devices, lon_neighbours(): across = lax.ppermute(across, 'lon', pairs)  6.31 us
    ppermute x2, waiting for transfers between devices, lon_neighbours(): across = lax.ppermute(across, 'lon', pairs)  3.98 us
    pallas_call x1, Pallas kernels, finish(): pl.pallas_call(state_kernel, out_shape=jax.ShapeDtypeStruct(tile, BF16),...  2.75 us
    pallas_call x1, Pallas kernels, on_device(): pl.pallas_call(pack_kernel, out_shape=jax.ShapeDtypeStruct(packed, BF16),...  1.7 us
  transfers between devices with their start and end apart: 17, of which 10 were waited for; matrix products, arithmetic and copies ran while one was open for 1% of the time, Pallas kernels for 4%

profile of v9, /device:TPU:0, one launch (start us, length us, event | category | flops | bytes accessed | tf_op | source)
XLA Modules:
  0.0 65.3 jit_solution(4050654531611119514)
XLA Ops:
  0.7 1.7 %shard_map.203 = bf16[1,320,128]{2,1,0:T(8,128)(2,1)} custom-call(s32[1]{0:T(128)} %bitcast.7.lat, bf16[45,24,128]{2,1,0:T(8,128)(2,1)} %state_tile.1, bf16[45,24,128]{2,1,0:T(8,128)(2,1)} %cotangent.3, s32[24,45]{1,0:T(8,128)} %bitcast.61), custom_call_target="tpu_custom_call" | custom-call | tf_op jit(solution)/shard_map/pallas_call | solution.py:768
  2.4 3.0 %collective-permute-start = (bf16[320,128]{1,0:T(8,128)(2,1)}, bf16[320,128]{1,0:T(8,128)(2,1)S(1)}, u32[]{:S(2)}, u32[]{:S(2)}) collective-permute-start(bf16[320,128]{1,0:T(8,128)(2,1)} %bitcast.69), channel_id=1, source_target_pairs={{0,1},{1,0},{2,3},{3,2},{4,5},{5,4},{6,7},{7,6},{8,9},{9,8},{10,11... | collective-permute-start | bytes 245768 | tf_op jit(solution)/shard_map/ppermute | solution.py:668
  5.6 2.5 %collective-permute-done = bf16[320,128]{1,0:T(8,128)(2,1)S(1)} collective-permute-done((bf16[320,128]{1,0:T(8,128)(2,1)}, bf16[320,128]{1,0:T(8,128)(2,1)S(1)}, u32[]{:S(2)}, u32[]{:S(2)}) %collective-permute-start) | collective-permute-done | bytes 81952 | tf_op jit(solution)/shard_map/ppermute | solution.py:668
  8.1 0.2 fusion.18
  8.6 3.4 %collective-permute-start.2 = (bf16[664,128]{1,0:T(8,128)(2,1)S(1)}, bf16[664,128]{1,0:T(8,128)(2,1)S(1)}, u32[]{:S(2)}, u32[]{:S(2)}) collective-permute-start(bf16[664,128]{1,0:T(8,128)(2,1)S(1)} %get-tuple-element.47), channel_id=1, source_target_pairs={{0,30},{2,4},{4,2},{6,8},{8,6},{10,12},{12,10},{14,16},{16,14},{18... | collective-permute-start | bytes 509960 | tf_op jit(solution)/shard_map/ppermute | solution.py:648
  12.2 4.0 %collective-permute-done.2.across = bf16[664,128]{1,0:T(8,128)(2,1)S(1)} collective-permute-done((bf16[664,128]{1,0:T(8,128)(2,1)S(1)}, bf16[664,128]{1,0:T(8,128)(2,1)S(1)}, u32[]{:S(2)}, u32[]{:S(2)}) %collective-permute-start.2) | collective-permute-done | bytes 170016 | tf_op jit(solution)/shard_map/ppermute | solution.py:648
  16.2 19.1 %shard_map.204 = (bf16[45,24,128]{2,1,0:T(8,128)(2,1)}, bf16[45,24,128]{2,1,0:T(8,128)(2,1)S(1)}, bf16[45,24,128]{2,1,0:T(8,128)(2,1)S(1)}, bf16[2,136,128]{2,1,0:T(8,128)(2,1)S(1)}, bf16[2176,128]{1,0:T(8,128)(2,1)S(1)}) custom-call(s32[6]{0:T(128)S(1)} %stack.49.starts, bf16[45,24,128]{2,1,0:T(8,128)(2,1)S(1)} %copy-done, ...), custom_call_target="tpu_custom_call" | custom-call | flops 2013265920 | bytes 2211840 | tf_op jit(solution)/shard_map/pallas_call | solution.py:865
  35.7 1.3 %collective-permute-done.3 = bf16[1088,128]{1,0:T(8,128)(2,1)S(1)} collective-permute-done((bf16[1088,128]{1,0:T(8,128)(2,1)S(1)}, bf16[1088,128]{1,0:T(8,128)(2,1)S(1)}, u32[]{:S(2)}, u32[]{:S(2)}) %collective-permute-start.3) | collective-permute-done | bytes 278560 | tf_op jit(solution)/shard_map/ppermute | solution.py:668
  37.1 3.1 %collective-permute-start.4 = (bf16[272,128]{1,0:T(8,128)(2,1)S(1)}, bf16[272,128]{1,0:T(8,128)(2,1)S(1)}, u32[]{:S(2)}, u32[]{:S(2)}) collective-permute-start(bf16[272,128]{1,0:T(8,128)(2,1)S(1)} %get-tuple-element.53), channel_id=1, source_target_pairs={{0,1},{1,0},{2,3},{3,2},{4,5},{5,4},{6,7},{7,6},{8,9},{9,8},{10,11... | collective-permute-start | bytes 208904 | tf_op jit(solution)/shard_map/ppermute | solution.py:668
  40.4 1.4 %collective-permute-start.5 = (bf16[272,128]{1,0:T(8,128)(2,1)S(1)}, bf16[272,128]{1,0:T(8,128)(2,1)S(1)}, u32[]{:S(2)}, u32[]{:S(2)}) collective-permute-start(bf16[272,128]{1,0:T(8,128)(2,1)S(1)} %get-tuple-element.55), channel_id=1, source_target_pairs={{0,4},{1,5},{2,6},{3,7},{4,0},{5,1},{6,2},{7,3},{8,12},{9,13},{10,... | collective-permute-start | bytes 208904 | tf_op jit(solution)/shard_map/ppermute | solution.py:668
  41.7 1.0 %collective-permute-done.4 = bf16[272,128]{1,0:T(8,128)(2,1)S(1)} collective-permute-done((bf16[272,128]{1,0:T(8,128)(2,1)S(1)}, bf16[272,128]{1,0:T(8,128)(2,1)S(1)}, u32[]{:S(2)}, u32[]{:S(2)}) %collective-permute-start.4) | collective-permute-done | bytes 69664 | tf_op jit(solution)/shard_map/ppermute | solution.py:668
  42.7 2.9 %collective-permute-start.14 = (bf16[136,128]{1,0:T(8,128)(2,1)S(1)}, bf16[136,128]{1,0:T(8,128)(2,1)S(1)}, u32[]{:S(2)}, u32[]{:S(2)}) collective-permute-start(bf16[136,128]{1,0:T(8,128)(2,1)S(1)} %get-tuple-element.64), channel_id=1, source_target_pairs={{0,30},{2,4},{4,2},{6,8},{8,6},{10,12},{12,10},{14,16},{16,14},{18... | collective-permute-start | bytes 104456 | tf_op jit(solution)/shard_map/ppermute | solution.py:648
  45.8 3.8 %collective-permute-start.9 = (bf16[272,128]{1,0:T(8,128)(2,1)S(1)}, bf16[272,128]{1,0:T(8,128)(2,1)S(1)}, u32[]{:S(2)}, u32[]{:S(2)}) collective-permute-start(bf16[272,128]{1,0:T(8,128)(2,1)S(1)} %fusion.32), channel_id=1, source_target_pairs={{0,24},{1,25},{2,26},{3,27},{4,28},{5,29},{6,30},{7,31},{8,16},{9,... | collective-permute-start | bytes 208904 | tf_op jit(solution)/shard_map/ppermute | solution.py:668
  49.7 0.6 collective-permute-start.7
  50.3 1.2 %collective-permute-done.13.within = bf16[136,128]{1,0:T(8,128)(2,1)S(1)} collective-permute-done((bf16[136,128]{1,0:T(8,128)(2,1)S(1)}, bf16[136,128]{1,0:T(8,128)(2,1)S(1)}, u32[]{:S(2)}, u32[]{:S(2)}) %collective-permute-start.13) | collective-permute-done | bytes 34848 | tf_op jit(solution)/shard_map/ppermute | solution.py:668
  51.5 1.4 %collective-permute-start.15 = (bf16[96,128]{1,0:T(8,128)(2,1)S(1)}, bf16[96,128]{1,0:T(8,128)(2,1)S(1)}, u32[]{:S(2)}, u32[]{:S(2)}) collective-permute-start(bf16[96,128]{1,0:T(8,128)(2,1)S(1)} %fusion.41), channel_id=1, source_target_pairs={{0,1},{1,0},{2,3},{3,2},{4,5},{5,4},{6,7},{7,6},{8,9},{9,8},{10,11... | collective-permute-start | bytes 73736 | tf_op jit(solution)/shard_map/ppermute | solution.py:668
  53.0 2.3 %collective-permute-done.8 = bf16[272,128]{1,0:T(8,128)(2,1)S(1)} collective-permute-done((bf16[272,128]{1,0:T(8,128)(2,1)S(1)}, bf16[272,128]{1,0:T(8,128)(2,1)S(1)}, u32[]{:S(2)}, u32[]{:S(2)}) %collective-permute-start.8) | collective-permute-done | bytes 69664 | tf_op jit(solution)/shard_map/ppermute | solution.py:668
  55.4 1.7 %collective-permute-start.12 = (bf16[272,128]{1,0:T(8,128)(2,1)S(1)}, bf16[272,128]{1,0:T(8,128)(2,1)S(1)}, u32[]{:S(2)}, u32[]{:S(2)}) collective-permute-start(bf16[272,128]{1,0:T(8,128)(2,1)S(1)} %add_convert_fusion), channel_id=1, source_target_pairs={{0,5},{1,4},{2,7},{3,6},{4,1},{5,0},{6,3},{7,2},{8,13},{9,12},{10,... | collective-permute-start | bytes 208904 | tf_op jit(solution)/shard_map/ppermute | solution.py:668
  57.1 1.0 %collective-permute-start.11 = (bf16[272,128]{1,0:T(8,128)(2,1)S(1)}, bf16[272,128]{1,0:T(8,128)(2,1)S(1)}, u32[]{:S(2)}, u32[]{:S(2)}) collective-permute-start(bf16[272,128]{1,0:T(8,128)(2,1)S(1)} %add_convert_fusion), channel_id=1, source_target_pairs={{0,4},{1,5},{2,6},{3,7},{4,0},{5,1},{6,2},{7,3},{8,12},{9,13},{10,... | collective-permute-start | bytes 208904 | tf_op jit(solution)/shard_map/ppermute | solution.py:668
  58.1 0.8 %collective-permute-start.10 = (bf16[272,128]{1,0:T(8,128)(2,1)S(1)}, bf16[272,128]{1,0:T(8,128)(2,1)S(1)}, u32[]{:S(2)}, u32[]{:S(2)}) collective-permute-start(bf16[272,128]{1,0:T(8,128)(2,1)S(1)} %add_convert_fusion), channel_id=1, source_target_pairs={{0,1},{1,0},{2,3},{3,2},{4,5},{5,4},{6,7},{7,6},{8,9},{9,8},{10,11... | collective-permute-start | bytes 208904 | tf_op jit(solution)/shard_map/ppermute | solution.py:668
  58.9 2.8 %shard_map.205 = bf16[45,24,128]{2,1,0:T(8,128)(2,1)} custom-call(s32[2]{0:T(128)S(1)} %pad_add_fusion.starts, bf16[45,24,128]{2,1,0:T(8,128)(2,1)S(1)} %get-tuple-element.33.mixed, bf16[136,128]{1,0:T(8,128)(2,1)S(1)} %collective-permute-done.13.within, bf16[136,128]{1,0:T(8,128)(2,1)S(1)} %collective-permute-done.14.across, ...), custom_call_target="tpu_custom_call" | custom-call | flops 4000000000 | bytes 8000000 | tf_op jit(solution)/shard_map/pallas_call | solution.py:905
  61.7 0.7 %collective-permute-done.10 = bf16[272,128]{1,0:T(8,128)(2,1)S(1)} collective-permute-done((bf16[272,128]{1,0:T(8,128)(2,1)S(1)}, bf16[272,128]{1,0:T(8,128)(2,1)S(1)}, u32[]{:S(2)}, u32[]{:S(2)}) %collective-permute-start.10) | collective-permute-done | bytes 69664 | tf_op jit(solution)/shard_map/ppermute | solution.py:668
  62.6 1.5 %collective-permute-done.16.other = bf16[1088,128]{1,0:T(8,128)(2,1)S(1)} collective-permute-done((bf16[1088,128]{1,0:T(8,128)(2,1)S(1)}, bf16[1088,128]{1,0:T(8,128)(2,1)S(1)}, u32[]{:S(2)}, u32[]{:S(2)}) %collective-permute-start.16) | collective-permute-done | bytes 278560 | tf_op jit(solution)/shard_map/ppermute | solution.py:668
  64.2 1.1 %shard_map.206 = (f32[7,7,2,128]{3,2,1,0:T(2,128)}, f32[2,128]{1,0:T(2,128)}, f32[2,128]{1,0:T(2,128)}, f32[2,128]{1,0:T(2,128)}, f32[2,128,512]{2,1,0:T(8,128)}...) custom-call(s32[1]{0:T(128)} %bitcast.3.held, ...), custom_call_target="tpu_custom_call" | custom-call | tf_op jit(solution)/shard_map/pallas_call | solution.py:923
  (69 shorter events, 1.6 us)
Async XLA Ops:
  0.6 4.7 %copy-start.2 = (s32[45,24]{0,1:T(8,128)S(1)}, s32[45,24]{0,1:T(8,128)}, u32[]{:S(2)}) copy-start(s32[45,24]{0,1:T(8,128)} %param.13) | copy-start | bytes 12964
  0.7 4.7 %copy-start.1 = (bf16[45,24,128]{2,1,0:T(8,128)(2,1)S(1)}, bf16[45,24,128]{2,1,0:T(8,128)(2,1)}, u32[]{:S(2)}) copy-start(bf16[45,24,128]{2,1,0:T(8,128)(2,1)} %cotangent.3) | copy-start | bytes 829444
  0.7 4.8 %copy-start = (bf16[45,24,128]{2,1,0:T(8,128)(2,1)S(1)}, bf16[45,24,128]{2,1,0:T(8,128)(2,1)}, u32[]{:S(2)}) copy-start(bf16[45,24,128]{2,1,0:T(8,128)(2,1)} %state_tile.1) | copy-start | bytes 829444
  2.4 5.7 %collective-permute-start = (bf16[320,128]{1,0:T(8,128)(2,1)}, bf16[320,128]{1,0:T(8,128)(2,1)S(1)}, u32[]{:S(2)}, u32[]{:S(2)}) collective-permute-start(bf16[320,128]{1,0:T(8,128)(2,1)} %bitcast.69), channel_id=1, source_target_pairs={{0,1},{1,0},{2,3},{3,2},{4,5},{5,4},{6,7},{7,6},{8,9},{9,8},{10,11... | collective-permute-start | bytes 245768 | tf_op jit(solution)/shard_map/ppermute | solution.py:668
  8.5 7.7 %copy-start.3 = (bf16[2,128,512]{2,1,0:T(8,128)(2,1)S(1)}, bf16[2,128,512]{2,1,0:T(8,128)(2,1)}, u32[]{:S(2)}) copy-start(bf16[2,128,512]{2,1,0:T(8,128)(2,1)} %weight_in.1) | copy-start | bytes 786436
  8.5 7.7 %copy-start.4 = (bf16[2,512,128]{2,1,0:T(8,128)(2,1)S(1)}, bf16[2,512,128]{2,1,0:T(8,128)(2,1)}, u32[]{:S(2)}) copy-start(bf16[2,512,128]{2,1,0:T(8,128)(2,1)} %weight_out.1) | copy-start | bytes 786436
  8.6 7.6 %collective-permute-start.2 = (bf16[664,128]{1,0:T(8,128)(2,1)S(1)}, bf16[664,128]{1,0:T(8,128)(2,1)S(1)}, u32[]{:S(2)}, u32[]{:S(2)}) collective-permute-start(bf16[664,128]{1,0:T(8,128)(2,1)S(1)} %get-tuple-element.47), channel_id=1, source_target_pairs={{0,30},{2,4},{4,2},{6,8},{8,6},{10,12},{12,10},{14,16},{16,14},{18... | collective-permute-start | bytes 509960 | tf_op jit(solution)/shard_map/ppermute | solution.py:648
  12.0 4.2 %collective-permute-start.1 = (bf16[664,128]{1,0:T(8,128)(2,1)S(1)}, bf16[664,128]{1,0:T(8,128)(2,1)S(1)}, u32[]{:S(2)}, u32[]{:S(2)}) collective-permute-start(bf16[664,128]{1,0:T(8,128)(2,1)S(1)} %get-tuple-element.48), channel_id=1, source_target_pairs={{0,2},{1,3},{2,0},{3,1},{4,6},{5,7},{6,4},{7,5},{8,10},{9,11},{10,... | collective-permute-start | bytes 509960 | tf_op jit(solution)/shard_map/ppermute | solution.py:668
  12.0 4.2 %copy-start.9 = (f32[2,128]{1,0:T(2,128)S(1)}, f32[2,128]{1,0:T(2,128)}, u32[]{:S(2)}) copy-start(f32[2,128]{1,0:T(2,128)} %bias_out.1) | copy-start | bytes 3076
  12.0 4.2 %copy-start.10 = (f32[2,128]{1,0:T(2,128)S(1)}, f32[2,128]{1,0:T(2,128)}, u32[]{:S(2)}) copy-start(f32[2,128]{1,0:T(2,128)} %layer_scale.1) | copy-start | bytes 3076
  35.3 1.6 %collective-permute-start.3 = (bf16[1088,128]{1,0:T(8,128)(2,1)S(1)}, bf16[1088,128]{1,0:T(8,128)(2,1)S(1)}, u32[]{:S(2)}, u32[]{:S(2)}) collective-permute-start(bf16[1088,128]{1,0:T(8,128)(2,1)S(1)} %dynamic-slice_bitcast_fusion), channel_id=1, source_target_pairs={{0,2},{1,3},{2,0},{3,1},{4,6},{5,7},{6,4},{7,5},{8,10},{9,11},{10,... | collective-permute-start | bytes 835592 | tf_op jit(solution)/shard_map/ppermute | solution.py:668
  37.1 5.6 %collective-permute-start.4 = (bf16[272,128]{1,0:T(8,128)(2,1)S(1)}, bf16[272,128]{1,0:T(8,128)(2,1)S(1)}, u32[]{:S(2)}, u32[]{:S(2)}) collective-permute-start(bf16[272,128]{1,0:T(8,128)(2,1)S(1)} %get-tuple-element.53), channel_id=1, source_target_pairs={{0,1},{1,0},{2,3},{3,2},{4,5},{5,4},{6,7},{7,6},{8,9},{9,8},{10,11... | collective-permute-start | bytes 208904 | tf_op jit(solution)/shard_map/ppermute | solution.py:668
  40.2 5.4 %collective-permute-start.6 = (bf16[272,128]{1,0:T(8,128)(2,1)S(1)}, bf16[272,128]{1,0:T(8,128)(2,1)S(1)}, u32[]{:S(2)}, u32[]{:S(2)}) collective-permute-start(bf16[272,128]{1,0:T(8,128)(2,1)S(1)} %get-tuple-element.54), channel_id=1, source_target_pairs={{0,5},{1,4},{2,7},{3,6},{4,1},{5,0},{6,3},{7,2},{8,13},{9,12},{10,... | collective-permute-start | bytes 208904 | tf_op jit(solution)/shard_map/ppermute | solution.py:668
  40.4 5.4 %collective-permute-start.5 = (bf16[272,128]{1,0:T(8,128)(2,1)S(1)}, bf16[272,128]{1,0:T(8,128)(2,1)S(1)}, u32[]{:S(2)}, u32[]{:S(2)}) collective-permute-start(bf16[272,128]{1,0:T(8,128)(2,1)S(1)} %get-tuple-element.55), channel_id=1, source_target_pairs={{0,4},{1,5},{2,6},{3,7},{4,0},{5,1},{6,2},{7,3},{8,12},{9,13},{10,... | collective-permute-start | bytes 208904 | tf_op jit(solution)/shard_map/ppermute | solution.py:668
  42.7 7.6 %collective-permute-start.14 = (bf16[136,128]{1,0:T(8,128)(2,1)S(1)}, bf16[136,128]{1,0:T(8,128)(2,1)S(1)}, u32[]{:S(2)}, u32[]{:S(2)}) collective-permute-start(bf16[136,128]{1,0:T(8,128)(2,1)S(1)} %get-tuple-element.64), channel_id=1, source_target_pairs={{0,30},{2,4},{4,2},{6,8},{8,6},{10,12},{12,10},{14,16},{16,14},{18... | collective-permute-start | bytes 104456 | tf_op jit(solution)/shard_map/ppermute | solution.py:648
  45.8 7.1 %collective-permute-start.9 = (bf16[272,128]{1,0:T(8,128)(2,1)S(1)}, bf16[272,128]{1,0:T(8,128)(2,1)S(1)}, u32[]{:S(2)}, u32[]{:S(2)}) collective-permute-start(bf16[272,128]{1,0:T(8,128)(2,1)S(1)} %fusion.32), channel_id=1, source_target_pairs={{0,24},{1,25},{2,26},{3,27},{4,28},{5,29},{6,30},{7,31},{8,16},{9,... | collective-permute-start | bytes 208904 | tf_op jit(solution)/shard_map/ppermute | solution.py:668
  49.7 5.6 %collective-permute-start.8 = (bf16[272,128]{1,0:T(8,128)(2,1)S(1)}, bf16[272,128]{1,0:T(8,128)(2,1)S(1)}, u32[]{:S(2)}, u32[]{:S(2)}) collective-permute-start(bf16[272,128]{1,0:T(8,128)(2,1)S(1)} %fusion.32), channel_id=1, source_target_pairs={{0,16},{1,17},{2,18},{3,19},{4,20},{5,21},{6,22},{7,23},{8,24},{9,... | collective-permute-start | bytes 208904 | tf_op jit(solution)/shard_map/ppermute | solution.py:668
  49.7 5.7 %collective-permute-start.7 = (bf16[272,128]{1,0:T(8,128)(2,1)S(1)}, bf16[272,128]{1,0:T(8,128)(2,1)S(1)}, u32[]{:S(2)}, u32[]{:S(2)}) collective-permute-start(bf16[272,128]{1,0:T(8,128)(2,1)S(1)} %fusion.32), channel_id=1, source_target_pairs={{0,8},{1,9},{2,10},{3,11},{4,12},{5,13},{6,14},{7,15},{8,0},{9,1},... | collective-permute-start | bytes 208904 | tf_op jit(solution)/shard_map/ppermute | solution.py:668
  50.3 1.2 %collective-permute-start.13 = (bf16[136,128]{1,0:T(8,128)(2,1)S(1)}, bf16[136,128]{1,0:T(8,128)(2,1)S(1)}, u32[]{:S(2)}, u32[]{:S(2)}) collective-permute-start(bf16[136,128]{1,0:T(8,128)(2,1)S(1)} %get-tuple-element.65), channel_id=1, source_target_pairs={{0,2},{1,3},{2,0},{3,1},{4,6},{5,7},{6,4},{7,5},{8,10},{9,11},{10,... | collective-permute-start | bytes 104456 | tf_op jit(solution)/shard_map/ppermute | solution.py:668
  51.5 7.4 %collective-permute-start.15 = (bf16[96,128]{1,0:T(8,128)(2,1)S(1)}, bf16[96,128]{1,0:T(8,128)(2,1)S(1)}, u32[]{:S(2)}, u32[]{:S(2)}) collective-permute-start(bf16[96,128]{1,0:T(8,128)(2,1)S(1)} %fusion.41), channel_id=1, source_target_pairs={{0,1},{1,0},{2,3},{3,2},{4,5},{5,4},{6,7},{7,6},{8,9},{9,8},{10,11... | collective-permute-start | bytes 73736 | tf_op jit(solution)/shard_map/ppermute | solution.py:668
  55.4 6.3 %collective-permute-start.12 = (bf16[272,128]{1,0:T(8,128)(2,1)S(1)}, bf16[272,128]{1,0:T(8,128)(2,1)S(1)}, u32[]{:S(2)}, u32[]{:S(2)}) collective-permute-start(bf16[272,128]{1,0:T(8,128)(2,1)S(1)} %add_convert_fusion), channel_id=1, source_target_pairs={{0,5},{1,4},{2,7},{3,6},{4,1},{5,0},{6,3},{7,2},{8,13},{9,12},{10,... | collective-permute-start | bytes 208904 | tf_op jit(solution)/shard_map/ppermute | solution.py:668
  57.1 4.6 %collective-permute-start.11 = (bf16[272,128]{1,0:T(8,128)(2,1)S(1)}, bf16[272,128]{1,0:T(8,128)(2,1)S(1)}, u32[]{:S(2)}, u32[]{:S(2)}) collective-permute-start(bf16[272,128]{1,0:T(8,128)(2,1)S(1)} %add_convert_fusion), channel_id=1, source_target_pairs={{0,4},{1,5},{2,6},{3,7},{4,0},{5,1},{6,2},{7,3},{8,12},{9,13},{10,... | collective-permute-start | bytes 208904 | tf_op jit(solution)/shard_map/ppermute | solution.py:668
  58.1 4.3 %collective-permute-start.10 = (bf16[272,128]{1,0:T(8,128)(2,1)S(1)}, bf16[272,128]{1,0:T(8,128)(2,1)S(1)}, u32[]{:S(2)}, u32[]{:S(2)}) collective-permute-start(bf16[272,128]{1,0:T(8,128)(2,1)S(1)} %add_convert_fusion), channel_id=1, source_target_pairs={{0,1},{1,0},{2,3},{3,2},{4,5},{5,4},{6,7},{7,6},{8,9},{9,8},{10,11... | collective-permute-start | bytes 208904 | tf_op jit(solution)/shard_map/ppermute | solution.py:668
  62.5 1.6 %collective-permute-start.16 = (bf16[1088,128]{1,0:T(8,128)(2,1)S(1)}, bf16[1088,128]{1,0:T(8,128)(2,1)S(1)}, u32[]{:S(2)}, u32[]{:S(2)}) collective-permute-start(bf16[1088,128]{1,0:T(8,128)(2,1)S(1)} %pad_maximum_fusion.1.own), channel_id=1, source_target_pairs={{0,2},{1,3},{2,0},{3,1},{4,6},{5,7},{6,4},{7,5},{8,10},{9,11},{10,... | collective-permute-start | bytes 835592 | tf_op jit(solution)/shard_map/ppermute | solution.py:668
  (5 other events, 20.1 us)
